TPU v7x, 128 devices: a whole 4x4x4 slice. The times are simulated.
128 devices in a mesh: gx: 32 (over x, y_lo, z), gy: 2 (over y_hi), mode: 2 (over core).
Axes of the slice: x: 4, y: 4 (y_hi: 2, y_lo: 2; y = y_hi * 2 + y_lo), z: 4, core: 2. Of those that a mesh axis runs over, the one named last changes fastest.
Arguments:
- chaos_state: float32 [64, 48, 4, 8192], P('gx', 'mode', None, 'gy'), may hold values from -2.5 to 2.5
- mode_group: int32 [35], replicated, may hold values from 0 to 1, as said below
- mode_degrees: int32 [35, 4], replicated, may hold values from 0 to 3, as said below
Outputs:
- new_state: float32 [64, 48, 4, 8192], P('gx', 'mode', None, 'gy')
Inputs may be any that keep to these rules, and one draw needn't show every extreme that they name: mode_group[m] is the group of chaos mode m; every group holds at most 24 modes, and one group holds exactly 24. `mode_degrees`: the rows are the 35 multi-indices of 4 non-negative degrees with sum at most 3, each once, in some order.
All inputs are finite; a program needn't handle non-finite values.
Results may differ from a plain program's by a relative error of at most 0.00005.
Values sent between devices are 32-bit elements; how exact they have to be, the bound alone decides.
No kernel may reach another device: no remote copies, remote signals or barrier semaphores. Data moves between devices by JAX's collectives and lax.ppermute only.
A program may use at most 512 MiB of HBM per device.

v0:
```python
import math

import jax
import jax.numpy as jnp
from jax import lax
from jax.sharding import PartitionSpec as P

PARAMS = 4
QUAD = 81
NZ = 16


top_degree = lax.Precision.HIGHEST
time_step = 0.05
diffusion = 1.0


def padded(array, sides, width):
    for axis, dim in sides:
        peers, length = (lax.axis_size(axis), array.shape[dim])
        up = [(i, (i + 1) % peers) for i in range(peers)]
        down = [(j, i) for i, j in up]
        last = lax.slice_in_dim(array, length - width, length, axis=dim)
        initial = lax.slice_in_dim(array, 0, width, axis=dim)
        before = lax.ppermute(last, axis, up)
        after = lax.ppermute(initial, axis, down)
        array = jnp.concatenate([before, array, after], axis=dim)
    return array


def chaos_tables(mode_degrees):
    points = jnp.arange(QUAD, dtype=jnp.int32)
    powers = jnp.power(3, jnp.arange(PARAMS, dtype=jnp.int32)).astype(jnp.int32)
    digits = points[:, None] // powers[None, :] % 3
    abscissa = (digits - 1).astype(jnp.float32) * math.sqrt(3.0)
    weights = jnp.prod(jnp.where(digits == 1, 2.0 / 3.0, 1.0 / 6.0).astype(jnp.float32), axis=1)
    degree = mode_degrees[None, :, :]
    coordinate = abscissa[:, None, :]
    square_term = (coordinate * coordinate - 1.0) / math.sqrt(2.0)
    cubic_term = (coordinate * coordinate * coordinate - 3.0 * coordinate) / math.sqrt(6.0)
    factor = jnp.where(
        degree == 0,
        jnp.ones_like(coordinate),
        jnp.where(degree == 1, coordinate, jnp.where(degree == 2, square_term, cubic_term)),
    )
    chaos_basis_table = jnp.prod(factor, axis=2)
    return (abscissa, weights, chaos_basis_table)


def slot_index(mode_group, slots):
    mode_count = mode_group.shape[0]
    mode_order = jnp.arange(mode_count, dtype=jnp.int32)
    same_group = mode_group[:, None] == mode_group[None, :]
    before = mode_order[None, :] < mode_order[:, None]
    rank_in_group = jnp.sum(jnp.where(same_group & before, 1, 0).astype(jnp.int32), axis=1)
    return mode_group * slots + rank_in_group


def point_terms(point_values, abscissa):
    param_one = abscissa[:, 0][:, None, None]
    param_two = abscissa[:, 1][:, None, None]
    param_three = abscissa[:, 2][:, None, None]
    param_four = abscissa[:, 3][:, None, None]
    lead_field = point_values[:, 0:1, :]
    side_field = point_values[:, 1:2, :]
    speed_east = 0.6 + 0.25 * param_one + 0.5 * lead_field
    speed_north = 0.3 + 0.25 * param_two + 0.5 * side_field
    relaxation = 0.4 * jnp.exp(0.25 * param_three)
    coupling = 0.15 * (1.0 + 0.3 * param_four)
    eastward_flux = speed_east * point_values
    northward_flux = speed_north * point_values
    source_term = -relaxation * point_values + coupling * jnp.roll(
        point_values, -1, axis=1
    ) * jnp.roll(point_values, -2, axis=1)
    return (eastward_flux, northward_flux, source_term)


def project_rows(point_values, galerkin_projection, abscissa):

    def row_work(row_values):
        eastward_flux, northward_flux, source_term = point_terms(row_values, abscissa)
        eastward_modal_flux = jnp.einsum(
            "gr,rha->gha", galerkin_projection, eastward_flux, precision=top_degree
        )
        northward_modal_flux = jnp.einsum(
            "gr,rha->gha", galerkin_projection, northward_flux, precision=top_degree
        )
        source_modal_terms = jnp.einsum(
            "gr,rha->gha", galerkin_projection, source_term, precision=top_degree
        )
        return (eastward_modal_flux, northward_modal_flux, source_modal_terms)

    return lax.map(row_work, point_values)


def centered(plus_one, minus_one, plus_two, minus_two):
    return (8.0 * (plus_one - minus_one) - (plus_two - minus_two)) / 12.0


def plane_laplace(field_array):
    plane_index = jnp.arange(field_array.shape[-1], dtype=jnp.int32) % NZ
    above_plane = jnp.where(
        plane_index == NZ - 1,
        jnp.roll(field_array, NZ - 1, axis=-1),
        jnp.roll(field_array, -1, axis=-1),
    )
    below_plane = jnp.where(
        plane_index == 0, jnp.roll(field_array, 1 - NZ, axis=-1), jnp.roll(field_array, 1, axis=-1)
    )
    return above_plane - 2.0 * field_array + below_plane


def shards(chaos_state, mode_group, mode_degrees):
    groups = lax.axis_size("mode")
    slots = chaos_state.shape[1]
    abscissa, weights, chaos_basis_table = chaos_tables(mode_degrees)
    slot_of_mode = slot_index(mode_group, slots)
    onehot = (slot_of_mode[:, None] == jnp.arange(groups * slots, dtype=jnp.int32)[None, :]).astype(
        jnp.float32
    )
    slot_basis = jnp.einsum("pm,ms->ps", chaos_basis_table, onehot, precision=top_degree)
    slot_projector = jnp.transpose(slot_basis * weights[:, None])
    live_slots = jnp.sum(onehot, axis=0)
    first_slot = lax.axis_index("mode") * slots
    own_projector = lax.dynamic_slice_in_dim(slot_projector, first_slot, slots, 0)
    own_live_slots = lax.dynamic_slice_in_dim(live_slots, first_slot, slots, 0)
    coefficients = chaos_state * own_live_slots[None, :, None, None]

    def galerkin(modal):
        point_values = jnp.einsum(
            "ps,xsfc->xpfc",
            slot_basis,
            lax.all_gather(modal, "mode", axis=1, tiled=True),
            precision=top_degree,
        )
        return project_rows(point_values, own_projector, abscissa)

    def tendency(modal):
        eastward_modal_flux, northward_modal_flux, source_modal_terms = galerkin(modal)
        margin = 2 * NZ
        cell_count = northward_modal_flux.shape[3]
        padded_north = padded(northward_modal_flux, (("gy", 3),), 2 * NZ)
        north_term = centered(
            padded_north[:, :, :, margin + NZ : margin + NZ + cell_count],
            padded_north[:, :, :, margin - NZ : margin - NZ + cell_count],
            padded_north[:, :, :, margin + 2 * NZ : margin + 2 * NZ + cell_count],
            padded_north[:, :, :, 0:cell_count],
        )
        partial_value = source_modal_terms - north_term + diffusion * plane_laplace(modal)
        row_count = eastward_modal_flux.shape[0]
        padded_east = padded(eastward_modal_flux, (("gx", 0),), 2)
        east_term = centered(
            padded_east[3 : 3 + row_count],
            padded_east[1 : 1 + row_count],
            padded_east[4 : 4 + row_count],
            padded_east[0:row_count],
        )
        return partial_value - east_term

    section = coefficients + time_step * tendency(coefficients)
    advanced = 0.5 * coefficients + 0.5 * (section + time_step * tendency(section))
    return advanced


def solution(mesh):
    in_specs = (P("gx", "mode", None, "gy"), P(), P())
    out_specs = P("gx", "mode", None, "gy")
    return jax.shard_map(shards, mesh=mesh, in_specs=in_specs, out_specs=out_specs, check_vma=False)
```

profile of v0, /device:TPU:1, one launch (start us, length us, event | category | flops | bytes accessed | tf_op | source)
XLA Modules:
  0.0 408.7 jit_solution(51438004107792759)
XLA Ops:
  8.8 5.4 %copy_multiply_fusion = f32[2,24,4,4096]{3,1,2,0:T(8,128)} fusion(f32[2,24,4,4096]{3,2,1,0:T(4,128)} %param.7, f32[24]{0:T(128)S(1)} %dynamic_slice.13), kind=kLoop, calls=%fused_computation.126 | loop fusion | flops 786432 | bytes 6291552 | tf_op jit(solution)/shard_map/mul | solution.py:127
  17.1 1.7 fusion.151
  18.8 1.7 fusion.148
  20.5 17.0 %all-gather.3.cloned.1.call-done = f32[2,48,4,4096]{3,1,2,0:T(8,128)} async-done(((f32[2,24,4,4096]{3,1,2,0:T(8,128)}), f32[2,48,4,4096]{3,1,2,0:T(8,128)}) %all-gather.3.cloned.1.call-update) | async-done | bytes 6291472 | tf_op jit(solution)/shard_map/all_gather | solution.py:133
  37.5 19.1 %convolution_bitcast_fusion.1 = f32[2,81,4,4096]{3,1,2,0:T(8,128)} fusion(f32[2,48,4,4096]{3,1,2,0:T(8,128)} %all-gather.3.cloned.1.call-done, f32[81,48]{0,1:T(8,128)S(1)} %fusion.122), kind=kOutput, calls=%fused_computation.75 | convolution fusion | flops 1528823808 | bytes 16923840 | tf_op jit(solution)/shard_map/ps,xsfc->xpfc/dot_general | solution.py:130
  56.6 2.0 broadcast.630.clone
  58.6 2.0 broadcast.630.clone.1
  60.7 2.0 broadcast.630.clone.2
  62.7 51.9 %while.30 = (s32[]{:T(128)}, f32[2,24,4,4096]{3,1,2,0:T(8,128)}, f32[2,24,4,4096]{3,1,2,0:T(8,128)}, f32[2,24,4,4096]{3,1,2,0:T(8,128)}, f32[81,4]{0,1:T(4,128)}...) while((s32[]{:T(128)}, f32[2,24,4,4096]{3,1,2,0:T(8,128)}, ...), condition=%wide.region_5.6_spmd.clone, body=%wide.region_4.5_spmd.clone.sunk | while | flops 1158562560 | bytes 114781480 | solution.py:93
  62.9 3.2 dynamic-slice_bitcast_fusion.10
  68.8 5.5 %fusion.185 = f32[2,24,4,4096]{3,1,2,0:T(8,128)} fusion(f32[2,24,4,4096]{3,1,2,0:T(8,128)} %get-tuple-element.355, s32[]{:T(128)S(6)} %copy.33, f32[81,4096]{1,0:T(8,128)S(1)} %get-tuple-element.323, f32[24,81]{1,0:T(8,128)S(1)} %get-tuple-element.368, f32[2,81,4,4096]{3,1,2,0:T(8,128)S(1)} %copy-done.1), kind=kOutput, calls=%fused_computation.18.clone.1 | convolution fusion | flops 383533056 | bytes 8795136 | tf_op jit(solution)/shard_map/while/body/eval_jaxpr/gr,rha->gha/dot_general | solution.py:82
  74.3 5.6 %fusion.186 = f32[2,24,4,4096]{3,1,2,0:T(8,128)} fusion(f32[2,24,4,4096]{3,1,2,0:T(8,128)} %get-tuple-element.356, s32[]{:T(128)S(6)} %copy.33, f32[81,4096]{1,0:T(8,128)S(1)} %get-tuple-element.324, f32[24,81]{1,0:T(8,128)S(1)} %get-tuple-element.368, f32[2,81,4,4096]{3,1,2,0:T(8,128)S(1)} %copy-done.1), kind=kOutput, calls=%fused_computation.20.clone.1 | convolution fusion | flops 383533056 | bytes 8795136 | tf_op jit(solution)/shard_map/while/body/eval_jaxpr/gr,rha->gha/dot_general | solution.py:85
  81.0 7.5 %fusion.188 = f32[2,24,4,4096]{3,1,2,0:T(8,128)} fusion(f32[2,24,4,4096]{3,1,2,0:T(8,128)} %get-tuple-element.357, s32[]{:T(128)S(6)} %copy.33, f32[81,1,4096]{2,0,1:T(8,128)S(1)} %get-tuple-element.325, f32[81,3,4096]{2,0,1:T(8,128)S(1)} %slice.376, f32[81,2,4096]{2,0,1:T(8,128)S(1)} %get-tuple-element.326, ...), kind=kOutput, calls=%fused_computation.16.clone.1 | convolution fusion | flops 390168576 | bytes 18888704 | tf_op jit(solution)/shard_map/while/body/eval_jaxpr/gr,rha->gha/dot_general | solution.py:88
  88.6 3.2 dynamic-slice_bitcast_fusion.10
  94.6 5.5 %fusion.185 = f32[2,24,4,4096]{3,1,2,0:T(8,128)} fusion(f32[2,24,4,4096]{3,1,2,0:T(8,128)} %get-tuple-element.355, s32[]{:T(128)S(6)} %copy.33, f32[81,4096]{1,0:T(8,128)S(1)} %get-tuple-element.323, f32[24,81]{1,0:T(8,128)S(1)} %get-tuple-element.368, f32[2,81,4,4096]{3,1,2,0:T(8,128)S(1)} %copy-done.1), kind=kOutput, calls=%fused_computation.18.clone.1 | convolution fusion | flops 383533056 | bytes 8795136 | tf_op jit(solution)/shard_map/while/body/eval_jaxpr/gr,rha->gha/dot_general | solution.py:82
  100.0 5.5 %fusion.186 = f32[2,24,4,4096]{3,1,2,0:T(8,128)} fusion(f32[2,24,4,4096]{3,1,2,0:T(8,128)} %get-tuple-element.356, s32[]{:T(128)S(6)} %copy.33, f32[81,4096]{1,0:T(8,128)S(1)} %get-tuple-element.324, f32[24,81]{1,0:T(8,128)S(1)} %get-tuple-element.368, f32[2,81,4,4096]{3,1,2,0:T(8,128)S(1)} %copy-done.1), kind=kOutput, calls=%fused_computation.20.clone.1 | convolution fusion | flops 383533056 | bytes 8795136 | tf_op jit(solution)/shard_map/while/body/eval_jaxpr/gr,rha->gha/dot_general | solution.py:85
  106.7 7.6 %fusion.188 = f32[2,24,4,4096]{3,1,2,0:T(8,128)} fusion(f32[2,24,4,4096]{3,1,2,0:T(8,128)} %get-tuple-element.357, s32[]{:T(128)S(6)} %copy.33, f32[81,1,4096]{2,0,1:T(8,128)S(1)} %get-tuple-element.325, f32[81,3,4096]{2,0,1:T(8,128)S(1)} %slice.376, f32[81,2,4096]{2,0,1:T(8,128)S(1)} %get-tuple-element.326, ...), kind=kOutput, calls=%fused_computation.16.clone.1 | convolution fusion | flops 390168576 | bytes 18888704 | tf_op jit(solution)/shard_map/while/body/eval_jaxpr/gr,rha->gha/dot_general | solution.py:88
  116.1 4.5 %collective-permute-start.2 = (f32[2,24,4,4096]{3,1,2,0:T(8,128)}, f32[2,24,4,4096]{3,1,2,0:T(8,128)}, u32[]{:S(2)}, u32[]{:S(2)}) collective-permute-start(f32[2,24,4,4096]{3,1,2,0:T(8,128)} %get-tuple-element.103), channel_id=1, source_target_pairs={{4,0},{8,4},{12,8},{16,12},{20,16},{24,20},{28,24},{32,28},{36,32}... | collective-permute-start | bytes 9437192 | tf_op jit(solution)/shard_map/ppermute | solution.py:26
  120.6 4.2 %fusion.150 = (f32[2,24,4,4081]{3,1,2,0:T(8,128)S(1)}, f32[2,24,4,4081]{3,1,2,0:T(8,128)S(1)}) fusion(f32[2,24,4,4096]{3,1,2,0:T(8,128)} %copy_multiply_fusion), kind=kLoop, calls=%fused_computation.189 | loop fusion | bytes 12536832 | tf_op jit(solution)/shard_map/jit(_roll_static)/slice | solution.py:108
  127.1 2.7 collective-permute-start
  129.8 2.1 constant_dynamic-update-slice_fusion.1
  132.6 61.2 %collective-permute-done = f32[2,24,4,32]{3,1,2,0:T(8,128)S(1)} collective-permute-done((f32[2,24,4,32]{3,1,2,0:T(8,128)S(1)}, f32[2,24,4,32]{3,1,2,0:T(8,128)S(1)}, u32[]{:S(2)}, u32[]{:S(2)}) %collective-permute-start) | collective-permute-done | bytes 24608 | tf_op jit(solution)/shard_map/ppermute | solution.py:26
  193.8 2.1 collective-permute-done.1
  196.6 12.1 %fusion.105 = f32[2,24,4,4096]{3,1,2,0:T(8,128)} fusion(f32[2,24,4,4096]{3,1,2,0:T(8,128)S(1)} %copy-done.6, f32[2,24,4,32]{3,1,2,0:T(8,128)} %copy-done.16, f32[2,24,4,4096]{3,1,2,0:T(8,128)} %get-tuple-element.102, f32[2,24,4,4096]{3,1,2,0:T(8,128)} %get-tuple-element.103, f32[2,24,4,4096]{3,1,2,0:T(8,128)} %collective-permute-done.3, ...), kind=kLoop, calls=%fused_computation.101 | loop fusion | flops 22806528 | bytes 40927328 | tf_op jit(solution)/shard_map/add | solution.py:160
  208.7 1.7 fusion.146
  210.4 14.5 %all-gather.5.cloned.1.call-done = f32[2,48,4,4096]{3,1,2,0:T(8,128)} async-done(((f32[2,24,4,4096]{3,1,2,0:T(8,128)}), f32[2,48,4,4096]{3,1,2,0:T(8,128)}) %all-gather.5.cloned.1.call-update) | async-done | bytes 6291472 | tf_op jit(solution)/shard_map/all_gather | solution.py:133
  224.9 19.1 %convolution_bitcast_fusion = f32[2,81,4,4096]{3,1,2,0:T(8,128)} fusion(f32[2,48,4,4096]{3,1,2,0:T(8,128)} %all-gather.5.cloned.1.call-done, f32[81,48]{0,1:T(8,128)S(1)} %copy-done.14), kind=kOutput, calls=%fused_computation.74 | convolution fusion | flops 1528823808 | bytes 16923840 | tf_op jit(solution)/shard_map/ps,xsfc->xpfc/dot_general | solution.py:130
  244.0 2.0 broadcast.630
  246.0 2.0 broadcast.630.clone.3
  248.0 2.0 broadcast.630.clone.4
  250.0 51.5 %while.31 = (s32[]{:T(128)}, f32[2,24,4,4096]{3,1,2,0:T(8,128)}, f32[2,24,4,4096]{3,1,2,0:T(8,128)}, f32[2,24,4,4096]{3,1,2,0:T(8,128)}, f32[81,4]{0,1:T(4,128)}...) while((s32[]{:T(128)}, f32[2,24,4,4096]{3,1,2,0:T(8,128)}, ...), condition=%wide.region_7.8_spmd.clone, body=%wide.region_6.7_spmd.clone.sunk | while | flops 1158562560 | bytes 114781480 | solution.py:93
  250.1 3.2 dynamic-slice_bitcast_fusion.11
  256.1 5.5 %fusion.196 = f32[2,24,4,4096]{3,1,2,0:T(8,128)} fusion(f32[2,24,4,4096]{3,1,2,0:T(8,128)} %get-tuple-element.379, s32[]{:T(128)S(6)} %copy.46, f32[81,4096]{1,0:T(8,128)S(1)} %get-tuple-element.339, f32[24,81]{1,0:T(8,128)S(1)} %get-tuple-element.392, f32[2,81,4,4096]{3,1,2,0:T(8,128)S(1)} %copy-done), kind=kOutput, calls=%fused_computation.55.clone.1 | convolution fusion | flops 383533056 | bytes 8795136 | tf_op jit(solution)/shard_map/while/body/eval_jaxpr/gr,rha->gha/dot_general | solution.py:82
  261.6 5.5 %fusion.197 = f32[2,24,4,4096]{3,1,2,0:T(8,128)} fusion(f32[2,24,4,4096]{3,1,2,0:T(8,128)} %get-tuple-element.380, s32[]{:T(128)S(6)} %copy.46, f32[81,4096]{1,0:T(8,128)S(1)} %get-tuple-element.340, f32[24,81]{1,0:T(8,128)S(1)} %get-tuple-element.392, f32[2,81,4,4096]{3,1,2,0:T(8,128)S(1)} %copy-done), kind=kOutput, calls=%fused_computation.57.clone.1 | convolution fusion | flops 383533056 | bytes 8795136 | tf_op jit(solution)/shard_map/while/body/eval_jaxpr/gr,rha->gha/dot_general | solution.py:85
  268.2 7.5 %fusion.199 = f32[2,24,4,4096]{3,1,2,0:T(8,128)} fusion(f32[2,24,4,4096]{3,1,2,0:T(8,128)} %get-tuple-element.381, s32[]{:T(128)S(6)} %copy.46, f32[81,1,4096]{2,0,1:T(8,128)S(1)} %get-tuple-element.341, f32[81,3,4096]{2,0,1:T(8,128)S(1)} %slice.381, f32[81,2,4096]{2,0,1:T(8,128)S(1)} %get-tuple-element.342, ...), kind=kOutput, calls=%fused_computation.53.clone.1 | convolution fusion | flops 390168576 | bytes 18888704 | tf_op jit(solution)/shard_map/while/body/eval_jaxpr/gr,rha->gha/dot_general | solution.py:88
  275.7 3.2 dynamic-slice_bitcast_fusion.11
  281.7 5.5 %fusion.196 = f32[2,24,4,4096]{3,1,2,0:T(8,128)} fusion(f32[2,24,4,4096]{3,1,2,0:T(8,128)} %get-tuple-element.379, s32[]{:T(128)S(6)} %copy.46, f32[81,4096]{1,0:T(8,128)S(1)} %get-tuple-element.339, f32[24,81]{1,0:T(8,128)S(1)} %get-tuple-element.392, f32[2,81,4,4096]{3,1,2,0:T(8,128)S(1)} %copy-done), kind=kOutput, calls=%fused_computation.55.clone.1 | convolution fusion | flops 383533056 | bytes 8795136 | tf_op jit(solution)/shard_map/while/body/eval_jaxpr/gr,rha->gha/dot_general | solution.py:82
  287.2 5.5 %fusion.197 = f32[2,24,4,4096]{3,1,2,0:T(8,128)} fusion(f32[2,24,4,4096]{3,1,2,0:T(8,128)} %get-tuple-element.380, s32[]{:T(128)S(6)} %copy.46, f32[81,4096]{1,0:T(8,128)S(1)} %get-tuple-element.340, f32[24,81]{1,0:T(8,128)S(1)} %get-tuple-element.392, f32[2,81,4,4096]{3,1,2,0:T(8,128)S(1)} %copy-done), kind=kOutput, calls=%fused_computation.57.clone.1 | convolution fusion | flops 383533056 | bytes 8795136 | tf_op jit(solution)/shard_map/while/body/eval_jaxpr/gr,rha->gha/dot_general | solution.py:85
  293.8 7.5 %fusion.199 = f32[2,24,4,4096]{3,1,2,0:T(8,128)} fusion(f32[2,24,4,4096]{3,1,2,0:T(8,128)} %get-tuple-element.381, s32[]{:T(128)S(6)} %copy.46, f32[81,1,4096]{2,0,1:T(8,128)S(1)} %get-tuple-element.341, f32[81,3,4096]{2,0,1:T(8,128)S(1)} %slice.381, f32[81,2,4096]{2,0,1:T(8,128)S(1)} %get-tuple-element.342, ...), kind=kOutput, calls=%fused_computation.53.clone.1 | convolution fusion | flops 390168576 | bytes 18888704 | tf_op jit(solution)/shard_map/while/body/eval_jaxpr/gr,rha->gha/dot_general | solution.py:88
  303.0 4.5 %collective-permute-start.6 = (f32[2,24,4,4096]{3,1,2,0:T(8,128)}, f32[2,24,4,4096]{3,1,2,0:T(8,128)S(1)}, u32[]{:S(2)}, u32[]{:S(2)}) collective-permute-start(f32[2,24,4,4096]{3,1,2,0:T(8,128)} %get-tuple-element.106), channel_id=1, source_target_pairs={{4,0},{8,4},{12,8},{16,12},{20,16},{24,20},{28,24},{32,28},{36,32}... | collective-permute-start | bytes 9437192 | tf_op jit(solution)/shard_map/ppermute | solution.py:26
  308.5 4.2 %fusion.145 = (f32[2,24,4,4081]{3,1,2,0:T(8,128)S(1)}, f32[2,24,4,4081]{3,1,2,0:T(8,128)S(1)}) fusion(f32[2,24,4,4096]{3,1,2,0:T(8,128)} %fusion.105), kind=kLoop, calls=%fused_computation.184 | loop fusion | bytes 12536832 | tf_op jit(solution)/shard_map/jit(_roll_static)/slice | solution.py:108
  312.8 3.8 fusion.144
  317.6 2.7 collective-permute-start.4
  320.3 2.1 constant_dynamic-update-slice_fusion.3
  323.1 57.5 %collective-permute-done.4 = f32[2,24,4,32]{3,1,2,0:T(8,128)S(1)} collective-permute-done((f32[2,24,4,32]{3,1,2,0:T(8,128)S(1)}, f32[2,24,4,32]{3,1,2,0:T(8,128)S(1)}, u32[]{:S(2)}, u32[]{:S(2)}) %collective-permute-start.4) | collective-permute-done | bytes 24608 | tf_op jit(solution)/shard_map/ppermute | solution.py:26
  380.7 2.1 collective-permute-done.5
  385.5 12.5 %fusion.95 = f32[2,24,4,4096]{3,1,2,0:T(8,128)S(1)} fusion(f32[2,24,4,4096]{3,1,2,0:T(8,128)S(1)} %copy-done.2, f32[2,24,4,4096]{3,1,2,0:T(8,128)} %get-tuple-element.104, f32[2,24,4,32]{3,1,2,0:T(8,128)} %copy-done.15, f32[2,24,4,4096]{3,1,2,0:T(8,128)} %get-tuple-element.105, f32[2,24,4,4096]{3,1,2,0:T(8,128)} %get-tuple-element.106, ...), kind=kLoop, calls=%fused_computation.91 | loop fusion | flops 24379392 | bytes 44073056 | tf_op jit(solution)/shard_map/add | solution.py:161
  398.0 3.7 copy.16
  (103 shorter events, 32.7 us)
Async XLA Ops:
  6.5 31.0 %all-gather.3.cloned.1.call-start = ((), (), s32[]{:S(2)}) async-start(), calls=%async_computation | async-start | bytes 9437184 | tf_op jit(solution)/shard_map/all_gather | solution.py:133
  8.3 0.5 copy-start.21
  14.2 0.7 copy-start.24
  14.2 210.7 %all-gather.5.cloned.1.call-start = ((), (), s32[]{:S(2)}) async-start(), calls=%async_computation.1 | async-start | bytes 9437184 | tf_op jit(solution)/shard_map/all_gather | solution.py:133
  17.1 39.5 %copy-start.13 = (f32[81,48]{0,1:T(8,128)}, f32[81,48]{0,1:T(8,128)S(1)}, u32[]{:S(2)}) copy-start(f32[81,48]{0,1:T(8,128)S(1)} %fusion.122) | copy-start | bytes 46660
  62.9 6.0 %copy-start.1 = (f32[2,81,4,4096]{3,1,2,0:T(8,128)S(1)}, f32[2,81,4,4096]{3,1,2,0:T(8,128)}, u32[]{:S(2)}) copy-start(f32[2,81,4,4096]{3,1,2,0:T(8,128)} %get-tuple-element.367) | copy-start | bytes 31850500 | tf_op jit(solution)/shard_map/while
  88.6 6.0 %copy-start.1 = (f32[2,81,4,4096]{3,1,2,0:T(8,128)S(1)}, f32[2,81,4,4096]{3,1,2,0:T(8,128)}, u32[]{:S(2)}) copy-start(f32[2,81,4,4096]{3,1,2,0:T(8,128)} %get-tuple-element.367) | copy-start | bytes 31850500 | tf_op jit(solution)/shard_map/while
  114.6 81.9 %collective-permute-start.3 = (f32[2,24,4,4096]{3,1,2,0:T(8,128)}, f32[2,24,4,4096]{3,1,2,0:T(8,128)}, u32[]{:S(2)}, u32[]{:S(2)}) collective-permute-start(f32[2,24,4,4096]{3,1,2,0:T(8,128)} %get-tuple-element.103), channel_id=1, source_target_pairs={{0,4},{4,8},{8,12},{12,16},{16,20},{20,24},{24,28},{28,32},{32,36}... | collective-permute-start | bytes 9437192 | tf_op jit(solution)/shard_map/ppermute | solution.py:25
  116.1 80.5 %collective-permute-start.2 = (f32[2,24,4,4096]{3,1,2,0:T(8,128)}, f32[2,24,4,4096]{3,1,2,0:T(8,128)}, u32[]{:S(2)}, u32[]{:S(2)}) collective-permute-start(f32[2,24,4,4096]{3,1,2,0:T(8,128)} %get-tuple-element.103), channel_id=1, source_target_pairs={{4,0},{8,4},{12,8},{16,12},{20,16},{24,20},{28,24},{32,28},{36,32}... | collective-permute-start | bytes 9437192 | tf_op jit(solution)/shard_map/ppermute | solution.py:26
  120.6 75.9 %copy-start.17 = (pred[4096]{0:T(1024)(128)(4,1)}, pred[4096]{0:T(1024)(128)(4,1)S(1)}, u32[]{:S(2)}) copy-start(pred[4096]{0:T(1024)(128)(4,1)S(1)} %get-tuple-element.222) | copy-start | bytes 12292
  120.6 75.9 %copy-start.19 = (pred[4096]{0:T(1024)(128)(4,1)}, pred[4096]{0:T(1024)(128)(4,1)S(1)}, u32[]{:S(2)}) copy-start(pred[4096]{0:T(1024)(128)(4,1)S(1)} %get-tuple-element.223) | copy-start | bytes 12292
  120.6 4.2 %copy-start.3 = (f32[2,24,4,4096]{3,1,2,0:T(8,128)S(1)}, f32[2,24,4,4096]{3,1,2,0:T(8,128)}, u32[]{:S(2)}) copy-start(f32[2,24,4,4096]{3,1,2,0:T(8,128)} %copy_multiply_fusion) | copy-start | bytes 9437188
  124.8 71.7 %copy-start.12 = (f32[2,24,4,1]{3,1,2,0:T(8,128)S(1)}, f32[2,24,4,1]{3,1,2,0:T(8,128)}, u32[]{:S(2)}) copy-start(f32[2,24,4,1]{3,1,2,0:T(8,128)} %get-tuple-element.204) | copy-start | bytes 2308
  127.0 69.5 %copy-start.4 = (f32[2,24,4,4096]{3,2,1,0:T(4,128)S(1)}, f32[2,24,4,4096]{3,2,1,0:T(4,128)}, u32[]{:S(2)}) copy-start(f32[2,24,4,4096]{3,2,1,0:T(4,128)} %param.7) | copy-start | bytes 9437188
  127.0 69.5 %copy-start.6 = (f32[2,24,4,4096]{3,1,2,0:T(8,128)S(1)}, f32[2,24,4,4096]{3,1,2,0:T(8,128)}, u32[]{:S(2)}) copy-start(f32[2,24,4,4096]{3,1,2,0:T(8,128)} %get-tuple-element.101) | copy-start | bytes 9437188
  127.1 69.5 %copy-start.10 = (f32[2,24,4,15]{3,1,2,0:T(8,128)S(1)}, f32[2,24,4,15]{3,1,2,0:T(8,128)}, u32[]{:S(2)}) copy-start(f32[2,24,4,15]{3,1,2,0:T(8,128)} %get-tuple-element.210) | copy-start | bytes 34564
  127.1 69.5 %copy-start.11 = (f32[2,24,4,1]{3,1,2,0:T(8,128)S(1)}, f32[2,24,4,1]{3,1,2,0:T(8,128)}, u32[]{:S(2)}) copy-start(f32[2,24,4,1]{3,1,2,0:T(8,128)} %get-tuple-element.203) | copy-start | bytes 2308
  127.1 69.5 %copy-start.22 = (f32[24]{0:T(128)S(1)}, f32[24]{0:T(128)}, u32[]{:S(2)}) copy-start(f32[24]{0:T(128)} %copy-done.21) | copy-start | bytes 292
  127.1 66.7 %collective-permute-start = (f32[2,24,4,32]{3,1,2,0:T(8,128)S(1)}, f32[2,24,4,32]{3,1,2,0:T(8,128)S(1)}, u32[]{:S(2)}, u32[]{:S(2)}) collective-permute-start(f32[2,24,4,32]{3,1,2,0:T(8,128)S(1)} %get-tuple-element.211), channel_id=1, source_target_pairs={{2,0},{0,2},{3,1},{1,3},{6,4},{4,6},{7,5},{5,7},{10,8},{8,10},{11,... | collective-permute-start | bytes 73736 | tf_op jit(solution)/shard_map/ppermute | solution.py:26
  131.9 64.0 %collective-permute-start.1 = (f32[2,24,4,32]{3,1,2,0:T(8,128)S(1)}, f32[2,24,4,32]{3,1,2,0:T(8,128)S(1)}, u32[]{:S(2)}, u32[]{:S(2)}) collective-permute-start(f32[2,24,4,32]{3,1,2,0:T(8,128)S(1)} %get-tuple-element.212), channel_id=1, source_target_pairs={{0,2},{2,0},{1,3},{3,1},{4,6},{6,4},{5,7},{7,5},{8,10},{10,8},{9,1... | collective-permute-start | bytes 73736 | tf_op jit(solution)/shard_map/ppermute | solution.py:25
  195.9 0.6 copy-start.16
  208.7 16.2 %copy-start.14 = (f32[81,48]{0,1:T(8,128)S(1)}, f32[81,48]{0,1:T(8,128)}, u32[]{:S(2)}) copy-start(f32[81,48]{0,1:T(8,128)} %copy-done.13) | copy-start | bytes 46660
  250.1 6.0 %copy-start = (f32[2,81,4,4096]{3,1,2,0:T(8,128)S(1)}, f32[2,81,4,4096]{3,1,2,0:T(8,128)}, u32[]{:S(2)}) copy-start(f32[2,81,4,4096]{3,1,2,0:T(8,128)} %get-tuple-element.391) | copy-start | bytes 31850500 | tf_op jit(solution)/shard_map/while
  275.7 6.0 %copy-start = (f32[2,81,4,4096]{3,1,2,0:T(8,128)S(1)}, f32[2,81,4,4096]{3,1,2,0:T(8,128)}, u32[]{:S(2)}) copy-start(f32[2,81,4,4096]{3,1,2,0:T(8,128)} %get-tuple-element.391) | copy-start | bytes 31850500 | tf_op jit(solution)/shard_map/while
  301.5 81.3 %collective-permute-start.7 = (f32[2,24,4,4096]{3,1,2,0:T(8,128)}, f32[2,24,4,4096]{3,1,2,0:T(8,128)S(1)}, u32[]{:S(2)}, u32[]{:S(2)}) collective-permute-start(f32[2,24,4,4096]{3,1,2,0:T(8,128)} %get-tuple-element.106), channel_id=1, source_target_pairs={{0,4},{4,8},{8,12},{12,16},{16,20},{20,24},{24,28},{28,32},{32,36}... | collective-permute-start | bytes 9437192 | tf_op jit(solution)/shard_map/ppermute | solution.py:25
  303.0 79.8 %collective-permute-start.6 = (f32[2,24,4,4096]{3,1,2,0:T(8,128)}, f32[2,24,4,4096]{3,1,2,0:T(8,128)S(1)}, u32[]{:S(2)}, u32[]{:S(2)}) collective-permute-start(f32[2,24,4,4096]{3,1,2,0:T(8,128)} %get-tuple-element.106), channel_id=1, source_target_pairs={{4,0},{8,4},{12,8},{16,12},{20,16},{24,20},{28,24},{32,28},{36,32}... | collective-permute-start | bytes 9437192 | tf_op jit(solution)/shard_map/ppermute | solution.py:26
  308.5 4.3 %copy-start.2 = (f32[2,24,4,4096]{3,1,2,0:T(8,128)S(1)}, f32[2,24,4,4096]{3,1,2,0:T(8,128)}, u32[]{:S(2)}) copy-start(f32[2,24,4,4096]{3,1,2,0:T(8,128)} %fusion.105) | copy-start | bytes 9437188
  317.6 67.9 %copy-start.5 = (f32[2,24,4,4096]{3,2,1,0:T(4,128)S(1)}, f32[2,24,4,4096]{3,2,1,0:T(4,128)}, u32[]{:S(2)}) copy-start(f32[2,24,4,4096]{3,2,1,0:T(4,128)} %param.7) | copy-start | bytes 9437188
  317.6 67.9 %copy-start.9 = (f32[2,24,4,15]{3,1,2,0:T(8,128)S(1)}, f32[2,24,4,15]{3,1,2,0:T(8,128)}, u32[]{:S(2)}) copy-start(f32[2,24,4,15]{3,1,2,0:T(8,128)} %get-tuple-element.200) | copy-start | bytes 34564
  317.6 67.9 %copy-start.18 = (pred[4096]{0:T(1024)(128)(4,1)S(1)}, pred[4096]{0:T(1024)(128)(4,1)}, u32[]{:S(2)}) copy-start(pred[4096]{0:T(1024)(128)(4,1)} %copy-done.17) | copy-start | bytes 12292
  317.6 67.9 %copy-start.20 = (pred[4096]{0:T(1024)(128)(4,1)S(1)}, pred[4096]{0:T(1024)(128)(4,1)}, u32[]{:S(2)}) copy-start(pred[4096]{0:T(1024)(128)(4,1)} %copy-done.19) | copy-start | bytes 12292
  317.6 67.9 %copy-start.23 = (f32[24]{0:T(128)S(1)}, f32[24]{0:T(128)}, u32[]{:S(2)}) copy-start(f32[24]{0:T(128)} %copy-done.21) | copy-start | bytes 292
  317.6 63.0 %collective-permute-start.4 = (f32[2,24,4,32]{3,1,2,0:T(8,128)S(1)}, f32[2,24,4,32]{3,1,2,0:T(8,128)S(1)}, u32[]{:S(2)}, u32[]{:S(2)}) collective-permute-start(f32[2,24,4,32]{3,1,2,0:T(8,128)S(1)} %get-tuple-element.201), channel_id=1, source_target_pairs={{2,0},{0,2},{3,1},{1,3},{6,4},{4,6},{7,5},{5,7},{10,8},{8,10},{11,... | collective-permute-start | bytes 73736 | tf_op jit(solution)/shard_map/ppermute | solution.py:26
  322.5 60.3 %collective-permute-start.5 = (f32[2,24,4,32]{3,1,2,0:T(8,128)S(1)}, f32[2,24,4,32]{3,1,2,0:T(8,128)S(1)}, u32[]{:S(2)}, u32[]{:S(2)}) collective-permute-start(f32[2,24,4,32]{3,1,2,0:T(8,128)S(1)} %get-tuple-element.202), channel_id=1, source_target_pairs={{0,2},{2,0},{1,3},{3,1},{4,6},{6,4},{5,7},{7,5},{8,10},{10,8},{9,1... | collective-permute-start | bytes 73736 | tf_op jit(solution)/shard_map/ppermute | solution.py:25
  382.8 0.6 copy-start.15
  382.8 1.7 copy-start.7
  382.8 2.7 copy-start.8
Sparse Core Ops, SparseCore 0:
  14.3 23.1 all-gather.2
  208.8 16.0 all-gather.4
where the time goes:
time: 415 us; the launch traced here: 409 us
  waiting for transfers between devices  155 us (37%)
  matrix products  113 us (27%)
  local copies, waits for them, and re-layouts  66.2 us (16%)
  other arithmetic  41.7 us (10%)
  starting transfers between devices  18.7 us (5%)
  between operations  14 us (3%)
    ppermute x4, waiting for transfers between devices, padded(): after = lax.ppermute(initial, axis, down)  119 us
    dot_general x2, matrix products, galerkin(): jnp.einsum('ps,xsfc->xpfc', slot_basis, lax.all_gather(modal, 'mode', axi...  38.2 us
    all_gather x2, waiting for transfers between devices, galerkin(): lax.all_gather(modal, 'mode', axis=1, tiled=True)  31.5 us
    dot_general x4, matrix products, row_work(): jnp.einsum('gr,rha->gha', galerkin_projection, source_term, precision=top...  30.1 us
    dot_general x4, matrix products, row_work(): jnp.einsum('gr,rha->gha', galerkin_projection, northward_flux, precision=...  22.1 us
    dot_general x4, matrix products, row_work(): jnp.einsum('gr,rha->gha', galerkin_projection, eastward_flux, precision=t...  21.9 us
    ppermute x4, starting transfers between devices, padded(): after = lax.ppermute(initial, axis, down)  14.4 us
    squeeze x4, local copies, waits for them, and re-layouts, project_rows(): return lax.map(row_work, point_values)  12.7 us
  transfers between devices with their start and end apart: 10, of which 6 were waited for; matrix products, arithmetic and copies ran while one was open for 7% of the time, Pallas kernels for 0%

commit v1 on v0

v1 whole, which is shorter than its diff:
```python
import math

import jax
import jax.numpy as jnp
import numpy as np
from jax import lax
from jax.experimental import pallas as pl
from jax.experimental.pallas import tpu as pltpu
from jax.sharding import Mesh, PartitionSpec as P

MODES = 35
FIELDS = 4
QUAD = 81
POINTS = 96
NZ = 16
SLOTS = 24
SMALL = 16
ROWS = SLOTS + SMALL
LANES = 256
STRIP = 2 * NZ
XROWS = 16
STEP = 4
time_step = 0.05
VMEM = 56 * 1024 * 1024
F32, BF16 = jnp.float32, jnp.bfloat16


def point_constants():
    p = np.arange(POINTS)
    live = (p < QUAD).astype(np.float64)
    digits = [(p // 3**k) % 3 - 1.0 for k in range(4)]
    xi = [math.sqrt(3.0) * d for d in digits]
    weight = live * np.prod([np.where(d == 0, 4.0, 1.0) for d in digits], axis=0)
    east = 1.2 + 0.5 * xi[0]
    north = 0.6 + 0.5 * xi[1]
    decay = -9.6 * np.exp(0.25 * xi[2])
    rows = np.stack(digits + [weight, east, north, decay]).astype(np.float32)
    cols = np.zeros((POINTS, 8), np.float32)
    cols[:, :4] = np.stack(digits, 1)
    cols[:, 4] = live
    return np.concatenate([rows, rows], axis=1), cols


def degree_factor(n, d):
    square = 3.0 * d * d - 1.0
    cubic = d * d * d - d
    return jnp.where(n == 0.0, 1.0, jnp.where(n == 1.0, d, jnp.where(n == 2.0, square, cubic)))


def degree_norm(n):
    third = 3.0 * math.sqrt(3.0) / math.sqrt(6.0)
    return jnp.where(n == 0.0, 1.0, jnp.where(n == 1.0, math.sqrt(3.0), jnp.where(n == 2.0, 1.0 / math.sqrt(2.0), third)))


def table_kernel(grow_ref, gcol_ref, degrees_ref, degrees_t_ref, prow_ref, pcol_ref, eval_ref, proj_ref, scale_ref):
    grow, gcol = grow_ref[...], gcol_ref[...]
    same = gcol == grow
    sub = lax.broadcasted_iota(jnp.int32, (MODES, MODES), 0)
    lane = lax.broadcasted_iota(jnp.int32, (MODES, MODES), 1)
    rank_row = jnp.sum(jnp.where(same & (sub < lane), 1.0, 0.0), axis=0, keepdims=True)
    rank_col = jnp.sum(jnp.where(same & (lane < sub), 1.0, 0.0), axis=1, keepdims=True)
    ones = jnp.sum(grow, axis=1, keepdims=True)
    big = jnp.where(ones == float(SLOTS), 1.0, 0.0)
    place_row = jnp.where(grow == big, rank_row, rank_row + SLOTS)
    place_col = jnp.where(gcol == big, rank_col, rank_col + SLOTS)
    row_id = lax.broadcasted_iota(jnp.int32, (ROWS, MODES), 0).astype(F32)
    pick = jnp.where(row_id == place_row, 1.0, 0.0)
    live_col = jnp.sum(pick, axis=1, keepdims=True)
    degree_col = [jnp.sum(pick * degrees_t_ref[k : k + 1, :], axis=1, keepdims=True) for k in range(4)]
    lane_id = lax.broadcasted_iota(jnp.int32, (MODES, 128), 1)
    lane_row = jnp.where(lane_id < ROWS, lane_id, jnp.where(lane_id < 2 * ROWS, lane_id - ROWS, lane_id - 2 * ROWS)).astype(F32)
    pick_t = jnp.where(lane_row == place_col, 1.0, 0.0)
    live_row = jnp.sum(pick_t, axis=0, keepdims=True)
    degree_row = [jnp.sum(pick_t * degrees_ref[:, k : k + 1], axis=0, keepdims=True) for k in range(4)]
    basis = live_row * pcol_ref[:, 4:5]
    for k in range(4):
        basis = basis * degree_factor(degree_row[k], pcol_ref[:, k : k + 1])
    projector = live_col * prow_ref[4:5, :]
    scale, inverse = live_col, live_col
    for k in range(4):
        projector = projector * degree_factor(degree_col[k], prow_ref[k : k + 1, :])
        norm = degree_norm(degree_col[k])
        scale = scale * norm
        inverse = inverse / norm
    column = lax.broadcasted_iota(jnp.int32, (1, 128), 1)
    eval_ref[0:POINTS, :] = jnp.where(column < 2 * ROWS, basis, 0.0).astype(BF16)
    linear = []
    for k in range(3):
        left = projector[:, :POINTS] * prow_ref[5 + k : 6 + k, :POINTS]
        full = jnp.dot(left, basis, precision=lax.Precision.HIGHEST, preferred_element_type=F32)
        first = full.astype(BF16).astype(F32)
        linear.append(jnp.where(column < 2 * ROWS, first, jnp.where(column < 3 * ROWS, full - first, 0.0)))
    linear.append(jnp.zeros((8, 128), F32))
    eval_ref[POINTS:, :] = jnp.concatenate(linear, axis=0).astype(BF16)
    proj_ref[...] = jnp.concatenate([projector, projector * prow_ref[3:4, :]], axis=0).astype(BF16)
    scale_ref[0] = jnp.broadcast_to(scale, (ROWS, LANES))
    scale_ref[1] = jnp.broadcast_to(scale * scale * (time_step / (24.0 * 1296.0)), (ROWS, LANES))
    scale_ref[2] = jnp.broadcast_to(inverse, (ROWS, LANES))


def make_tables(mode_group, mode_degrees):
    prow, pcol = point_constants()
    group = mode_group.astype(F32)
    degrees = mode_degrees.astype(F32)
    return pl.pallas_call(
        table_kernel,
        out_shape=[
            jax.ShapeDtypeStruct((POINTS + 128, 128), BF16),
            jax.ShapeDtypeStruct((2 * ROWS, 2 * POINTS), BF16),
            jax.ShapeDtypeStruct((3, ROWS, LANES), F32),
        ],
        name="tables",
    )(group[None, :], group[:, None], degrees, degrees.T, jnp.asarray(prow), jnp.asarray(pcol))


def lane_index():
    return lax.broadcasted_iota(jnp.int32, (1, LANES), 1)


def shift_masks():
    lane = lane_index()
    return [
        jnp.where(lane < LANES - NZ, 8.0, 0.0),
        jnp.where(lane >= NZ, 8.0, 0.0),
        jnp.where(lane < LANES - 2 * NZ, 1.0, 0.0),
        jnp.where(lane >= 2 * NZ, 1.0, 0.0),
    ]


def rolled(value, shift):
    return pltpu.roll(value, shift % value.shape[1], 1)


def difference_y(value):
    up, down, up_two, down_two = shift_masks()
    return (up * rolled(value, -NZ) - down * rolled(value, NZ)) - (up_two * rolled(value, -2 * NZ) - down_two * rolled(value, 2 * NZ))


def plane_laplace(value):
    plane = lane_index() % NZ
    above = jnp.where(plane == NZ - 1, rolled(value, NZ - 1), rolled(value, -1))
    below = jnp.where(plane == 0, rolled(value, 1 - NZ), rolled(value, 1))
    return above - 2.0 * value + below


def row_fluxes(fields, eval_ref, proj_ref):
    points, east, north, source = [], [], [], []
    for value in fields:
        first = value.astype(BF16).astype(F32)
        stack = jnp.concatenate([first, value - first, first, jnp.zeros((8, LANES), F32)], axis=0).astype(BF16)
        result = jnp.dot(eval_ref[...], stack, preferred_element_type=F32)
        points.append(result[0:POINTS])
        east.append(result[POINTS : POINTS + ROWS])
        north.append(result[POINTS + ROWS : POINTS + 2 * ROWS])
        source.append(result[POINTS + 2 * ROWS : POINTS + 3 * ROWS])

    def project(a, b, both):
        product = points[a] * points[b]
        first = product.astype(BF16)
        second = (product - first.astype(F32)).astype(BF16)
        stack = jnp.concatenate([first, second], axis=0)
        left = proj_ref[...] if both else proj_ref[0:48, :]
        return jnp.dot(left, stack, preferred_element_type=F32)

    def couple(f, result):
        source[f] = source[f] + (3.6 * result[0:ROWS] + (1.08 * math.sqrt(3.0)) * result[ROWS : 2 * ROWS])

    east[0] = east[0] + project(0, 0, False)[0:ROWS]
    result = project(0, 1, True)
    east[1] = east[1] + result[0:ROWS]
    north[0] = north[0] + result[0:ROWS]
    couple(3, result)
    east[2] = east[2] + project(0, 2, False)[0:ROWS]
    result = project(0, 3, True)
    east[3] = east[3] + result[0:ROWS]
    couple(2, result)
    north[1] = north[1] + project(1, 1, False)[0:ROWS]
    result = project(1, 2, True)
    north[2] = north[2] + result[0:ROWS]
    couple(0, result)
    north[3] = north[3] + project(1, 3, False)[0:ROWS]
    couple(1, project(2, 3, True))
    return east, north, source


def emit_row(r, fields, base, weight, eval_ref, proj_ref, scale_ref, east_ref, next_ref, low_ref, high_ref):
    east, north, source = row_fluxes(fields, eval_ref, proj_ref)
    gain = scale_ref[1]
    lane = lax.broadcasted_iota(jnp.int32, (1, 128), 1)
    here = (lane >= r * STRIP) & (lane < (r + 1) * STRIP)
    for f in range(FIELDS):
        rows = slice(f * ROWS, (f + 1) * ROWS)
        east_ref[r, rows, :] = east[f]
        known = gain * (source[f] - difference_y(north[f])) + time_step * plane_laplace(fields[f])
        next_ref[r, rows, :] = base[f] + weight * known
        low = pltpu.roll(north[f][:, :128], r * STRIP, 1)
        high = pltpu.roll(north[f][:, 128:], (r * STRIP + STRIP) % 128, 1)
        if r == 0:
            low_ref[0, rows, :] = low
            high_ref[0, rows, :] = high
        else:
            low_ref[0, rows, :] = jnp.where(here, low, low_ref[0, rows, :])
            high_ref[0, rows, :] = jnp.where(here, high, high_ref[0, rows, :])


def from_neighbours(r, f, centre, before_ref, after_ref, low_ref, high_ref, first, last, edge_before, edge_after):
    rows = slice(f * ROWS, (f + 1) * ROWS)

    def row(k):
        if k < 0:
            return jnp.where(first, edge_before[k + 2, rows, :], before_ref[k + 2, rows, :])
        if k >= STEP:
            return jnp.where(last, edge_after[k - STEP, rows, :], after_ref[k - STEP, rows, :])
        return centre[k, rows, :]

    total = 8.0 * (row(r + 1) - row(r - 1)) - (row(r + 2) - row(r - 2))
    lane = lax.broadcasted_iota(jnp.int32, (1, 128), 1)
    below = pltpu.roll(high_ref[0, rows, :], (128 - r * STRIP) % 128, 1)
    above = pltpu.roll(low_ref[0, rows, :], (96 - r * STRIP) % 128, 1)
    low = jnp.where(lane < STRIP, below, 0.0) - jnp.where(lane < NZ, 8.0, 0.0) * pltpu.roll(below, 128 - NZ, 1)
    high = jnp.where(lane >= 128 - NZ, 8.0, 0.0) * pltpu.roll(above, NZ, 1) - jnp.where(lane >= 128 - STRIP, above, 0.0)
    return total + jnp.concatenate([low, high], axis=1)


def first_kernel(big_ref, state_ref, eval_ref, proj_ref, scale_ref, coef_ref, east_ref, next_ref, low_ref, high_ref):
    big = big_ref[0]
    for r in range(STEP):
        chip, x = divmod(r, 2)
        fields = []
        for f in range(FIELDS):
            halves = []
            for half in range(2):
                full = state_ref[2 * chip + big, x, half, pl.ds(f, SLOTS, stride=FIELDS), :]
                rest = state_ref[2 * chip + 1 - big, x, half, pl.ds(f, SMALL, stride=FIELDS), :]
                halves.append(jnp.concatenate([full, rest], axis=0))
            value = scale_ref[0] * jnp.concatenate(halves, axis=1)
            coef_ref[r, f * ROWS : (f + 1) * ROWS, :] = value
            fields.append(value)
        emit_row(r, fields, fields, 1.0, eval_ref, proj_ref, scale_ref, east_ref, next_ref, low_ref, high_ref)


def middle_kernel(coef_ref, next_ref, east_ref, before_ref, after_ref, low_ref, high_ref, edge_before, edge_after, eval_ref, proj_ref, scale_ref, east_out, next_out, low_out, high_out):
    first = pl.program_id(0) == 0
    last = pl.program_id(0) == pl.num_programs(0) - 1
    for r in range(STEP):
        section, base = [], []
        for f in range(FIELDS):
            rows = slice(f * ROWS, (f + 1) * ROWS)
            missing = from_neighbours(r, f, east_ref, before_ref, after_ref, low_ref, high_ref, first, last, edge_before, edge_after)
            section.append(next_ref[r, rows, :] - scale_ref[1] * missing)
            base.append(0.5 * (coef_ref[r, rows, :] + section[f]))
        emit_row(r, section, base, 0.5, eval_ref, proj_ref, scale_ref, east_out, next_out, low_out, high_out)


def last_kernel(big_ref, next_ref, east_ref, before_ref, after_ref, low_ref, high_ref, edge_before, edge_after, scale_ref, state_out):
    big = big_ref[0]
    first = pl.program_id(0) == 0
    last = pl.program_id(0) == pl.num_programs(0) - 1
    for r in range(STEP):
        chip, x = divmod(r, 2)
        for f in range(FIELDS):
            rows = slice(f * ROWS, (f + 1) * ROWS)
            missing = from_neighbours(r, f, east_ref, before_ref, after_ref, low_ref, high_ref, first, last, edge_before, edge_after)
            value = scale_ref[2] * (next_ref[r, rows, :] - 0.5 * scale_ref[1] * missing)
            rest = jnp.concatenate([value[SLOTS:], jnp.zeros((SLOTS - SMALL, LANES), F32)], axis=0)
            for half in range(2):
                lanes = slice(half * 128, (half + 1) * 128)
                state_out[2 * chip + big, x, half, pl.ds(f, SLOTS, stride=FIELDS), :] = value[:SLOTS, lanes]
                state_out[2 * chip + 1 - big, x, half, pl.ds(f, SLOTS, stride=FIELDS), :] = rest[:, lanes]


def whole(shape):
    return pl.BlockSpec(shape, lambda i: (0,) * len(shape))


def kernels():
    steps = XROWS // STEP
    tall = FIELDS * ROWS
    smem = pl.BlockSpec(memory_space=pltpu.SMEM)
    rows = pl.BlockSpec((STEP, tall, LANES), lambda i: (i, 0, 0))
    before = pl.BlockSpec((2, tall, LANES), lambda i: (jnp.maximum(2 * i - 1, 0), 0, 0))
    after = pl.BlockSpec((2, tall, LANES), lambda i: (jnp.minimum(2 * i + 2, 2 * steps - 1), 0, 0))
    strip = pl.BlockSpec((1, tall, 128), lambda i: (i, 0, 0))
    edge = whole((2, tall, LANES))
    state = pl.BlockSpec((STEP, 2, 2, SLOTS * FIELDS, 128), lambda i: (i, 0, 0, 0, 0))
    evaluate, proj, scale = whole((POINTS + 128, 128)), whole((2 * ROWS, 2 * POINTS)), whole((3, ROWS, LANES))
    rows_shape = jax.ShapeDtypeStruct((XROWS, tall, LANES), F32)
    strip_shape = jax.ShapeDtypeStruct((steps, tall, 128), F32)
    state_shape = jax.ShapeDtypeStruct((16, 2, 2, SLOTS * FIELDS, 128), F32)
    params = pltpu.CompilerParams(vmem_limit_bytes=VMEM, dimension_semantics=("arbitrary",))
    neighbours = [rows, before, after, strip, strip, edge, edge]
    first = pl.pallas_call(
        first_kernel,
        grid=(steps,),
        in_specs=[smem, state, evaluate, proj, scale],
        out_specs=[rows, rows, rows, strip, strip],
        out_shape=[rows_shape, rows_shape, rows_shape, strip_shape, strip_shape],
        compiler_params=params,
        name="first_section",
    )
    middle = pl.pallas_call(
        middle_kernel,
        grid=(steps,),
        in_specs=[rows, rows] + neighbours + [evaluate, proj, scale],
        out_specs=[rows, rows, strip, strip],
        out_shape=[rows_shape, rows_shape, strip_shape, strip_shape],
        compiler_params=params,
        name="second_section",
    )
    final = pl.pallas_call(
        last_kernel,
        grid=(steps,),
        in_specs=[smem, rows] + neighbours + [scale],
        out_specs=state,
        out_shape=state_shape,
        compiler_params=params,
        name="advanced",
    )
    return first, middle, final


def ring(size, step):
    return [(i, (i + step) % size) for i in range(size)]


def exchange(east, low, high):
    before = lax.ppermute(east[XROWS - 2 :], "gx_hi", ring(lax.axis_size("gx_hi"), 1))
    after = lax.ppermute(east[:2], "gx_hi", ring(lax.axis_size("gx_hi"), -1))
    axes = ("gx_lo", "gy", "mode")
    place = [(chip * 2 + side) * 2 + core for side in range(2) for chip in range(8) for core in range(2)]
    up = [(place[i], place[(i + 1) % 32]) for i in range(32)]
    below = lax.ppermute(high, axes, up)
    above = lax.ppermute(low, axes, [(b, a) for a, b in up])
    return above, below, before, after


def shards(chaos_state, mode_group, mode_degrees):
    big = jnp.where(jnp.sum(mode_group) == SLOTS, 1, 0).astype(jnp.int32).reshape(1)
    evaluate, proj, scale = make_tables(mode_group, mode_degrees)
    first, middle, final = kernels()
    blocks = chaos_state.reshape(2, SLOTS, FIELDS, 16, 2, 128).transpose(3, 0, 4, 1, 2, 5)
    blocks = blocks.reshape(16, 2, 2, SLOTS * FIELDS, 128)
    tile = lax.all_to_all(blocks, ("gx_lo", "mode"), 0, 0, tiled=True)
    coef, east, following, low, high = first(big, tile, evaluate, proj, scale)
    above, below, before, after = exchange(east, low, high)
    east, following, low, high = middle(coef, following, east, east, east, above, below, before, after, evaluate, proj, scale)
    above, below, before, after = exchange(east, low, high)
    tile = final(big, following, east, east, east, above, below, before, after, scale)
    blocks = lax.all_to_all(tile, ("gx_lo", "mode"), 0, 0, tiled=True)
    blocks = blocks.reshape(16, 2, 2, SLOTS, FIELDS, 128).transpose(1, 3, 4, 0, 2, 5)
    return blocks.reshape(2, SLOTS, FIELDS, 16 * LANES)


def solution(mesh):
    fine = Mesh(mesh.devices.reshape(4, 8, 2, 2), ("gx_hi", "gx_lo", "gy", "mode"))
    spec = P(("gx_hi", "gx_lo"), "mode", None, "gy")
    return jax.shard_map(shards, mesh=fine, in_specs=(spec, P(), P()), out_specs=spec, check_vma=False)
```

time: 415 us -> 178 us (0.43); the launches traced: 409 us -> 177 us
  matrix products: 113 us -> 0 us
  waiting for transfers between devices: 155 us -> 47.5 us
  blocking collectives: 0 us -> 46.5 us
  local copies, waits for them, and re-layouts: 66.2 us -> 21.5 us
  other arithmetic: 41.7 us -> 1.84 us
  Pallas kernels: 0 us -> 35.4 us
  between operations: 14 us -> 0.76 us
  starting transfers between devices: 18.7 us -> 23.7 us
    dot_general x15 -> x0, matrix products: 113 us -> none  [the longest x2 38.2 us: galerkin(): jnp.einsum('ps,xsfc->xpfc', slot_basis, lax.all_gather(modal, 'mode', axi...]
    ppermute x8, waiting for transfers between devices: 123 us -> 13.3 us  [the longest x2 4.85 us: exchange(): lax.ppermute(east[XROWS - 2:], 'gx_hi', ring(lax.axis_size('gx_hi'), 1))]
    all_to_all x0 -> x1, blocking collectives: none -> 46.5 us  [shards(): blocks = lax.all_to_all(tile, ('gx_lo', 'mode'), 0, 0, tiled=True)]
    pallas_call x0 -> x4, Pallas kernels: none -> 35.4 us  [the longest x1 15.6 us: shards(): middle(coef, following, east, east, east, above, below, before, after, ev...]
    all_to_all x0 -> x1, waiting for transfers between devices: none -> 34.2 us  [shards(): tile = lax.all_to_all(blocks, ('gx_lo', 'mode'), 0, 0, tiled=True)]
    all_gather x2 -> x0, waiting for transfers between devices: 31.5 us -> none  [galerkin(): lax.all_gather(modal, 'mode', axis=1, tiled=True)]
    add x3 -> x0, other arithmetic: 25.2 us -> none  [the longest x1 12.5 us: shards(): 0.5 * coefficients + 0.5 * (section + time_step * tendency(section))]
    slice x18 -> x2, local copies, waits for them, and re-layouts: 25.9 us -> 2.23 us  [exchange(): after = lax.ppermute(east[:2], 'gx_hi', ring(lax.axis_size('gx_hi'), -1))]
  transfers between devices with their start and end apart: 10 -> 9, of which waited for: 6 -> 9; matrix products, arithmetic and copies ran while one was open for 7% -> 3% of each run, Pallas kernels for 0% -> 1%
where the time goes in v1:
time: 178 us; the launch traced here: 177 us
  waiting for transfers between devices  47.5 us (27%)
  blocking collectives  46.5 us (26%)
  Pallas kernels  35.4 us (20%)
  starting transfers between devices  23.7 us (13%)
  local copies, waits for them, and re-layouts  21.5 us (12%)
  other arithmetic  1.84 us (1%)
    all_to_all x1, blocking collectives, shards(): blocks = lax.all_to_all(tile, ('gx_lo', 'mode'), 0, 0, tiled=True)  46.5 us
    all_to_all x1, waiting for transfers between devices, shards(): tile = lax.all_to_all(blocks, ('gx_lo', 'mode'), 0, 0, tiled=True)  34.2 us
    pallas_call x1, Pallas kernels, shards(): middle(coef, following, east, east, east, above, below, before, after, ev...  15.6 us
    pallas_call x1, Pallas kernels, shards(): coef, east, following, low, high = first(big, tile, evaluate, proj, scale)  10.2 us
    reshape x2, local copies, waits for them, and re-layouts, shards(): chaos_state.reshape(2, SLOTS, FIELDS, 16, 2, 128)  8.29 us
    all_to_all x1, starting transfers between devices, shards(): tile = lax.all_to_all(blocks, ('gx_lo', 'mode'), 0, 0, tiled=True)  7.97 us
    pallas_call x1, Pallas kernels, shards(): final(big, following, east, east, east, above, below, before, after, scale)  7.4 us
    ppermute x2, starting transfers between devices, exchange(): above = lax.ppermute(low, axes, [(b, a) for a, b in up])  7.32 us
  transfers between devices with their start and end apart: 9, of which 9 were waited for; matrix products, arithmetic and copies ran while one was open for 3% of the time, Pallas kernels for 1%

profile of v1, /device:TPU:1, one launch (start us, length us, event | category | flops | bytes accessed | tf_op | source)
XLA Modules:
  0.0 177.3 jit_solution(1604553938164593482)
XLA Ops:
  0.0 4.6 %reshape.16 = f32[2,24,4,16,2,128]{5,4,3,2,1,0:T(2,128)S(1)} reshape(f32[2,24,4,4096]{3,2,1,0:T(4,128)} %param.5) | data formatting | bytes 6291456 | tf_op jit(solution)/shard_map/reshape | solution.py:341
  4.6 3.7 %copy.6 = f32[2,24,4,16,2,128]{5,2,1,4,0,3:T(4,128)} copy(f32[2,24,4,16,2,128]{5,4,3,2,1,0:T(2,128)S(1)} %reshape.16) | data formatting | bytes 6291456 | tf_op jit(solution)/shard_map/reshape | solution.py:341
  8.3 0.0 copy-start.10
  8.3 0.0 copy-start.9
  8.3 8.0 %all-to-all-start = ((f32[16,2,2,96,128]{4,3,2,1,0:T(8,128)}), f32[16,2,2,96,128]{4,3,2,1,0:T(8,128)S(1)}, u32[]{:S(2)}, u32[]{:S(2)}) async-start(f32[16,2,2,96,128]{4,3,2,1,0:T(8,128)} %bitcast.13), calls=%async_computation | async-start | bytes 6291456 | tf_op jit(solution)/shard_map/all_to_all | solution.py:343
  16.3 0.0 copy-done.10
  16.3 1.3 convert_bitcast_fusion
  17.5 0.7 copy.7.gcol_ref
  18.2 0.0 copy-done.9
  18.2 0.6 convert_bitcast_fusion.2
  18.8 0.7 copy.8.degrees_ref
  20.2 2.2 %tables.1 = (bf16[224,128]{1,0:T(8,128)(2,1)}, bf16[80,192]{1,0:T(8,128)(2,1)}, f32[3,40,256]{2,1,0:T(8,128)}) custom-call(f32[1,35]{1,0:T(1,128)} %get-tuple-element.36.grow_ref, f32[35,1]{1,0:T(8,128)} %copy.7.gcol_ref, f32[35,4]{1,0:T(8,128)} %copy.8.degrees_ref, f32[4,35]{1,0:T(4,128)} %get-tuple-element.33.degrees_t_ref, ...), custom_call_target="tpu_custom_call" | custom-call | tf_op jit(solution)/shard_map/tables/pallas_call | solution.py:105
  22.4 34.2 %all-to-all-done.state_ref = f32[16,2,2,96,128]{4,3,2,1,0:T(8,128)S(1)} async-done(((f32[16,2,2,96,128]{4,3,2,1,0:T(8,128)}), f32[16,2,2,96,128]{4,3,2,1,0:T(8,128)S(1)}, u32[]{:S(2)}, u32[]{:S(2)}) %all-to-all-start) | async-done | bytes 3145760 | tf_op jit(solution)/shard_map/all_to_all | solution.py:343
  56.6 0.0 copy-start
  56.6 1.7 copy-done
  58.3 10.2 %first_section.1 = (f32[16,160,256]{2,1,0:T(8,128)}, f32[16,160,256]{2,1,0:T(8,128)}, f32[16,160,256]{2,1,0:T(8,128)}, f32[4,160,128]{2,1,0:T(8,128)}, f32[4,160,128]{2,1,0:T(8,128)}) custom-call(s32[1]{0:T(128)} %bitcast.big_ref, f32[16,2,2,96,128]{4,3,2,1,0:T(8,128)} %copy-done, bf16[224,128]{1,0:T(8,128)(2,1)} %get-tuple-element.17.eval_ref, ...), custom_call_target="tpu_custom_call" | custom-call | tf_op jit(solution)/shard_map/first_section/pallas_call | solution.py:344
  68.5 0.6 collective-permute-start
  69.1 4.3 %collective-permute-start.1 = (f32[4,160,128]{2,1,0:T(8,128)}, f32[4,160,128]{2,1,0:T(8,128)S(1)}, u32[]{:S(2)}, u32[]{:S(2)}) collective-permute-start(f32[4,160,128]{2,1,0:T(8,128)} %get-tuple-element.24), channel_id=1, source_target_pairs={{0,1},{1,4},{4,5},{5,8},{8,9},{9,12},{12,13},{13,16},{16,17},{17,2... | collective-permute-start | bytes 983048 | tf_op jit(solution)/shard_map/ppermute | solution.py:332
  73.4 1.1 fusion.1
  74.6 2.5 %collective-permute-start.3 = (f32[2,160,256]{2,1,0:T(8,128)S(1)}, f32[2,160,256]{2,1,0:T(8,128)S(1)}, u32[]{:S(2)}, u32[]{:S(2)}) collective-permute-start(f32[2,160,256]{2,1,0:T(8,128)S(1)} %get-tuple-element.31), channel_id=1, source_target_pairs={{0,96},{32,0},{64,32},{96,64},{1,97},{33,1},{65,33},{97,65},{2,98}... | collective-permute-start | bytes 983048 | tf_op jit(solution)/shard_map/ppermute | solution.py:328
  77.1 0.0 collective-permute-start.2
  77.1 1.2 collective-permute-done.low_ref
  78.3 0.0 copy-start.1
  78.3 1.7 collective-permute-done.1.high_ref
  80.0 1.1 collective-permute-done.3.edge_after
  81.1 3.1 %collective-permute-done.2.edge_before = f32[2,160,256]{2,1,0:T(8,128)S(1)} collective-permute-done((f32[2,160,256]{2,1,0:T(8,128)S(1)}, f32[2,160,256]{2,1,0:T(8,128)S(1)}, u32[]{:S(2)}, u32[]{:S(2)}) %collective-permute-start.2) | collective-permute-done | bytes 327712 | tf_op jit(solution)/shard_map/ppermute | solution.py:327
  84.2 0.0 copy-done.1
  84.2 0.0 copy-done.2
  84.2 0.0 copy-done.5
  84.3 0.7 copy-done.6
  85.0 15.6 %second_section.1 = (f32[16,160,256]{2,1,0:T(8,128)}, f32[16,160,256]{2,1,0:T(8,128)}, f32[4,160,128]{2,1,0:T(8,128)}, f32[4,160,128]{2,1,0:T(8,128)}) custom-call(f32[16,160,256]{2,1,0:T(8,128)} %get-tuple-element.20.coef_ref, f32[16,160,256]{2,1,0:T(8,128)} %get-tuple-element.21.next_ref, f32[16,160,256]{2,1,0:T(8,128)} %get-tuple-element.22.east_ref.before_ref.after_ref, ...), custom_call_target="tpu_custom_call" | custom-call | tf_op jit(solution)/shard_map/second_section/pallas_call | solution.py:346
  100.5 6.7 %collective-permute-start.4 = (f32[4,160,128]{2,1,0:T(8,128)}, f32[4,160,128]{2,1,0:T(8,128)S(1)}, u32[]{:S(2)}, u32[]{:S(2)}) collective-permute-start(f32[4,160,128]{2,1,0:T(8,128)} %get-tuple-element.27), channel_id=1, source_target_pairs={{1,0},{4,1},{5,4},{8,5},{9,8},{12,9},{13,12},{16,13},{17,16},{20,1... | collective-permute-start | bytes 983048 | tf_op jit(solution)/shard_map/ppermute | solution.py:333
  107.3 0.0 collective-permute-start.5
  107.3 1.1 fusion
  108.4 0.6 collective-permute-start.7
  109.0 0.9 collective-permute-start.6
  109.9 0.6 collective-permute-done.4.low_ref
  110.6 1.7 collective-permute-done.5.high_ref
  112.2 2.2 %collective-permute-done.7.edge_after = f32[2,160,256]{2,1,0:T(8,128)S(1)} collective-permute-done((f32[2,160,256]{2,1,0:T(8,128)S(1)}, f32[2,160,256]{2,1,0:T(8,128)S(1)}, u32[]{:S(2)}, u32[]{:S(2)}) %collective-permute-start.7) | collective-permute-done | bytes 327712 | tf_op jit(solution)/shard_map/ppermute | solution.py:328
  114.4 1.7 collective-permute-done.6.edge_before
  116.1 0.0 copy-done.3
  116.1 0.0 copy-done.4
  116.1 0.0 copy-done.7
  116.1 0.7 copy-done.8
  116.9 7.4 %advanced.1 = f32[16,2,2,96,128]{4,3,2,1,0:T(8,128)} custom-call(s32[1]{0:T(128)} %bitcast.big_ref, f32[16,160,256]{2,1,0:T(8,128)} %get-tuple-element.25.next_ref, f32[16,160,256]{2,1,0:T(8,128)} %get-tuple-element.26.east_ref.before_ref.after_ref, f32[16,160,256]{2,1,0:T(8,128)} %get-tuple-element.26.east_ref.before_ref.after_ref, ...), custom_call_target="tpu_custom_call" | custom-call | tf_op jit(solution)/shard_map/advanced/pallas_call | solution.py:348
  124.3 46.5 %all_to_all.10 = f32[16,2,2,96,128]{4,3,2,1,0:T(8,128)S(1)} all-to-all(f32[16,2,2,96,128]{4,3,2,1,0:T(8,128)} %advanced.1), channel_id=1, replica_groups=mesh['gx_hi'=4,'gx_lo'=8,'gy'=2,'mode'=2] {'gx_lo','mode'}, dimensions={0} | all-to-all | bytes 6291456 | tf_op jit(solution)/shard_map/all_to_all | solution.py:349
  170.8 2.4 %copy.9 = f32[2,24,4,16,2,128]{5,4,3,2,1,0:T(2,128)S(1)} copy(f32[2,24,4,16,2,128]{5,2,1,4,0,3:T(4,128)S(1)} %bitcast.14) | data formatting | bytes 6291456 | tf_op jit(solution)/shard_map/transpose | solution.py:350
  173.2 4.1 %reshape.19 = f32[2,24,4,4096]{3,2,1,0:T(4,128)} reshape(f32[2,24,4,16,2,128]{5,4,3,2,1,0:T(2,128)S(1)} %copy.9) | data formatting | bytes 6291456 | tf_op jit(solution)/shard_map/reshape | solution.py:351
  (7 shorter events, 0.0 us)
Async XLA Ops:
  8.3 8.0 %copy-start.10 = (s32[35]{0:T(128)S(1)}, s32[35]{0:T(128)}, u32[]{:S(2)}) copy-start(s32[35]{0:T(128)} %param.6) | copy-start | bytes 424
  8.3 9.9 %copy-start.9 = (s32[35,4]{0,1:T(4,128)S(1)}, s32[35,4]{0,1:T(4,128)}, u32[]{:S(2)}) copy-start(s32[35,4]{0,1:T(4,128)} %param.7) | copy-start | bytes 1684
  8.3 48.3 %all-to-all-start = ((f32[16,2,2,96,128]{4,3,2,1,0:T(8,128)}), f32[16,2,2,96,128]{4,3,2,1,0:T(8,128)S(1)}, u32[]{:S(2)}, u32[]{:S(2)}) async-start(f32[16,2,2,96,128]{4,3,2,1,0:T(8,128)} %bitcast.13), calls=%async_computation | async-start | bytes 6291456 | tf_op jit(solution)/shard_map/all_to_all | solution.py:343
  56.6 1.7 copy-start
  68.5 9.8 %collective-permute-start = (f32[4,160,128]{2,1,0:T(8,128)}, f32[4,160,128]{2,1,0:T(8,128)S(1)}, u32[]{:S(2)}, u32[]{:S(2)}) collective-permute-start(f32[4,160,128]{2,1,0:T(8,128)} %get-tuple-element.23), channel_id=1, source_target_pairs={{1,0},{4,1},{5,4},{8,5},{9,8},{12,9},{13,12},{16,13},{17,16},{20,1... | collective-permute-start | bytes 983048 | tf_op jit(solution)/shard_map/ppermute | solution.py:333
  69.1 10.9 %collective-permute-start.1 = (f32[4,160,128]{2,1,0:T(8,128)}, f32[4,160,128]{2,1,0:T(8,128)S(1)}, u32[]{:S(2)}, u32[]{:S(2)}) collective-permute-start(f32[4,160,128]{2,1,0:T(8,128)} %get-tuple-element.24), channel_id=1, source_target_pairs={{0,1},{1,4},{4,5},{5,8},{8,9},{9,12},{12,13},{13,16},{16,17},{17,2... | collective-permute-start | bytes 983048 | tf_op jit(solution)/shard_map/ppermute | solution.py:332
  74.6 6.6 %collective-permute-start.3 = (f32[2,160,256]{2,1,0:T(8,128)S(1)}, f32[2,160,256]{2,1,0:T(8,128)S(1)}, u32[]{:S(2)}, u32[]{:S(2)}) collective-permute-start(f32[2,160,256]{2,1,0:T(8,128)S(1)} %get-tuple-element.31), channel_id=1, source_target_pairs={{0,96},{32,0},{64,32},{96,64},{1,97},{33,1},{65,33},{97,65},{2,98}... | collective-permute-start | bytes 983048 | tf_op jit(solution)/shard_map/ppermute | solution.py:328
  77.1 7.1 %collective-permute-start.2 = (f32[2,160,256]{2,1,0:T(8,128)S(1)}, f32[2,160,256]{2,1,0:T(8,128)S(1)}, u32[]{:S(2)}, u32[]{:S(2)}) collective-permute-start(f32[2,160,256]{2,1,0:T(8,128)S(1)} %get-tuple-element.32), channel_id=1, source_target_pairs={{0,32},{32,64},{64,96},{96,0},{1,33},{33,65},{65,97},{97,1},{2,34}... | collective-permute-start | bytes 983048 | tf_op jit(solution)/shard_map/ppermute | solution.py:327
  78.3 5.9 %copy-start.1 = (f32[4,160,128]{2,1,0:T(8,128)}, f32[4,160,128]{2,1,0:T(8,128)S(1)}, u32[]{:S(2)}) copy-start(f32[4,160,128]{2,1,0:T(8,128)S(1)} %collective-permute-done.low_ref) | copy-start | bytes 983044
  80.0 4.3 %copy-start.2 = (f32[4,160,128]{2,1,0:T(8,128)}, f32[4,160,128]{2,1,0:T(8,128)S(1)}, u32[]{:S(2)}) copy-start(f32[4,160,128]{2,1,0:T(8,128)S(1)} %collective-permute-done.1.high_ref) | copy-start | bytes 983044
  81.1 3.1 %copy-start.5 = (f32[2,160,256]{2,1,0:T(8,128)}, f32[2,160,256]{2,1,0:T(8,128)S(1)}, u32[]{:S(2)}) copy-start(f32[2,160,256]{2,1,0:T(8,128)S(1)} %collective-permute-done.3.edge_after) | copy-start | bytes 983044
  84.2 0.7 copy-start.6
  100.5 10.0 %collective-permute-start.4 = (f32[4,160,128]{2,1,0:T(8,128)}, f32[4,160,128]{2,1,0:T(8,128)S(1)}, u32[]{:S(2)}, u32[]{:S(2)}) collective-permute-start(f32[4,160,128]{2,1,0:T(8,128)} %get-tuple-element.27), channel_id=1, source_target_pairs={{1,0},{4,1},{5,4},{8,5},{9,8},{12,9},{13,12},{16,13},{17,16},{20,1... | collective-permute-start | bytes 983048 | tf_op jit(solution)/shard_map/ppermute | solution.py:333
  107.3 5.0 %collective-permute-start.5 = (f32[4,160,128]{2,1,0:T(8,128)}, f32[4,160,128]{2,1,0:T(8,128)S(1)}, u32[]{:S(2)}, u32[]{:S(2)}) collective-permute-start(f32[4,160,128]{2,1,0:T(8,128)} %get-tuple-element.28), channel_id=1, source_target_pairs={{0,1},{1,4},{4,5},{5,8},{8,9},{9,12},{12,13},{13,16},{16,17},{17,2... | collective-permute-start | bytes 983048 | tf_op jit(solution)/shard_map/ppermute | solution.py:332
  108.4 6.0 %collective-permute-start.7 = (f32[2,160,256]{2,1,0:T(8,128)S(1)}, f32[2,160,256]{2,1,0:T(8,128)S(1)}, u32[]{:S(2)}, u32[]{:S(2)}) collective-permute-start(f32[2,160,256]{2,1,0:T(8,128)S(1)} %get-tuple-element.29), channel_id=1, source_target_pairs={{0,96},{32,0},{64,32},{96,64},{1,97},{33,1},{65,33},{97,65},{2,98}... | collective-permute-start | bytes 983048 | tf_op jit(solution)/shard_map/ppermute | solution.py:328
  109.0 7.1 %collective-permute-start.6 = (f32[2,160,256]{2,1,0:T(8,128)S(1)}, f32[2,160,256]{2,1,0:T(8,128)S(1)}, u32[]{:S(2)}, u32[]{:S(2)}) collective-permute-start(f32[2,160,256]{2,1,0:T(8,128)S(1)} %get-tuple-element.30), channel_id=1, source_target_pairs={{0,32},{32,64},{64,96},{96,0},{1,33},{33,65},{65,97},{97,1},{2,34}... | collective-permute-start | bytes 983048 | tf_op jit(solution)/shard_map/ppermute | solution.py:327
  110.6 5.6 %copy-start.3 = (f32[4,160,128]{2,1,0:T(8,128)}, f32[4,160,128]{2,1,0:T(8,128)S(1)}, u32[]{:S(2)}) copy-start(f32[4,160,128]{2,1,0:T(8,128)S(1)} %collective-permute-done.4.low_ref) | copy-start | bytes 983044
  112.2 3.9 %copy-start.4 = (f32[4,160,128]{2,1,0:T(8,128)}, f32[4,160,128]{2,1,0:T(8,128)S(1)}, u32[]{:S(2)}) copy-start(f32[4,160,128]{2,1,0:T(8,128)S(1)} %collective-permute-done.5.high_ref) | copy-start | bytes 983044
  114.4 1.7 copy-start.7
  116.1 0.7 copy-start.8

commit v2 on v1

v2 whole, which is shorter than its diff:
```python
import math

import jax
import jax.numpy as jnp
import numpy as np
from jax import lax
from jax.experimental import pallas as pl
from jax.experimental.pallas import tpu as pltpu
from jax.sharding import Mesh, PartitionSpec as P

MODES = 35
FIELDS = 4
QUAD = 81
POINTS = 96
NZ = 16
SLOTS = 24
REST = MODES - SLOTS
SMALL = 16
PIECE = 2 * MODES * FIELDS
FULL_AT = 2 * REST * FIELDS
ROWS = SLOTS + SMALL
LANES = 256
STRIP = 2 * NZ
XROWS = 16
STEP = 4
time_step = 0.05
LIMIT = 40 * 1024 * 1024
F32, BF16 = jnp.float32, jnp.bfloat16


def point_constants():
    p = np.arange(POINTS)
    live = (p < QUAD).astype(np.float64)
    digits = [(p // 3**k) % 3 - 1.0 for k in range(4)]
    xi = [math.sqrt(3.0) * d for d in digits]
    weight = live * np.prod([np.where(d == 0, 4.0, 1.0) for d in digits], axis=0)
    east = 1.2 + 0.5 * xi[0]
    north = 0.6 + 0.5 * xi[1]
    decay = -9.6 * np.exp(0.25 * xi[2])
    rows = np.stack(digits + [weight, east, north, decay]).astype(np.float32)
    cols = np.zeros((POINTS, 8), np.float32)
    cols[:, :4] = np.stack(digits, 1)
    cols[:, 4] = live
    return np.concatenate([rows, rows], axis=1), cols


def degree_factor(n, d):
    square = 3.0 * d * d - 1.0
    cubic = d * d * d - d
    return jnp.where(n == 0.0, 1.0, jnp.where(n == 1.0, d, jnp.where(n == 2.0, square, cubic)))


def degree_norm(n):
    third = 3.0 * math.sqrt(3.0) / math.sqrt(6.0)
    return jnp.where(n == 0.0, 1.0, jnp.where(n == 1.0, math.sqrt(3.0), jnp.where(n == 2.0, 1.0 / math.sqrt(2.0), third)))


def table_kernel(group_ref, degrees_ref, prow_ref, pcol_ref, eval_ref, proj_ref, scale_ref, big_ref):
    sub = lax.broadcasted_iota(jnp.int32, (MODES, MODES), 0)
    lane = lax.broadcasted_iota(jnp.int32, (MODES, MODES), 1)
    grow = group_ref[...].astype(F32)
    gcol = jnp.sum(jnp.where(sub == lane, grow, 0.0), axis=1, keepdims=True)
    degrees = degrees_ref[...].astype(F32)
    degrees_t = [jnp.sum(jnp.where(sub == lane, degrees[:, k : k + 1], 0.0), axis=0, keepdims=True) for k in range(4)]
    big_ref[0] = jnp.where(jnp.sum(grow) == float(SLOTS), 1, 0).astype(jnp.int32)
    same = gcol == grow
    rank_row = jnp.sum(jnp.where(same & (sub < lane), 1.0, 0.0), axis=0, keepdims=True)
    rank_col = jnp.sum(jnp.where(same & (lane < sub), 1.0, 0.0), axis=1, keepdims=True)
    ones = jnp.sum(grow, axis=1, keepdims=True)
    big = jnp.where(ones == float(SLOTS), 1.0, 0.0)
    place_row = jnp.where(grow == big, rank_row, rank_row + SLOTS)
    place_col = jnp.where(gcol == big, rank_col, rank_col + SLOTS)
    row_id = lax.broadcasted_iota(jnp.int32, (ROWS, MODES), 0).astype(F32)
    pick = jnp.where(row_id == place_row, 1.0, 0.0)
    live_col = jnp.sum(pick, axis=1, keepdims=True)
    degree_col = [jnp.sum(pick * degrees_t[k], axis=1, keepdims=True) for k in range(4)]
    lane_id = lax.broadcasted_iota(jnp.int32, (MODES, 128), 1)
    lane_row = jnp.where(lane_id < ROWS, lane_id, jnp.where(lane_id < 2 * ROWS, lane_id - ROWS, lane_id - 2 * ROWS)).astype(F32)
    pick_t = jnp.where(lane_row == place_col, 1.0, 0.0)
    live_row = jnp.sum(pick_t, axis=0, keepdims=True)
    degree_row = [jnp.sum(pick_t * degrees[:, k : k + 1], axis=0, keepdims=True) for k in range(4)]
    basis = live_row * pcol_ref[:, 4:5]
    for k in range(4):
        basis = basis * degree_factor(degree_row[k], pcol_ref[:, k : k + 1])
    projector = live_col * prow_ref[4:5, :]
    scale, inverse = live_col, live_col
    for k in range(4):
        projector = projector * degree_factor(degree_col[k], prow_ref[k : k + 1, :])
        norm = degree_norm(degree_col[k])
        scale = scale * norm
        inverse = inverse / norm
    column = lax.broadcasted_iota(jnp.int32, (1, 128), 1)
    eval_ref[0:POINTS, :] = jnp.where(column < 2 * ROWS, basis, 0.0).astype(BF16)
    linear = []
    for k in range(3):
        left = projector[:, :POINTS] * prow_ref[5 + k : 6 + k, :POINTS]
        full = jnp.dot(left, basis, precision=lax.Precision.HIGHEST, preferred_element_type=F32)
        first = full.astype(BF16).astype(F32)
        linear.append(jnp.where(column < 2 * ROWS, first, jnp.where(column < 3 * ROWS, full - first, 0.0)))
    linear.append(jnp.zeros((8, 128), F32))
    eval_ref[POINTS:, :] = jnp.concatenate(linear, axis=0).astype(BF16)
    proj_ref[...] = jnp.concatenate([projector, projector * prow_ref[3:4, :]], axis=0).astype(BF16)
    scale_ref[0] = jnp.broadcast_to(scale, (ROWS, LANES))
    scale_ref[1] = jnp.broadcast_to(scale * scale * (time_step / (24.0 * 1296.0)), (ROWS, LANES))
    scale_ref[2] = jnp.broadcast_to(inverse, (ROWS, LANES))


def make_tables(mode_group, mode_degrees):
    prow, pcol = point_constants()
    vmem = pl.BlockSpec(memory_space=pltpu.VMEM)
    return pl.pallas_call(
        table_kernel,
        in_specs=[vmem] * 4,
        out_specs=[vmem, vmem, vmem, pl.BlockSpec(memory_space=pltpu.SMEM)],
        out_shape=[
            jax.ShapeDtypeStruct((POINTS + 128, 128), BF16),
            jax.ShapeDtypeStruct((2 * ROWS, 2 * POINTS), BF16),
            jax.ShapeDtypeStruct((3, ROWS, LANES), F32),
            jax.ShapeDtypeStruct((1,), jnp.int32),
        ],
        name="tables",
    )(mode_group[None, :], mode_degrees, jnp.asarray(prow), jnp.asarray(pcol))


def lane_operators():
    source, target = np.meshgrid(np.arange(LANES), np.arange(LANES), indexing="ij")
    gap = source - target
    north = 8.0 * (gap == NZ) - 8.0 * (gap == -NZ) - 1.0 * (gap == 2 * NZ) + 1.0 * (gap == -2 * NZ)
    same_y = source // NZ == target // NZ
    turn = (source - target) % NZ
    laplace = same_y * (1.0 * (turn == 1) + 1.0 * (turn == NZ - 1) - 2.0 * (turn == 0))
    return jnp.asarray(np.stack([np.concatenate([m, m]) for m in (north, laplace)]), BF16)


def pieces_of(value):
    first = value.astype(BF16)
    return first, value - first.astype(F32)


def row_fluxes(fields, eval_ref, proj_ref, lanes_ref):
    points, east, north, source, laplace = [], [], [], [], []
    for value in fields:
        first, second = pieces_of(value)
        both = jnp.concatenate([first, second.astype(BF16)], axis=1)
        laplace.append(jnp.dot(both, lanes_ref[1], preferred_element_type=F32))
        first = first.astype(F32)
        stack = jnp.concatenate([first, second, first, jnp.zeros((8, LANES), F32)], axis=0).astype(BF16)
        result = jnp.dot(eval_ref[...], stack, preferred_element_type=F32)
        points.append(result[0:POINTS])
        east.append(result[POINTS : POINTS + ROWS])
        north.append(result[POINTS + ROWS : POINTS + 2 * ROWS])
        source.append(result[POINTS + 2 * ROWS : POINTS + 3 * ROWS])

    def project(a, b, both):
        product = points[a] * points[b]
        first, second = pieces_of(product)
        stack = jnp.concatenate([first, second.astype(BF16)], axis=0)
        left = proj_ref[...] if both else proj_ref[0:48, :]
        return jnp.dot(left, stack, preferred_element_type=F32)

    def couple(f, result):
        source[f] = source[f] + (3.6 * result[0:ROWS] + (1.08 * math.sqrt(3.0)) * result[ROWS : 2 * ROWS])

    east[0] = east[0] + project(0, 0, False)[0:ROWS]
    result = project(0, 1, True)
    east[1] = east[1] + result[0:ROWS]
    north[0] = north[0] + result[0:ROWS]
    couple(3, result)
    east[2] = east[2] + project(0, 2, False)[0:ROWS]
    result = project(0, 3, True)
    east[3] = east[3] + result[0:ROWS]
    couple(2, result)
    north[1] = north[1] + project(1, 1, False)[0:ROWS]
    result = project(1, 2, True)
    north[2] = north[2] + result[0:ROWS]
    couple(0, result)
    north[3] = north[3] + project(1, 3, False)[0:ROWS]
    couple(1, project(2, 3, True))
    return east, north, source, laplace


def emit_rows(g, rows_of, eval_ref, proj_ref, lanes_ref, scale_ref, east_ref, next_ref, low_ref, high_ref):
    lane = lax.broadcasted_iota(jnp.int32, (1, 128), 1)
    gain = scale_ref[1]
    low, high = [None] * FIELDS, [None] * FIELDS
    for r in range(STEP):
        fields, base, weight = rows_of(r)
        east, north, source, laplace = row_fluxes(fields, eval_ref, proj_ref, lanes_ref)
        here = (lane >= r * STRIP) & (lane < (r + 1) * STRIP)
        for f in range(FIELDS):
            rows = slice(f * ROWS, (f + 1) * ROWS)
            east_ref[STEP * g + r, rows, :] = east[f]
            first, second = pieces_of(north[f])
            slope = jnp.dot(jnp.concatenate([first, second.astype(BF16)], axis=1), lanes_ref[0], preferred_element_type=F32)
            known = gain * (source[f] - slope) + time_step * laplace[f]
            next_ref[STEP * g + r, rows, :] = base[f] + weight * known
            start = pltpu.roll(north[f][:, :128], r * STRIP, 1) if r else north[f][:, :128]
            end = north[f][:, 128:] if r == STEP - 1 else pltpu.roll(north[f][:, 128:], (r + 1) * STRIP, 1)
            low[f] = jnp.where(here, start, low[f]) if r else start
            high[f] = jnp.where(here, end, high[f]) if r else end
    for f in range(FIELDS):
        low_ref[g, f * ROWS : (f + 1) * ROWS, :] = low[f]
        high_ref[g, f * ROWS : (f + 1) * ROWS, :] = high[f]


def from_neighbours(g, r, f, row, low_ref, high_ref):
    rows = slice(f * ROWS, (f + 1) * ROWS)
    total = 8.0 * (row(r + 1, rows) - row(r - 1, rows)) - (row(r + 2, rows) - row(r - 2, rows))
    lane = lax.broadcasted_iota(jnp.int32, (1, 128), 1)
    below, above = high_ref[g, rows, :], low_ref[g, rows, :]
    if r:
        below = pltpu.roll(below, 128 - r * STRIP, 1)
    if r != STEP - 1:
        above = pltpu.roll(above, 96 - r * STRIP, 1)
    low = jnp.where(lane < STRIP, below, 0.0) - jnp.where(lane < NZ, 8.0, 0.0) * pltpu.roll(below, 128 - NZ, 1)
    high = jnp.where(lane >= 128 - NZ, 8.0, 0.0) * pltpu.roll(above, NZ, 1) - jnp.where(lane >= 128 - STRIP, above, 0.0)
    return total + jnp.concatenate([low, high], axis=1)


GROUPS = XROWS // STEP


def over_groups(outer, body):
    lax.fori_loop(0, 2, lambda i, _: (body((GROUPS - 1) * i if outer else 1 + i, i), 0)[1], 0)


def edges_of(east_ref, start_ref, end_ref):
    for k in range(2):
        start_ref[k] = east_ref[k]
        end_ref[k] = east_ref[XROWS - 2 + k]


def first_kernel(outer, *refs):
    state_ref, eval_ref, proj_ref, lanes_ref, scale_ref = refs[:5]
    coef_ref, east_ref, next_ref, low_ref, high_ref = refs[5:10] if outer else refs[10:15]

    def body(g, _):
        def rows_of(r):
            fields = []
            for f in range(FIELDS):
                halves = []
                for half in range(2):
                    full = state_ref[STEP * g + r, pl.ds(FULL_AT + half * SLOTS * FIELDS + f, SLOTS, stride=FIELDS), :]
                    rest = state_ref[STEP * g + r, pl.ds(half * REST * FIELDS + f, SMALL, stride=FIELDS), :]
                    halves.append(jnp.concatenate([full, rest], axis=0))
                value = scale_ref[0] * jnp.concatenate(halves, axis=1)
                coef_ref[STEP * g + r, f * ROWS : (f + 1) * ROWS, :] = value
                fields.append(value)
            return fields, fields, 1.0

        emit_rows(g, rows_of, eval_ref, proj_ref, lanes_ref, scale_ref, east_ref, next_ref, low_ref, high_ref)

    over_groups(outer, body)
    if outer:
        edges_of(east_ref, *refs[10:12])


def side_rows(outer, east_ref, edge_before, edge_after, side_ref):
    if outer:
        side_ref[0, 0:2] = edge_before[...]
        side_ref[0, 2:4] = east_ref[STEP : STEP + 2]
        side_ref[1, 0:2] = east_ref[XROWS - STEP - 2 : XROWS - STEP]
        side_ref[1, 2:4] = edge_after[...]

    def row_at(g, i):
        def row(k, rows):
            if outer and k < 0:
                return side_ref[i, k + 2, rows, :]
            if outer and k >= STEP:
                return side_ref[i, k - STEP + 2, rows, :]
            return east_ref[STEP * g + k, rows, :]

        return row

    return row_at


def middle_kernel(outer, *refs):
    coef_ref, following_ref, from_ref, below_ref, above_ref, eval_ref, proj_ref, lanes_ref, scale_ref = refs[:9]
    if outer:
        edges, (east_ref, next_ref, low_ref, high_ref), ends, side = refs[9:11], refs[15:19], refs[19:21], refs[21]
    else:
        edges, (east_ref, next_ref, low_ref, high_ref), ends, side = (None, None), refs[9:13], None, None
    row_at = side_rows(outer, from_ref, *edges, side)

    def body(g, i):
        def rows_of(r):
            section, base = [], []
            for f in range(FIELDS):
                rows = slice(f * ROWS, (f + 1) * ROWS)
                missing = from_neighbours(g, r, f, row_at(g, i), above_ref, below_ref)
                section.append(following_ref[STEP * g + r, rows, :] - scale_ref[1] * missing)
                base.append(0.5 * (coef_ref[STEP * g + r, rows, :] + section[f]))
            return section, base, 0.5

        emit_rows(g, rows_of, eval_ref, proj_ref, lanes_ref, scale_ref, east_ref, next_ref, low_ref, high_ref)

    over_groups(outer, body)
    if outer:
        edges_of(east_ref, *ends)


def last_kernel(outer, *refs):
    following_ref, from_ref, below_ref, above_ref, scale_ref = refs[:5]
    if outer:
        edges, state_ref, side = refs[5:7], refs[8], refs[9]
    else:
        edges, state_ref, side = (None, None), refs[5], None
    row_at = side_rows(outer, from_ref, *edges, side)

    def body(g, i):
        for r in range(STEP):
            for f in range(FIELDS):
                rows = slice(f * ROWS, (f + 1) * ROWS)
                missing = from_neighbours(g, r, f, row_at(g, i), above_ref, below_ref)
                value = scale_ref[2] * (following_ref[STEP * g + r, rows, :] - 0.5 * scale_ref[1] * missing)
                for half in range(2):
                    lanes = slice(half * 128, (half + 1) * 128)
                    state_ref[STEP * g + r, pl.ds(FULL_AT + half * SLOTS * FIELDS + f, SLOTS, stride=FIELDS), :] = value[:SLOTS, lanes]
                    state_ref[STEP * g + r, pl.ds(half * REST * FIELDS + f, REST, stride=FIELDS), :] = value[SLOTS:MODES, lanes]

    over_groups(outer, body)


TALL = FIELDS * ROWS
ROWS_SHAPE = jax.ShapeDtypeStruct((XROWS, TALL, LANES), F32)
EDGE_SHAPE = jax.ShapeDtypeStruct((2, TALL, LANES), F32)
STRIP_SHAPE = jax.ShapeDtypeStruct((GROUPS, TALL, 128), F32)
PIECES_SHAPE = jax.ShapeDtypeStruct((XROWS, PIECE, 128), F32)


def in_vmem(kernel, ins, outs, name, aliases={}, scratch=()):
    vmem = pl.BlockSpec(memory_space=pltpu.VMEM)
    return pl.pallas_call(
        kernel,
        in_specs=[vmem] * len(ins),
        out_specs=[vmem] * len(outs),
        out_shape=outs,
        input_output_aliases=aliases,
        scratch_shapes=list(scratch),
        compiler_params=pltpu.CompilerParams(vmem_limit_bytes=LIMIT),
        name=name,
    )(*ins)


SIDE = pltpu.VMEM((2, 4, TALL, LANES), F32)


def first_section(tile, tables):
    held = [ROWS_SHAPE] * 3 + [STRIP_SHAPE] * 2
    *outer, start, end = in_vmem(lambda *refs: first_kernel(True, *refs), [tile, *tables], held + [EDGE_SHAPE] * 2, "first_outer")
    known = in_vmem(lambda *refs: first_kernel(False, *refs), [tile, *tables, *outer], held, "first_inner", {5 + i: i for i in range(5)})
    return known, start, end


def second_section(coef, following, east, sides, tables):
    below, above, before, after = sides
    held = [ROWS_SHAPE] * 2 + [STRIP_SHAPE] * 2
    shared = [coef, following, east, below, above, *tables]
    inner = in_vmem(lambda *refs: middle_kernel(False, *refs), shared, held, "second_inner")
    *known, start, end = in_vmem(
        lambda *refs: middle_kernel(True, *refs), [*shared, before, after, *inner], held + [EDGE_SHAPE] * 2, "second_outer", {11 + i: i for i in range(4)}, [SIDE]
    )
    return known, start, end


def advanced(following, east, sides, scale):
    below, above, before, after = sides
    shared = [following, east, below, above, scale]
    (inner,) = in_vmem(lambda *refs: last_kernel(False, *refs), shared, [PIECES_SHAPE], "advanced_inner")
    (tile,) = in_vmem(lambda *refs: last_kernel(True, *refs), [*shared, before, after, inner], [PIECES_SHAPE], "advanced_outer", {7: 0}, [SIDE])
    return tile


CHUNK = 4


def pack_kernel(core_ref, state_ref, out_ref, done):
    copy = pltpu.make_async_copy(state_ref.at[1 - core_ref[0]], out_ref, done)
    copy.start()
    copy.wait()


def merge_kernel(core_ref, big_ref, own_ref, got_ref, out_ref):
    step = pl.program_id(0)
    own_big = core_ref[0] == big_ref[0]

    def put(read, slots, start):
        for block in range(CHUNK):
            for half in range(2):
                for s in range(slots):
                    row = start + (half * slots + s) * FIELDS
                    out_ref[step * CHUNK + block, row : row + FIELDS, :] = read(s, block * LANES + half * 128)

    def own(s, lane):
        return own_ref[0, s, :, lane : lane + 128]

    def got(s, lane):
        return got_ref[s, :, pl.ds(pl.multiple_of(step * (CHUNK * LANES) + lane, 128), 128)]

    @pl.when(own_big)
    def _():
        put(own, SLOTS, FULL_AT)
        put(got, REST, 0)

    @pl.when(jnp.logical_not(own_big))
    def _():
        put(own, REST, 0)
        put(got, SLOTS, FULL_AT)


def split_kernel(core_ref, big_ref, pieces_ref, out_ref, send_ref):
    step = pl.program_id(0)
    own_big = core_ref[0] == big_ref[0]

    def take(slots, start, write):
        for block in range(CHUNK):
            for half in range(2):
                for s in range(SLOTS):
                    row = start + (half * slots + s) * FIELDS
                    value = pieces_ref[step * CHUNK + block, row : row + FIELDS, :] if s < slots else jnp.zeros((FIELDS, 128), F32)
                    write(s, block * LANES + half * 128, value)

    def own(s, lane, value):
        out_ref[0, s, :, lane : lane + 128] = value

    def send(s, lane, value):
        send_ref[s, :, pl.ds(pl.multiple_of(step * (CHUNK * LANES) + lane, 128), 128)] = value

    @pl.when(own_big)
    def _():
        take(SLOTS, FULL_AT, own)
        take(REST, 0, send)

    @pl.when(jnp.logical_not(own_big))
    def _():
        take(REST, 0, own)
        take(SLOTS, FULL_AT, send)


def finish_kernel(core_ref, got_ref, _, out_ref, done):
    copy = pltpu.make_async_copy(got_ref, out_ref.at[1 - core_ref[0]], done)
    copy.start()
    copy.wait()


ROW_SHAPE = jax.ShapeDtypeStruct((SLOTS, FIELDS, 16 * LANES), F32)
STATE_SHAPE = jax.ShapeDtypeStruct((2, SLOTS, FIELDS, 16 * LANES), F32)


def moved(kernel, grid, scalars, ins, outs, shapes, name, aliases={}, scratch=()):
    spec = pltpu.PrefetchScalarGridSpec(num_scalar_prefetch=scalars, grid=grid, in_specs=ins, out_specs=outs, scratch_shapes=list(scratch))
    params = pltpu.CompilerParams(vmem_limit_bytes=LIMIT)
    return pl.pallas_call(kernel, grid_spec=spec, out_shape=shapes, input_output_aliases=aliases, compiler_params=params, name=name)


def movers():
    vmem = pl.BlockSpec(memory_space=pltpu.VMEM)
    anywhere = pl.BlockSpec(memory_space=pl.ANY)
    row = pl.BlockSpec((1, SLOTS, FIELDS, CHUNK * LANES), lambda i, core, *_: (core[0], 0, 0, i))
    grid, semaphore = (16 // CHUNK,), [pltpu.SemaphoreType.DMA]
    pack = moved(pack_kernel, (1,), 1, [anywhere], vmem, ROW_SHAPE, "pack", scratch=semaphore)
    merge = moved(merge_kernel, grid, 2, [row, vmem], vmem, PIECES_SHAPE, "merge")
    split = moved(split_kernel, grid, 2, [vmem], [row, vmem], [STATE_SHAPE, ROW_SHAPE], "split")
    finish = moved(finish_kernel, (1,), 1, [vmem, anywhere], anywhere, STATE_SHAPE, "finish", {2: 0}, semaphore)
    return pack, merge, split, finish


def ring(size, step):
    return [(i, (i + step) % size) for i in range(size)]


def exchange(start, end, low, high):
    size = lax.axis_size("gx_hi")
    before = lax.ppermute(end, "gx_hi", ring(size, 1))
    after = lax.ppermute(start, "gx_hi", ring(size, -1))
    axes = ("gx_lo", "gy", "mode")
    place = [(chip * 2 + side) * 2 + core for side in range(2) for chip in range(8) for core in range(2)]
    up = [(place[i], place[(i + 1) % 32]) for i in range(32)]
    below = lax.ppermute(high, axes, up)
    above = lax.ppermute(low, axes, [(b, a) for a, b in up])
    return below, above, before, after


def shards(chaos_state, mode_group, mode_degrees):
    core = lax.axis_index("mode").astype(jnp.int32).reshape(1)
    pack, merge, split, finish = movers()
    swap = [(0, 1), (1, 0)]
    got = lax.ppermute(pack(core, chaos_state), "mode", swap)
    evaluate, proj, scale, big = make_tables(mode_group, mode_degrees)
    tables = (evaluate, proj, lane_operators(), scale)
    pieces = merge(core, big, chaos_state, got)
    tile = lax.all_to_all(pieces, ("gx_lo", "mode"), 0, 0, tiled=True)
    (coef, east, following, low, high), start, end = first_section(tile, tables)
    sides = exchange(start, end, low, high)
    (east, following, low, high), start, end = second_section(coef, following, east, sides, tables)
    sides = exchange(start, end, low, high)
    tile = advanced(following, east, sides, scale)
    pieces = lax.all_to_all(tile, ("gx_lo", "mode"), 0, 0, tiled=True)
    state, send = split(core, big, pieces)
    return finish(core, lax.ppermute(send, "mode", swap), state)


def solution(mesh):
    fine = Mesh(mesh.devices.reshape(4, 8, 2, 2), ("gx_hi", "gx_lo", "gy", "mode"))
    spec = P(("gx_hi", "gx_lo"), "mode", None, "gy")
    return jax.shard_map(shards, mesh=fine, in_specs=(spec, P(), P()), out_specs=spec, check_vma=False)
```

time: 178 us -> 140 us (0.79)
  waiting for transfers between devices: 47.5 us -> 9.84 us
  blocking collectives: 46.5 us -> 73.7 us
  local copies, waits for them, and re-layouts: 21.5 us -> 4.11 us
  starting transfers between devices: 23.7 us -> 12.5 us
  Pallas kernels: 35.4 us -> 39.3 us
  other arithmetic: 1.84 us -> 0 us
    all_to_all x1 -> x0, waiting for transfers between devices: 34.2 us -> none  [shards(): tile = lax.all_to_all(blocks, ('gx_lo', 'mode'), 0, 0, tiled=True)]
    all_to_all x1 -> x2, blocking collectives: 46.5 us -> 73.7 us  [the longest x1 37.9 us: shards(): pieces = lax.all_to_all(tile, ('gx_lo', 'mode'), 0, 0, tiled=True)]
    reshape x3 -> x0, local copies, waits for them, and re-layouts: 12.4 us -> none  [the longest x2 8.29 us: shards(): chaos_state.reshape(2, SLOTS, FIELDS, 16, 2, 128)]
    all_to_all x1 -> x0, starting transfers between devices: 7.97 us -> none  [shards(): tile = lax.all_to_all(blocks, ('gx_lo', 'mode'), 0, 0, tiled=True)]
    ppermute x2, starting transfers between devices: 4.35 us -> 0.08 us  [exchange(): below = lax.ppermute(high, axes, up)]
    pallas_call x4 -> x11, Pallas kernels: 35.4 us -> 39.3 us  [the longest x6 29.2 us: in_vmem(): pl.pallas_call(kernel, in_specs=[vmem] * len(ins), out_specs=[vmem] * len...]
    ppermute x4 -> x6, starting transfers between devices: 4.09 us -> 7.69 us  [the longest x2 2.92 us: exchange(): after = lax.ppermute(start, 'gx_hi', ring(size, -1))]
    ppermute x2, waiting for transfers between devices: 3.32 us -> 0.54 us  [exchange(): below = lax.ppermute(high, axes, up)]
  transfers between devices with their start and end apart: 9 -> 10, of which waited for: 9 -> 5; matrix products, arithmetic and copies ran while one was open for 3% -> 0% of each run, Pallas kernels for 1% -> 8%
where the time goes in v2:
time: 140 us
  blocking collectives  73.7 us (53%)
  Pallas kernels  39.3 us (28%)
  starting transfers between devices  12.5 us (9%)
  waiting for transfers between devices  9.84 us (7%)
  local copies, waits for them, and re-layouts  4.11 us (3%)
    all_to_all x1, blocking collectives, shards(): pieces = lax.all_to_all(tile, ('gx_lo', 'mode'), 0, 0, tiled=True)  37.9 us
    all_to_all x1, blocking collectives, shards(): tile = lax.all_to_all(pieces, ('gx_lo', 'mode'), 0, 0, tiled=True)  35.8 us
    pallas_call x6, Pallas kernels, in_vmem(): pl.pallas_call(kernel, in_specs=[vmem] * len(ins), out_specs=[vmem] * len...  29.2 us
    ppermute x2, starting transfers between devices, exchange(): above = lax.ppermute(low, axes, [(b, a) for a, b in up])  4.69 us
    unnamed x17, local copies, waits for them, and re-layouts  4.11 us
    ppermute x1, waiting for transfers between devices, shards(): return finish(core, lax.ppermute(send, 'mode', swap), state)  3.04 us
    ppermute x2, waiting for transfers between devices, exchange(): before = lax.ppermute(end, 'gx_hi', ring(size, 1))  3.03 us
    ppermute x2, starting transfers between devices, exchange(): after = lax.ppermute(start, 'gx_hi', ring(size, -1))  2.92 us
  transfers between devices with their start and end apart: 10, of which 5 were waited for; matrix products, arithmetic and copies ran while one was open for 0% of the time, Pallas kernels for 8%

profile of v2, /device:TPU:1, one launch (start us, length us, event | category | flops | bytes accessed | tf_op | source)
XLA Modules:
  0.0 139.8 jit_solution(11417140616823493144)
XLA Ops:
  0.0 0.0 copy-start.7
  0.0 1.9 %copy-done.1 = f32[2,24,4,4096]{3,2,1,0:T(4,128)S(1)} copy-done((f32[2,24,4,4096]{3,2,1,0:T(4,128)S(1)}, f32[2,24,4,4096]{3,2,1,0:T(4,128)}, u32[]{:S(2)}) %copy-start.1) | copy-done | bytes 3145752
  1.9 1.3 pack.1
  3.2 1.5 %collective-permute-start = (f32[24,4,4096]{2,1,0:T(4,128)}, f32[24,4,4096]{2,1,0:T(4,128)}, u32[]{:S(2)}, u32[]{:S(2)}) collective-permute-start(f32[24,4,4096]{2,1,0:T(4,128)} %pack.1), channel_id=1, source_target_pairs={{0,1},{1,0},{2,3},{3,2},{4,5},{5,4},{6,7},{7,6},{8,9},{9,8},{10,11... | collective-permute-start | bytes 4718600 | tf_op jit(solution)/shard_map/ppermute | solution.py:489
  4.7 0.0 copy-done.7
  4.7 0.7 copy.18.degrees_ref
  5.4 2.2 %tables.1 = (bf16[224,128]{1,0:T(8,128)(2,1)}, bf16[80,192]{1,0:T(8,128)(2,1)}, f32[3,40,256]{2,1,0:T(8,128)}, s32[1]{0:T(128)}) custom-call(s32[1,35]{1,0:T(1,128)} %bitcast.2, s32[35,4]{1,0:T(8,128)} %copy.18.degrees_ref, f32[8,192]{1,0:T(8,128)} %constant.10.clone.prow_ref, f32[96,8]{1,0:T(8,128)} %constant.11.clone.pcol_ref), custom_call_target="tpu_custom_call" | custom-call | tf_op jit(solution)/shard_map/tables/pallas_call | solution.py:111
  7.6 0.4 collective-permute-done.got_ref
  8.1 0.0 copy-done.2
  8.1 2.8 %merge.1 = f32[16,280,128]{2,1,0:T(8,128)S(1)} custom-call(s32[1]{0:T(128)} %bitcast.core_ref, s32[1]{0:T(128)} %get-tuple-element.33.big_ref, f32[2,24,4,4096]{3,2,1,0:T(4,128)S(1)} %copy-done.2, f32[24,4,4096]{2,1,0:T(4,128)} %collective-permute-done.got_ref), custom_call_target="tpu_custom_call" | custom-call | tf_op jit(solution)/shard_map/merge/pallas_call | solution.py:492
  10.8 0.0 copy-start.3
  10.8 0.0 copy-start.4
  10.9 0.0 copy-start.5
  10.9 0.0 copy-start.6
  10.9 35.8 %all_to_all.10.refs_0_ = f32[16,280,128]{2,1,0:T(8,128)S(1)} all-to-all(f32[16,280,128]{2,1,0:T(8,128)S(1)} %merge.1), channel_id=1, replica_groups=mesh['gx_hi'=4,'gx_lo'=8,'gy'=2,'mode'=2] {'gx_lo','mode'}, dimensions={0} | all-to-all | bytes 4587520 | tf_op jit(solution)/shard_map/all_to_all | solution.py:493
  46.7 0.0 copy-done.3
  46.7 0.0 copy-done.4
  46.7 0.0 copy-done.5
  46.7 0.0 copy-done.6
  46.7 5.1 %first_outer.1 = (f32[16,160,256]{2,1,0:T(8,128)S(1)}, f32[16,160,256]{2,1,0:T(8,128)S(1)}, f32[16,160,256]{2,1,0:T(8,128)S(1)}, f32[4,160,128]{2,1,0:T(8,128)S(...) custom-call(f32[16,280,128]{2,1,0:T(8,128)S(1)} %all_to_all.10.refs_0_, ...), custom_call_target="tpu_custom_call" | custom-call | tf_op jit(solution)/shard_map/first_outer/pallas_call | solution.py:334
  51.8 5.1 %first_inner.1 = (f32[16,160,256]{2,1,0:T(8,128)S(1)}, f32[16,160,256]{2,1,0:T(8,128)S(1)}, f32[16,160,256]{2,1,0:T(8,128)S(1)}, f32[4,160,128]{2,1,0:T(8,128)S(1)}, f32[4,160,128]{2,1,0:T(8,128)S(1)}) custom-call(f32[16,280,128]{2,1,0:T(8,128)S(1)} %all_to_all.10.refs_0_, ...), custom_call_target="tpu_custom_call", output_to_operand_aliasing={{0}: (5, {}), {1}: (6, {}), {2}: (7, {}), {3}: (8, {}), {4}... | custom-call | tf_op jit(solution)/shard_map/first_inner/pallas_call | solution.py:334
  57.0 0.0 copy-start
  57.0 1.5 %copy-done = f32[16,160,256]{2,1,0:T(8,128)} copy-done((f32[16,160,256]{2,1,0:T(8,128)}, f32[16,160,256]{2,1,0:T(8,128)S(1)}, u32[]{:S(2)}) %copy-start) | copy-done | bytes 2621464
  58.5 0.0 collective-permute-start.1
  58.5 0.8 collective-permute-start.2
  59.3 1.2 collective-permute-start.3
  60.5 1.5 %collective-permute-start.4 = (f32[2,160,256]{2,1,0:T(8,128)S(1)}, f32[2,160,256]{2,1,0:T(8,128)S(1)}, u32[]{:S(2)}, u32[]{:S(2)}) collective-permute-start(f32[2,160,256]{2,1,0:T(8,128)S(1)} %get-tuple-element.48), channel_id=1, source_target_pairs={{0,96},{32,0},{64,32},{96,64},{1,97},{33,1},{65,33},{97,65},{2,98}... | collective-permute-start | bytes 983048 | tf_op jit(solution)/shard_map/ppermute | solution.py:476
  61.9 0.5 collective-permute-done.1.refs_3_
  62.5 2.8 %collective-permute-done.2.refs_4_ = f32[4,160,128]{2,1,0:T(8,128)S(1)} collective-permute-done((f32[4,160,128]{2,1,0:T(8,128)S(1)}, f32[4,160,128]{2,1,0:T(8,128)S(1)}, u32[]{:S(2)}, u32[]{:S(2)}) %collective-permute-start.2) | collective-permute-done | bytes 327712 | tf_op jit(solution)/shard_map/ppermute | solution.py:481
  65.2 7.6 %second_inner.1 = (f32[16,160,256]{2,1,0:T(8,128)S(1)}, f32[16,160,256]{2,1,0:T(8,128)S(1)}, f32[4,160,128]{2,1,0:T(8,128)S(1)}, f32[4,160,128]{2,1,0:T(8,128)S(1)}) custom-call(f32[16,160,256]{2,1,0:T(8,128)S(1)} %get-tuple-element.42.refs_0_, f32[16,160,256]{2,1,0:T(8,128)S(1)} %get-tuple-element.43.refs_1_, f32[16,160,256]{2,1,0:T(8,128)} %copy-done, ...), custom_call_target="tpu_custom_call" | custom-call | tf_op jit(solution)/shard_map/second_inner/pallas_call | solution.py:334
  72.8 0.0 collective-permute-done.3.refs_9_
  72.8 0.0 collective-permute-done.4.refs_10_
  72.8 7.8 %second_outer.1 = (f32[16,160,256]{2,1,0:T(8,128)S(1)}, f32[16,160,256]{2,1,0:T(8,128)S(1)}, f32[4,160,128]{2,1,0:T(8,128)S(1)}, f32[4,160,128]{2,1,0:T(8,128)S(...) custom-call(f32[16,160,256]{2,1,0:T(8,128)S(1)} %get-tuple-element.4, ...), custom_call_target="tpu_custom_call", output_to_operand_aliasing={{0}: (11, {}), {1}: (12, {}), {2}: (13, {}), {3}: (14, {})} | custom-call | tf_op jit(solution)/shard_map/second_outer/pallas_call | solution.py:334
  80.7 0.1 collective-permute-start.5
  80.7 3.9 %collective-permute-start.6 = (f32[4,160,128]{2,1,0:T(8,128)S(1)}, f32[4,160,128]{2,1,0:T(8,128)S(1)}, u32[]{:S(2)}, u32[]{:S(2)}) collective-permute-start(f32[4,160,128]{2,1,0:T(8,128)S(1)} %get-tuple-element.56), channel_id=1, source_target_pairs={{1,0},{4,1},{5,4},{8,5},{9,8},{12,9},{13,12},{16,13},{17,16},{20,1... | collective-permute-start | bytes 983048 | tf_op jit(solution)/shard_map/ppermute | solution.py:481
  84.6 1.2 collective-permute-start.7
  85.8 1.5 %collective-permute-start.8 = (f32[2,160,256]{2,1,0:T(8,128)S(1)}, f32[2,160,256]{2,1,0:T(8,128)S(1)}, u32[]{:S(2)}, u32[]{:S(2)}) collective-permute-start(f32[2,160,256]{2,1,0:T(8,128)S(1)} %get-tuple-element.58), channel_id=1, source_target_pairs={{0,96},{32,0},{64,32},{96,64},{1,97},{33,1},{65,33},{97,65},{2,98}... | collective-permute-start | bytes 983048 | tf_op jit(solution)/shard_map/ppermute | solution.py:476
  87.3 0.0 collective-permute-done.5.refs_2_
  87.3 0.0 collective-permute-done.6.refs_3_
  87.3 1.7 %advanced_inner.1.refs_7_ = f32[16,280,128]{2,1,0:T(8,128)S(1)} custom-call(f32[16,160,256]{2,1,0:T(8,128)S(1)} %get-tuple-element.53.refs_0_, f32[16,160,256]{2,1,0:T(8,128)S(1)} %get-tuple-element.54.refs_1_, f32[4,160,128]{2,1,0:T(8,128)S(1)} %collective-permute-done.5.refs_2_, f32[4,160,128]{2,1,0:T(8,128)S(1)} %collective-permute-done.6.refs_3_, ...), custom_call_target="tpu_custom_call" | custom-call | tf_op jit(solution)/shard_map/advanced_inner/pallas_call | solution.py:334
  89.0 3.0 %collective-permute-done.7.refs_5_ = f32[2,160,256]{2,1,0:T(8,128)S(1)} collective-permute-done((f32[2,160,256]{2,1,0:T(8,128)S(1)}, f32[2,160,256]{2,1,0:T(8,128)S(1)}, u32[]{:S(2)}, u32[]{:S(2)}) %collective-permute-start.7) | collective-permute-done | bytes 327712 | tf_op jit(solution)/shard_map/ppermute | solution.py:475
  92.1 0.0 collective-permute-done.8.refs_6_
  92.1 1.9 %advanced_outer.1 = f32[16,280,128]{2,1,0:T(8,128)S(1)} custom-call(f32[16,160,256]{2,1,0:T(8,128)S(1)} %get-tuple-element.53.refs_0_, f32[16,160,256]{2,1,0:T(8,128)S(1)} %get-tuple-element.54.refs_1_, f32[4,160,128]{2,1,0:T(8,128)S(1)} %collective-permute-done.5.refs_2_, ...), custom_call_target="tpu_custom_call", output_to_operand_aliasing={{}: (7, {})} | custom-call | tf_op jit(solution)/shard_map/advanced_outer/pallas_call | solution.py:334
  93.9 37.9 %all_to_all.11.pieces_ref = f32[16,280,128]{2,1,0:T(8,128)S(1)} all-to-all(f32[16,280,128]{2,1,0:T(8,128)S(1)} %advanced_outer.1), channel_id=1, replica_groups=mesh['gx_hi'=4,'gx_lo'=8,'gy'=2,'mode'=2] {'gx_lo','mode'}, dimensions={0} | all-to-all | bytes 4587520 | tf_op jit(solution)/shard_map/all_to_all | solution.py:499
  131.9 2.7 %split.1 = (f32[2,24,4,4096]{3,2,1,0:T(4,128)}, f32[24,4,4096]{2,1,0:T(4,128)S(1)}) custom-call(s32[1]{0:T(128)} %bitcast.core_ref, s32[1]{0:T(128)} %get-tuple-element.33.big_ref, f32[16,280,128]{2,1,0:T(8,128)S(1)} %all_to_all.11.pieces_ref), custom_call_target="tpu_custom_call" | custom-call | tf_op jit(solution)/shard_map/split/pallas_call | solution.py:500
  134.6 0.8 collective-permute-start.9
  135.4 3.0 %collective-permute-done.9.got_ref = f32[24,4,4096]{2,1,0:T(4,128)S(1)} collective-permute-done((f32[24,4,4096]{2,1,0:T(4,128)S(1)}, f32[24,4,4096]{2,1,0:T(4,128)S(1)}, u32[]{:S(2)}, u32[]{:S(2)}) %collective-permute-start.9) | collective-permute-done | bytes 1572896 | tf_op jit(solution)/shard_map/ppermute | solution.py:501
  138.4 1.1 finish.1
  (2 shorter events, 0.0 us)
Async XLA Ops:
  0.0 4.7 %copy-start.7 = (s32[35,4]{0,1:T(4,128)S(1)}, s32[35,4]{0,1:T(4,128)}, u32[]{:S(2)}) copy-start(s32[35,4]{0,1:T(4,128)} %param.8) | copy-start | bytes 1684
  0.0 1.9 %copy-start.1 = (f32[2,24,4,4096]{3,2,1,0:T(4,128)S(1)}, f32[2,24,4,4096]{3,2,1,0:T(4,128)}, u32[]{:S(2)}) copy-start(f32[2,24,4,4096]{3,2,1,0:T(4,128)} %own_ref.1) | copy-start | bytes 9437188
  1.9 6.2 %copy-start.2 = (f32[2,24,4,4096]{3,2,1,0:T(4,128)S(1)}, f32[2,24,4,4096]{3,2,1,0:T(4,128)}, u32[]{:S(2)}) copy-start(f32[2,24,4,4096]{3,2,1,0:T(4,128)} %own_ref.1) | copy-start | bytes 9437188
  3.2 4.9 %collective-permute-start = (f32[24,4,4096]{2,1,0:T(4,128)}, f32[24,4,4096]{2,1,0:T(4,128)}, u32[]{:S(2)}, u32[]{:S(2)}) collective-permute-start(f32[24,4,4096]{2,1,0:T(4,128)} %pack.1), channel_id=1, source_target_pairs={{0,1},{1,0},{2,3},{3,2},{4,5},{5,4},{6,7},{7,6},{8,9},{9,8},{10,11... | collective-permute-start | bytes 4718600 | tf_op jit(solution)/shard_map/ppermute | solution.py:489
  10.8 35.8 %copy-start.3 = (bf16[2,512,256]{2,1,0:T(8,128)(2,1)S(1)}, bf16[2,512,256]{2,1,0:T(8,128)(2,1)}, u32[]{:S(2)}) copy-start(bf16[2,512,256]{2,1,0:T(8,128)(2,1)} %constant.12.clone.refs_3_.refs_7_) | copy-start | bytes 1572868
  10.8 35.8 %copy-start.4 = (f32[3,40,256]{2,1,0:T(8,128)S(1)}, f32[3,40,256]{2,1,0:T(8,128)}, u32[]{:S(2)}) copy-start(f32[3,40,256]{2,1,0:T(8,128)} %get-tuple-element.36.refs_4_.refs_8_) | copy-start | bytes 368644
  10.9 35.8 %copy-start.5 = (bf16[224,128]{1,0:T(8,128)(2,1)S(1)}, bf16[224,128]{1,0:T(8,128)(2,1)}, u32[]{:S(2)}) copy-start(bf16[224,128]{1,0:T(8,128)(2,1)} %get-tuple-element.34.refs_1_.refs_5_) | copy-start | bytes 172036
  10.9 35.8 %copy-start.6 = (bf16[80,192]{1,0:T(8,128)(2,1)S(1)}, bf16[80,192]{1,0:T(8,128)(2,1)}, u32[]{:S(2)}) copy-start(bf16[80,192]{1,0:T(8,128)(2,1)} %get-tuple-element.35.refs_2_.refs_6_) | copy-start | bytes 92164
  57.0 1.5 %copy-start = (f32[16,160,256]{2,1,0:T(8,128)}, f32[16,160,256]{2,1,0:T(8,128)S(1)}, u32[]{:S(2)}) copy-start(f32[16,160,256]{2,1,0:T(8,128)S(1)} %get-tuple-element.44.refs_2_) | copy-start | bytes 7864324
  58.5 4.0 %collective-permute-start.1 = (f32[4,160,128]{2,1,0:T(8,128)S(1)}, f32[4,160,128]{2,1,0:T(8,128)S(1)}, u32[]{:S(2)}, u32[]{:S(2)}) collective-permute-start(f32[4,160,128]{2,1,0:T(8,128)S(1)} %get-tuple-element.45), channel_id=1, source_target_pairs={{0,1},{1,4},{4,5},{5,8},{8,9},{9,12},{12,13},{13,16},{16,17},{17,2... | collective-permute-start | bytes 983048 | tf_op jit(solution)/shard_map/ppermute | solution.py:480
  58.5 6.8 %collective-permute-start.2 = (f32[4,160,128]{2,1,0:T(8,128)S(1)}, f32[4,160,128]{2,1,0:T(8,128)S(1)}, u32[]{:S(2)}, u32[]{:S(2)}) collective-permute-start(f32[4,160,128]{2,1,0:T(8,128)S(1)} %get-tuple-element.46), channel_id=1, source_target_pairs={{1,0},{4,1},{5,4},{8,5},{9,8},{12,9},{13,12},{16,13},{17,16},{20,1... | collective-permute-start | bytes 983048 | tf_op jit(solution)/shard_map/ppermute | solution.py:481
  59.3 13.6 %collective-permute-start.3 = (f32[2,160,256]{2,1,0:T(8,128)S(1)}, f32[2,160,256]{2,1,0:T(8,128)S(1)}, u32[]{:S(2)}, u32[]{:S(2)}) collective-permute-start(f32[2,160,256]{2,1,0:T(8,128)S(1)} %get-tuple-element.47), channel_id=1, source_target_pairs={{0,32},{32,64},{64,96},{96,0},{1,33},{33,65},{65,97},{97,1},{2,34}... | collective-permute-start | bytes 983048 | tf_op jit(solution)/shard_map/ppermute | solution.py:475
  60.5 12.4 %collective-permute-start.4 = (f32[2,160,256]{2,1,0:T(8,128)S(1)}, f32[2,160,256]{2,1,0:T(8,128)S(1)}, u32[]{:S(2)}, u32[]{:S(2)}) collective-permute-start(f32[2,160,256]{2,1,0:T(8,128)S(1)} %get-tuple-element.48), channel_id=1, source_target_pairs={{0,96},{32,0},{64,32},{96,64},{1,97},{33,1},{65,33},{97,65},{2,98}... | collective-permute-start | bytes 983048 | tf_op jit(solution)/shard_map/ppermute | solution.py:476
  80.7 6.7 %collective-permute-start.5 = (f32[4,160,128]{2,1,0:T(8,128)S(1)}, f32[4,160,128]{2,1,0:T(8,128)S(1)}, u32[]{:S(2)}, u32[]{:S(2)}) collective-permute-start(f32[4,160,128]{2,1,0:T(8,128)S(1)} %get-tuple-element.55), channel_id=1, source_target_pairs={{0,1},{1,4},{4,5},{5,8},{8,9},{9,12},{12,13},{13,16},{16,17},{17,2... | collective-permute-start | bytes 983048 | tf_op jit(solution)/shard_map/ppermute | solution.py:480
  80.7 6.6 %collective-permute-start.6 = (f32[4,160,128]{2,1,0:T(8,128)S(1)}, f32[4,160,128]{2,1,0:T(8,128)S(1)}, u32[]{:S(2)}, u32[]{:S(2)}) collective-permute-start(f32[4,160,128]{2,1,0:T(8,128)S(1)} %get-tuple-element.56), channel_id=1, source_target_pairs={{1,0},{4,1},{5,4},{8,5},{9,8},{12,9},{13,12},{16,13},{17,16},{20,1... | collective-permute-start | bytes 983048 | tf_op jit(solution)/shard_map/ppermute | solution.py:481
  84.6 7.4 %collective-permute-start.7 = (f32[2,160,256]{2,1,0:T(8,128)S(1)}, f32[2,160,256]{2,1,0:T(8,128)S(1)}, u32[]{:S(2)}, u32[]{:S(2)}) collective-permute-start(f32[2,160,256]{2,1,0:T(8,128)S(1)} %get-tuple-element.57), channel_id=1, source_target_pairs={{0,32},{32,64},{64,96},{96,0},{1,33},{33,65},{65,97},{97,1},{2,34}... | collective-permute-start | bytes 983048 | tf_op jit(solution)/shard_map/ppermute | solution.py:475
  85.8 6.2 %collective-permute-start.8 = (f32[2,160,256]{2,1,0:T(8,128)S(1)}, f32[2,160,256]{2,1,0:T(8,128)S(1)}, u32[]{:S(2)}, u32[]{:S(2)}) collective-permute-start(f32[2,160,256]{2,1,0:T(8,128)S(1)} %get-tuple-element.58), channel_id=1, source_target_pairs={{0,96},{32,0},{64,32},{96,64},{1,97},{33,1},{65,33},{97,65},{2,98}... | collective-permute-start | bytes 983048 | tf_op jit(solution)/shard_map/ppermute | solution.py:476
  134.6 3.9 %collective-permute-start.9 = (f32[24,4,4096]{2,1,0:T(4,128)S(1)}, f32[24,4,4096]{2,1,0:T(4,128)S(1)}, u32[]{:S(2)}, u32[]{:S(2)}) collective-permute-start(f32[24,4,4096]{2,1,0:T(4,128)S(1)} %get-tuple-element.59), channel_id=1, source_target_pairs={{0,1},{1,0},{2,3},{3,2},{4,5},{5,4},{6,7},{7,6},{8,9},{9,8},{10,11... | collective-permute-start | bytes 4718600 | tf_op jit(solution)/shard_map/ppermute | solution.py:501

commit v3 on v2

--- a/solution.py
+++ b/solution.py
@@ -24,7 +24,7 @@
 XROWS = 16
 STEP = 4
 time_step = 0.05
-LIMIT = 40 * 1024 * 1024
+LIMIT = 10 * 1024 * 1024
 F32, BF16 = jnp.float32, jnp.bfloat16
 
 
@@ -179,7 +179,8 @@
     return east, north, source, laplace
 
 
-def emit_rows(g, rows_of, eval_ref, proj_ref, lanes_ref, scale_ref, east_ref, next_ref, low_ref, high_ref):
+def emit_rows(core_ref, g, i, rows_of, tables, east_ref, next_ref, inside_ref, outside_ref):
+    eval_ref, proj_ref, lanes_ref, scale_ref = tables
     lane = lax.broadcasted_iota(jnp.int32, (1, 128), 1)
     gain = scale_ref[1]
     low, high = [None] * FIELDS, [None] * FIELDS
@@ -198,16 +199,21 @@
             end = north[f][:, 128:] if r == STEP - 1 else pltpu.roll(north[f][:, 128:], (r + 1) * STRIP, 1)
             low[f] = jnp.where(here, start, low[f]) if r else start
             high[f] = jnp.where(here, end, high[f]) if r else end
-    for f in range(FIELDS):
-        low_ref[g, f * ROWS : (f + 1) * ROWS, :] = low[f]
-        high_ref[g, f * ROWS : (f + 1) * ROWS, :] = high[f]
-
-
-def from_neighbours(g, r, f, row, low_ref, high_ref):
+
+    def store(inside, outside):
+        for f in range(FIELDS):
+            inside_ref[i, f * ROWS : (f + 1) * ROWS, :] = inside[f]
+            outside_ref[i, f * ROWS : (f + 1) * ROWS, :] = outside[f]
+
+    pl.when(core_ref[0] == 0)(lambda: store(high, low))
+    pl.when(core_ref[0] == 1)(lambda: store(low, high))
+
+
+def from_neighbours(i, r, f, row, strips):
     rows = slice(f * ROWS, (f + 1) * ROWS)
     total = 8.0 * (row(r + 1, rows) - row(r - 1, rows)) - (row(r + 2, rows) - row(r - 2, rows))
     lane = lax.broadcasted_iota(jnp.int32, (1, 128), 1)
-    below, above = high_ref[g, rows, :], low_ref[g, rows, :]
+    below, above = strips[0, i, rows, :], strips[1, i, rows, :]
     if r:
         below = pltpu.roll(below, 128 - r * STRIP, 1)
     if r != STEP - 1:
@@ -230,11 +236,11 @@
         end_ref[k] = east_ref[XROWS - 2 + k]
 
 
-def first_kernel(outer, *refs):
-    state_ref, eval_ref, proj_ref, lanes_ref, scale_ref = refs[:5]
-    coef_ref, east_ref, next_ref, low_ref, high_ref = refs[5:10] if outer else refs[10:15]
-
-    def body(g, _):
+def first_kernel(outer, core_ref, *refs):
+    state_ref, tables = refs[0], refs[1:5]
+    coef_ref, east_ref, next_ref, inside_ref, outside_ref = refs[5:10] if outer else refs[8:13]
+
+    def body(g, i):
         def rows_of(r):
             fields = []
             for f in range(FIELDS):
@@ -243,16 +249,25 @@
                     full = state_ref[STEP * g + r, pl.ds(FULL_AT + half * SLOTS * FIELDS + f, SLOTS, stride=FIELDS), :]
                     rest = state_ref[STEP * g + r, pl.ds(half * REST * FIELDS + f, SMALL, stride=FIELDS), :]
                     halves.append(jnp.concatenate([full, rest], axis=0))
-                value = scale_ref[0] * jnp.concatenate(halves, axis=1)
+                value = tables[3][0] * jnp.concatenate(halves, axis=1)
                 coef_ref[STEP * g + r, f * ROWS : (f + 1) * ROWS, :] = value
                 fields.append(value)
             return fields, fields, 1.0
 
-        emit_rows(g, rows_of, eval_ref, proj_ref, lanes_ref, scale_ref, east_ref, next_ref, low_ref, high_ref)
+        emit_rows(core_ref, g, i, rows_of, tables, east_ref, next_ref, inside_ref, outside_ref)
 
     over_groups(outer, body)
     if outer:
         edges_of(east_ref, *refs[10:12])
+
+
+def neighbour_strips(core_ref, inside_ref, outside_ref, strips):
+    def hold(below_ref, above_ref):
+        strips[0] = below_ref[...]
+        strips[1] = above_ref[...]
+
+    pl.when(core_ref[0] == 0)(lambda: hold(outside_ref, inside_ref))
+    pl.when(core_ref[0] == 1)(lambda: hold(inside_ref, outside_ref))
 
 
 def side_rows(outer, east_ref, edge_before, edge_after, side_ref):
@@ -275,44 +290,47 @@
     return row_at
 
 
-def middle_kernel(outer, *refs):
-    coef_ref, following_ref, from_ref, below_ref, above_ref, eval_ref, proj_ref, lanes_ref, scale_ref = refs[:9]
+def middle_kernel(outer, core_ref, *refs):
+    coef_ref, following_ref, from_ref, inside_from, outside_from = refs[:5]
+    tables = refs[5:9]
     if outer:
-        edges, (east_ref, next_ref, low_ref, high_ref), ends, side = refs[9:11], refs[15:19], refs[19:21], refs[21]
+        edges, (east_ref, next_ref, inside_ref, outside_ref), ends, (strips, side) = refs[9:11], refs[11:15], refs[15:17], refs[17:]
     else:
-        edges, (east_ref, next_ref, low_ref, high_ref), ends, side = (None, None), refs[9:13], None, None
+        edges, (east_ref, next_ref, inside_ref, outside_ref), ends, (strips, side) = (None, None), refs[11:15], None, (refs[15], None)
     row_at = side_rows(outer, from_ref, *edges, side)
+    neighbour_strips(core_ref, inside_from, outside_from, strips)
 
     def body(g, i):
         def rows_of(r):
             section, base = [], []
             for f in range(FIELDS):
                 rows = slice(f * ROWS, (f + 1) * ROWS)
-                missing = from_neighbours(g, r, f, row_at(g, i), above_ref, below_ref)
-                section.append(following_ref[STEP * g + r, rows, :] - scale_ref[1] * missing)
+                missing = from_neighbours(i, r, f, row_at(g, i), strips)
+                section.append(following_ref[STEP * g + r, rows, :] - tables[3][1] * missing)
                 base.append(0.5 * (coef_ref[STEP * g + r, rows, :] + section[f]))
             return section, base, 0.5
 
-        emit_rows(g, rows_of, eval_ref, proj_ref, lanes_ref, scale_ref, east_ref, next_ref, low_ref, high_ref)
+        emit_rows(core_ref, g, i, rows_of, tables, east_ref, next_ref, inside_ref, outside_ref)
 
     over_groups(outer, body)
     if outer:
         edges_of(east_ref, *ends)
 
 
-def last_kernel(outer, *refs):
-    following_ref, from_ref, below_ref, above_ref, scale_ref = refs[:5]
+def last_kernel(outer, core_ref, *refs):
+    following_ref, from_ref, inside_from, outside_from, scale_ref = refs[:5]
     if outer:
-        edges, state_ref, side = refs[5:7], refs[8], refs[9]
+        edges, state_ref, (strips, side) = refs[5:7], refs[7], refs[8:]
     else:
-        edges, state_ref, side = (None, None), refs[5], None
+        edges, state_ref, (strips, side) = (None, None), refs[6], (refs[7], None)
     row_at = side_rows(outer, from_ref, *edges, side)
+    neighbour_strips(core_ref, inside_from, outside_from, strips)
 
     def body(g, i):
         for r in range(STEP):
             for f in range(FIELDS):
                 rows = slice(f * ROWS, (f + 1) * ROWS)
-                missing = from_neighbours(g, r, f, row_at(g, i), above_ref, below_ref)
+                missing = from_neighbours(i, r, f, row_at(g, i), strips)
                 value = scale_ref[2] * (following_ref[STEP * g + r, rows, :] - 0.5 * scale_ref[1] * missing)
                 for half in range(2):
                     lanes = slice(half * 128, (half + 1) * 128)
@@ -325,50 +343,60 @@
 TALL = FIELDS * ROWS
 ROWS_SHAPE = jax.ShapeDtypeStruct((XROWS, TALL, LANES), F32)
 EDGE_SHAPE = jax.ShapeDtypeStruct((2, TALL, LANES), F32)
-STRIP_SHAPE = jax.ShapeDtypeStruct((GROUPS, TALL, 128), F32)
+STRIP_SHAPE = jax.ShapeDtypeStruct((2, TALL, 128), F32)
 PIECES_SHAPE = jax.ShapeDtypeStruct((XROWS, PIECE, 128), F32)
-
-
-def in_vmem(kernel, ins, outs, name, aliases={}, scratch=()):
+SIDE = pltpu.VMEM((2, 4, TALL, LANES), F32)
+STRIPS = pltpu.VMEM((2, 2, TALL, 128), F32)
+
+
+def in_vmem(kernel, core, ins, outs, name, cost, aliases={}, scratch=()):
     vmem = pl.BlockSpec(memory_space=pltpu.VMEM)
     return pl.pallas_call(
         kernel,
-        in_specs=[vmem] * len(ins),
+        in_specs=[pl.BlockSpec(memory_space=pltpu.SMEM)] + [vmem] * len(ins),
         out_specs=[vmem] * len(outs),
         out_shape=outs,
-        input_output_aliases=aliases,
+        input_output_aliases={1 + i: o for i, o in aliases.items()},
         scratch_shapes=list(scratch),
+        cost_estimate=pl.CostEstimate(flops=int(cost * 1e9), bytes_accessed=int(cost * 3e6), transcendentals=0),
         compiler_params=pltpu.CompilerParams(vmem_limit_bytes=LIMIT),
         name=name,
-    )(*ins)
-
-
-SIDE = pltpu.VMEM((2, 4, TALL, LANES), F32)
-
-
-def first_section(tile, tables):
-    held = [ROWS_SHAPE] * 3 + [STRIP_SHAPE] * 2
-    *outer, start, end = in_vmem(lambda *refs: first_kernel(True, *refs), [tile, *tables], held + [EDGE_SHAPE] * 2, "first_outer")
-    known = in_vmem(lambda *refs: first_kernel(False, *refs), [tile, *tables, *outer], held, "first_inner", {5 + i: i for i in range(5)})
-    return known, start, end
-
-
-def second_section(coef, following, east, sides, tables):
-    below, above, before, after = sides
-    held = [ROWS_SHAPE] * 2 + [STRIP_SHAPE] * 2
-    shared = [coef, following, east, below, above, *tables]
-    inner = in_vmem(lambda *refs: middle_kernel(False, *refs), shared, held, "second_inner")
-    *known, start, end = in_vmem(
-        lambda *refs: middle_kernel(True, *refs), [*shared, before, after, *inner], held + [EDGE_SHAPE] * 2, "second_outer", {11 + i: i for i in range(4)}, [SIDE]
-    )
-    return known, start, end
-
-
-def advanced(following, east, sides, scale):
-    below, above, before, after = sides
-    shared = [following, east, below, above, scale]
-    (inner,) = in_vmem(lambda *refs: last_kernel(False, *refs), shared, [PIECES_SHAPE], "advanced_inner")
-    (tile,) = in_vmem(lambda *refs: last_kernel(True, *refs), [*shared, before, after, inner], [PIECES_SHAPE], "advanced_outer", {7: 0}, [SIDE])
+    )(core, *ins)
+
+
+def first_section(core, tile, tables):
+    def run(outer):
+        return lambda *refs: first_kernel(outer, *refs)
+
+    held, strips = [ROWS_SHAPE] * 3, [STRIP_SHAPE] * 2
+    *known, inside, outside, start, end = in_vmem(run(True), core, [tile, *tables], held + strips + [EDGE_SHAPE] * 2, "first_outer", 5)
+    outer = exchange_x(start, end) + exchange_y(inside, outside)
+    *known, inside, outside = in_vmem(run(False), core, [tile, *tables, *known], held + strips, "first_inner", 20, {5: 0, 6: 1, 7: 2})
+    return known, outer, exchange_y(inside, outside)
+
+
+def second_section(core, coef, following, east, outer, inner, tables):
+    def run(outer):
+        return lambda *refs: middle_kernel(outer, *refs)
+
+    held, strips = [ROWS_SHAPE] * 2, [STRIP_SHAPE] * 2
+    shared = [coef, following, east]
+    ins = [*shared, *outer[2:], *tables, *outer[:2]]
+    *known, inside, outside, start, end = in_vmem(run(True), core, ins, held + strips + [EDGE_SHAPE] * 2, "second_outer", 8, scratch=[STRIPS, SIDE])
+    outer = exchange_x(start, end) + exchange_y(inside, outside)
+    ins = [*shared, *inner, *tables, *known]
+    *known, inside, outside = in_vmem(run(False), core, ins, held + strips, "second_inner", 20, {9: 0, 10: 1}, [STRIPS])
+    return known, outer, exchange_y(inside, outside)
+
+
+def advanced(core, following, east, outer, inner, scale):
+    def run(outer):
+        return lambda *refs: last_kernel(outer, *refs)
+
+    ins = [following, east, *outer[2:], scale, *outer[:2]]
+    (tile,) = in_vmem(run(True), core, ins, [PIECES_SHAPE], "advanced_outer", 8, scratch=[STRIPS, SIDE])
+    ins = [following, east, *inner, scale, tile]
+    (tile,) = in_vmem(run(False), core, ins, [PIECES_SHAPE], "advanced_inner", 8, {5: 0}, [STRIPS])
     return tile
 
 
@@ -456,7 +484,7 @@
 
 def movers():
     vmem = pl.BlockSpec(memory_space=pltpu.VMEM)
-    anywhere = pl.BlockSpec(memory_space=pl.ANY)
+    anywhere = pl.BlockSpec(memory_space=pltpu.HBM)
     row = pl.BlockSpec((1, SLOTS, FIELDS, CHUNK * LANES), lambda i, core, *_: (core[0], 0, 0, i))
     grid, semaphore = (16 // CHUNK,), [pltpu.SemaphoreType.DMA]
     pack = moved(pack_kernel, (1,), 1, [anywhere], vmem, ROW_SHAPE, "pack", scratch=semaphore)
@@ -470,16 +498,16 @@
     return [(i, (i + step) % size) for i in range(size)]
 
 
-def exchange(start, end, low, high):
+def exchange_x(start, end):
     size = lax.axis_size("gx_hi")
-    before = lax.ppermute(end, "gx_hi", ring(size, 1))
-    after = lax.ppermute(start, "gx_hi", ring(size, -1))
-    axes = ("gx_lo", "gy", "mode")
+    return lax.ppermute(end, "gx_hi", ring(size, 1)), lax.ppermute(start, "gx_hi", ring(size, -1))
+
+
+def exchange_y(inside, outside):
     place = [(chip * 2 + side) * 2 + core for side in range(2) for chip in range(8) for core in range(2)]
-    up = [(place[i], place[(i + 1) % 32]) for i in range(32)]
-    below = lax.ppermute(high, axes, up)
-    above = lax.ppermute(low, axes, [(b, a) for a, b in up])
-    return below, above, before, after
+    pairs = [(place[i], place[(i + 1) % 32]) for i in range(1, 32, 2)]
+    swap = pairs + [(b, a) for a, b in pairs]
+    return lax.ppermute(inside, "mode", [(0, 1), (1, 0)]), lax.ppermute(outside, ("gx_lo", "gy", "mode"), swap)
 
 
 def shards(chaos_state, mode_group, mode_degrees):
@@ -491,11 +519,9 @@
     tables = (evaluate, proj, lane_operators(), scale)
     pieces = merge(core, big, chaos_state, got)
     tile = lax.all_to_all(pieces, ("gx_lo", "mode"), 0, 0, tiled=True)
-    (coef, east, following, low, high), start, end = first_section(tile, tables)
-    sides = exchange(start, end, low, high)
-    (east, following, low, high), start, end = second_section(coef, following, east, sides, tables)
-    sides = exchange(start, end, low, high)
-    tile = advanced(following, east, sides, scale)
+    (coef, east, following), outer, inner = first_section(core, tile, tables)
+    (east, following), outer, inner = second_section(core, coef, following, east, outer, inner, tables)
+    tile = advanced(core, following, east, outer, inner, scale)
     pieces = lax.all_to_all(tile, ("gx_lo", "mode"), 0, 0, tiled=True)
     state, send = split(core, big, pieces)
     return finish(core, lax.ppermute(send, "mode", swap), state)

time: 140 us -> 134 us (0.957)
  starting transfers between devices: 12.5 us -> 17.7 us
  waiting for transfers between devices: 9.84 us -> 6.31 us
  Pallas kernels: 39.3 us -> 36.1 us
  blocking collectives: 73.7 us -> 70.9 us
  local copies, waits for them, and re-layouts: 4.11 us -> 2.62 us
    ppermute x8 -> x12, starting transfers between devices: 10.1 us -> 15.4 us  [the longest x4 9.99 us: exchange_y(): lax.ppermute(inside, 'mode', [(0, 1), (1, 0)])]
    ppermute x8 -> x12, waiting for transfers between devices: 6.36 us -> 2.84 us  [the longest x4 2.82 us: exchange_y(): lax.ppermute(outside, ('gx_lo', 'gy', 'mode'), swap)]
    pallas_call x6, Pallas kernels: 29.2 us -> 26.1 us  [in_vmem(): pl.pallas_call(kernel, in_specs=[pl.BlockSpec(memory_space=pltpu.SMEM)] +...]
    all_to_all x1, blocking collectives: 37.9 us -> 35.1 us  [shards(): pieces = lax.all_to_all(tile, ('gx_lo', 'mode'), 0, 0, tiled=True)]
    unnamed x17 -> x15, local copies, waits for them, and re-layouts: 4.11 us -> 2.62 us
  transfers between devices with their start and end apart: 10 -> 14, of which waited for: 5 -> 3; matrix products, arithmetic and copies ran while one was open for 0% -> 1% of each run, Pallas kernels for 8% -> 16%
where the time goes in v3:
time: 134 us
  blocking collectives  70.9 us (53%)
  Pallas kernels  36.1 us (27%)
  starting transfers between devices  17.7 us (13%)
  waiting for transfers between devices  6.31 us (5%)
  local copies, waits for them, and re-layouts  2.62 us (2%)
    all_to_all x1, blocking collectives, shards(): tile = lax.all_to_all(pieces, ('gx_lo', 'mode'), 0, 0, tiled=True)  35.8 us
    all_to_all x1, blocking collectives, shards(): pieces = lax.all_to_all(tile, ('gx_lo', 'mode'), 0, 0, tiled=True)  35.1 us
    pallas_call x6, Pallas kernels, in_vmem(): pl.pallas_call(kernel, in_specs=[pl.BlockSpec(memory_space=pltpu.SMEM)] +...  26.1 us
    ppermute x4, starting transfers between devices, exchange_y(): lax.ppermute(inside, 'mode', [(0, 1), (1, 0)])  9.99 us
    ppermute x2, starting transfers between devices, exchange_x(): lax.ppermute(start, 'gx_hi', ring(size, -1))  4.13 us
    ppermute x1, waiting for transfers between devices, shards(): return finish(core, lax.ppermute(send, 'mode', swap), state)  3.04 us
    ppermute x4, waiting for transfers between devices, exchange_y(): lax.ppermute(outside, ('gx_lo', 'gy', 'mode'), swap)  2.82 us
    pallas_call x1, Pallas kernels, shards(): pieces = merge(core, big, chaos_state, got)  2.7 us
  transfers between devices with their start and end apart: 14, of which 3 were waited for; matrix products, arithmetic and copies ran while one was open for 1% of the time, Pallas kernels for 16%

profile of v3, /device:TPU:1, one launch (start us, length us, event | category | flops | bytes accessed | tf_op | source)
XLA Modules:
  0.0 134.0 jit_solution(5890988676881642100)
XLA Ops:
  0.0 1.9 %copy-done = f32[2,24,4,4096]{3,2,1,0:T(4,128)S(1)} copy-done((f32[2,24,4,4096]{3,2,1,0:T(4,128)S(1)}, f32[2,24,4,4096]{3,2,1,0:T(4,128)}, u32[]{:S(2)}) %copy-start) | copy-done | bytes 3145752
  1.9 1.3 pack.1
  3.2 1.5 %collective-permute-start = (f32[24,4,4096]{2,1,0:T(4,128)}, f32[24,4,4096]{2,1,0:T(4,128)}, u32[]{:S(2)}, u32[]{:S(2)}) collective-permute-start(f32[24,4,4096]{2,1,0:T(4,128)} %pack.1), channel_id=1, source_target_pairs={{0,1},{1,0},{2,3},{3,2},{4,5},{5,4},{6,7},{7,6},{8,9},{9,8},{10,11... | collective-permute-start | bytes 4718600 | tf_op jit(solution)/shard_map/ppermute | solution.py:517
  4.7 0.0 copy-done.6
  4.7 0.7 copy.14.degrees_ref
  5.4 2.2 %tables.1 = (bf16[224,128]{1,0:T(8,128)(2,1)}, bf16[80,192]{1,0:T(8,128)(2,1)}, f32[3,40,256]{2,1,0:T(8,128)}, s32[1]{0:T(128)}) custom-call(s32[1,35]{1,0:T(1,128)} %bitcast.2, s32[35,4]{1,0:T(8,128)} %copy.14.degrees_ref, f32[8,192]{1,0:T(8,128)} %constant.10.clone.prow_ref, f32[96,8]{1,0:T(8,128)} %constant.11.clone.pcol_ref), custom_call_target="tpu_custom_call" | custom-call | tf_op jit(solution)/shard_map/tables/pallas_call | solution.py:111
  7.6 0.4 collective-permute-done.got_ref
  8.1 0.0 copy-done.1
  8.1 2.7 %merge.1 = f32[16,280,128]{2,1,0:T(8,128)S(1)} custom-call(s32[1]{0:T(128)} %bitcast.core_ref.refs_0_, s32[1]{0:T(128)} %get-tuple-element.33.big_ref, f32[2,24,4,4096]{3,2,1,0:T(4,128)S(1)} %copy-done.1, f32[24,4,4096]{2,1,0:T(4,128)} %collective-permute-done.got_ref), custom_call_target="tpu_custom_call" | custom-call | tf_op jit(solution)/shard_map/merge/pallas_call | solution.py:520
  10.8 0.0 copy-start.2
  10.8 0.0 copy-start.5
  10.8 35.8 %all_to_all.10.refs_1_ = f32[16,280,128]{2,1,0:T(8,128)S(1)} all-to-all(f32[16,280,128]{2,1,0:T(8,128)S(1)} %merge.1), channel_id=1, replica_groups=mesh['gx_hi'=4,'gx_lo'=8,'gy'=2,'mode'=2] {'gx_lo','mode'}, dimensions={0} | all-to-all | bytes 4587520 | tf_op jit(solution)/shard_map/all_to_all | solution.py:521
  46.6 0.0 copy-done.3
  46.6 5.1 %first_outer.1 = (f32[16,160,256]{2,1,0:T(8,128)S(1)}, f32[16,160,256]{2,1,0:T(8,128)S(1)}, f32[16,160,256]{2,1,0:T(8,128)S(1)}, f32[2,160,128]{2,1,0:T(8,128)S(...) custom-call(s32[1]{0:T(128)} %bitcast.core_ref.refs_0_, ...), custom_call_target="tpu_custom_call" | custom-call | flops 5000000000 | bytes 15000000 | tf_op jit(solution)/shard_map/first_outer/pallas_call | solution.py:354
  51.8 0.9 collective-permute-start.3
  52.6 0.0 collective-permute-start.4
  52.6 1.2 collective-permute-start.5
  53.9 1.5 %collective-permute-start.6 = (f32[2,160,256]{2,1,0:T(8,128)S(1)}, f32[2,160,256]{2,1,0:T(8,128)S(1)}, u32[]{:S(2)}, u32[]{:S(2)}) collective-permute-start(f32[2,160,256]{2,1,0:T(8,128)S(1)} %get-tuple-element.48), channel_id=1, source_target_pairs={{0,96},{32,0},{64,32},{96,64},{1,97},{33,1},{65,33},{97,65},{2,98}... | collective-permute-start | bytes 983048 | tf_op jit(solution)/shard_map/ppermute | solution.py:503
  55.3 5.1 %first_inner.1 = (f32[16,160,256]{2,1,0:T(8,128)S(1)}, f32[16,160,256]{2,1,0:T(8,128)S(1)}, f32[16,160,256]{2,1,0:T(8,128)S(1)}, f32[2,160,128]{2,1,0:T(8,128)S(1)}, f32[2,160,128]{2,1,0:T(8,128)S(1)}) custom-call(s32[1]{0:T(128)} %bitcast.core_ref.refs_0_, ...), custom_call_target="tpu_custom_call", output_to_operand_aliasing={{0}: (6, {}), {1}: (7, {}), {2}: (8, {})} | custom-call | flops 20000000000 | bytes 60000000 | tf_op jit(solution)/shard_map/first_inner/pallas_call | solution.py:354
  60.4 3.2 %collective-permute-start.1 = (f32[2,160,128]{2,1,0:T(8,128)S(1)}, f32[2,160,128]{2,1,0:T(8,128)S(1)}, u32[]{:S(2)}, u32[]{:S(2)}) collective-permute-start(f32[2,160,128]{2,1,0:T(8,128)S(1)} %get-tuple-element.43), channel_id=1, source_target_pairs={{0,1},{1,0},{2,3},{3,2},{4,5},{5,4},{6,7},{7,6},{8,9},{9,8},{10,11... | collective-permute-start | bytes 491528 | tf_op jit(solution)/shard_map/ppermute | solution.py:510
  63.6 0.0 collective-permute-done.3.refs_4_
  63.6 0.0 collective-permute-start.2
  63.6 0.0 collective-permute-done.4.refs_5_
  63.6 0.0 collective-permute-done.5.refs_10_
  63.6 0.0 collective-permute-done.6.refs_11_
  63.6 6.1 %second_outer.1 = (f32[16,160,256]{2,1,0:T(8,128)S(1)}, f32[16,160,256]{2,1,0:T(8,128)S(1)}, f32[2,160,128]{2,1,0:T(8,128)S(1)}, f32[2,160,128]{2,1,0:T(8,128)S(...) custom-call(s32[1]{0:T(128)} %bitcast.core_ref.refs_0_, f32[16,160,256]{2,1,0:T(8,128)S(1)} %get-tuple-element.40.refs_1_, ...), custom_call_target="tpu_custom_call" | custom-call | flops 8000000000 | bytes 24000000 | tf_op jit(solution)/shard_map/second_outer/pallas_call | solution.py:354
  69.7 2.2 %collective-permute-start.9 = (f32[2,160,128]{2,1,0:T(8,128)S(1)}, f32[2,160,128]{2,1,0:T(8,128)S(1)}, u32[]{:S(2)}, u32[]{:S(2)}) collective-permute-start(f32[2,160,128]{2,1,0:T(8,128)S(1)} %get-tuple-element.55), channel_id=1, source_target_pairs={{0,1},{1,0},{2,3},{3,2},{4,5},{5,4},{6,7},{7,6},{8,9},{9,8},{10,11... | collective-permute-start | bytes 491528 | tf_op jit(solution)/shard_map/ppermute | solution.py:510
  71.9 0.0 collective-permute-start.10
  71.9 0.0 collective-permute-start.11
  72.0 0.0 collective-permute-done.1.refs_4_
  72.0 2.7 %collective-permute-start.12 = (f32[2,160,256]{2,1,0:T(8,128)S(1)}, f32[2,160,256]{2,1,0:T(8,128)S(1)}, u32[]{:S(2)}, u32[]{:S(2)}) collective-permute-start(f32[2,160,256]{2,1,0:T(8,128)S(1)} %get-tuple-element.58), channel_id=1, source_target_pairs={{0,96},{32,0},{64,32},{96,64},{1,97},{33,1},{65,33},{97,65},{2,98}... | collective-permute-start | bytes 983048 | tf_op jit(solution)/shard_map/ppermute | solution.py:503
  74.6 0.0 collective-permute-done.2.refs_5_
  74.6 6.2 %second_inner.1 = (f32[16,160,256]{2,1,0:T(8,128)S(1)}, f32[16,160,256]{2,1,0:T(8,128)S(1)}, f32[2,160,128]{2,1,0:T(8,128)S(1)}, f32[2,160,128]{2,1,0:T(8,128)S(1)}) custom-call(s32[1]{0:T(128)} %bitcast.core_ref.refs_0_, f32[16,160,256]{2,1,0:T(8,128)S(1)} %get-tuple-element.40.refs_1_, ...), custom_call_target="tpu_custom_call", output_to_operand_aliasing={{0}: (10, {}), {1}: (11, {})} | custom-call | flops 20000000000 | bytes 60000000 | tf_op jit(solution)/shard_map/second_inner/pallas_call | solution.py:354
  80.8 3.7 %collective-permute-start.7 = (f32[2,160,128]{2,1,0:T(8,128)S(1)}, f32[2,160,128]{2,1,0:T(8,128)S(1)}, u32[]{:S(2)}, u32[]{:S(2)}) collective-permute-start(f32[2,160,128]{2,1,0:T(8,128)S(1)} %get-tuple-element.53), channel_id=1, source_target_pairs={{0,1},{1,0},{2,3},{3,2},{4,5},{5,4},{6,7},{7,6},{8,9},{9,8},{10,11... | collective-permute-start | bytes 491528 | tf_op jit(solution)/shard_map/ppermute | solution.py:510
  84.5 0.0 collective-permute-done.9.refs_3_
  84.5 0.0 collective-permute-start.8
  84.5 0.0 collective-permute-done.10.refs_4_
  84.5 0.0 collective-permute-done.11.refs_6_
  84.5 0.0 collective-permute-done.12.refs_7_
  84.6 1.9 %advanced_outer.1.refs_6_ = f32[16,280,128]{2,1,0:T(8,128)S(1)} custom-call(s32[1]{0:T(128)} %bitcast.core_ref.refs_0_, f32[16,160,256]{2,1,0:T(8,128)S(1)} %get-tuple-element.51.refs_1_, f32[16,160,256]{2,1,0:T(8,128)S(1)} %get-tuple-element.52.refs_2_, f32[2,160,128]{2,1,0:T(8,128)S(1)} %collective-permute-done.9.refs_3_, ...), custom_call_target="tpu_custom_call" | custom-call | flops 8000000000 | bytes 24000000 | tf_op jit(solution)/shard_map/advanced_outer/pallas_call | solution.py:354
  86.4 0.0 collective-permute-done.7.refs_3_
  86.5 2.8 %collective-permute-done.8.refs_4_ = f32[2,160,128]{2,1,0:T(8,128)S(1)} collective-permute-done((f32[2,160,128]{2,1,0:T(8,128)S(1)}, f32[2,160,128]{2,1,0:T(8,128)S(1)}, u32[]{:S(2)}, u32[]{:S(2)}) %collective-permute-start.8) | collective-permute-done | bytes 163872 | tf_op jit(solution)/shard_map/ppermute | solution.py:510
  89.3 1.8 %advanced_inner.1 = f32[16,280,128]{2,1,0:T(8,128)S(1)} custom-call(s32[1]{0:T(128)} %bitcast.core_ref.refs_0_, f32[16,160,256]{2,1,0:T(8,128)S(1)} %get-tuple-element.51.refs_1_, f32[16,160,256]{2,1,0:T(8,128)S(1)} %get-tuple-element.52.refs_2_, f32[2,160,128]{2,1,0:T(8,128)S(1)} %collective-permute-done.7.refs_3_, ...), custom_call_target="tpu_custom_call", output_to_operand_aliasing={{}: (6, {})} | custom-call | flops 8000000000 | bytes 24000000 | tf_op jit(solution)/shard_map/advanced_inner/pallas_call | solution.py:354
  91.1 35.1 %all_to_all.11.pieces_ref = f32[16,280,128]{2,1,0:T(8,128)S(1)} all-to-all(f32[16,280,128]{2,1,0:T(8,128)S(1)} %advanced_inner.1), channel_id=1, replica_groups=mesh['gx_hi'=4,'gx_lo'=8,'gy'=2,'mode'=2] {'gx_lo','mode'}, dimensions={0} | all-to-all | bytes 4587520 | tf_op jit(solution)/shard_map/all_to_all | solution.py:525
  126.1 2.6 %split.1 = (f32[2,24,4,4096]{3,2,1,0:T(4,128)}, f32[24,4,4096]{2,1,0:T(4,128)S(1)}) custom-call(s32[1]{0:T(128)} %bitcast.core_ref.refs_0_, s32[1]{0:T(128)} %get-tuple-element.33.big_ref, f32[16,280,128]{2,1,0:T(8,128)S(1)} %all_to_all.11.pieces_ref), custom_call_target="tpu_custom_call" | custom-call | tf_op jit(solution)/shard_map/split/pallas_call | solution.py:526
  128.8 0.8 collective-permute-start.13
  129.6 3.0 %collective-permute-done.13.got_ref = f32[24,4,4096]{2,1,0:T(4,128)S(1)} collective-permute-done((f32[24,4,4096]{2,1,0:T(4,128)S(1)}, f32[24,4,4096]{2,1,0:T(4,128)S(1)}, u32[]{:S(2)}, u32[]{:S(2)}) %collective-permute-start.13) | collective-permute-done | bytes 1572896 | tf_op jit(solution)/shard_map/ppermute | solution.py:527
  132.6 1.1 finish.1
  (8 shorter events, 0.0 us)
Async XLA Ops:
  0.0 4.7 %copy-start.6 = (s32[35,4]{0,1:T(4,128)S(1)}, s32[35,4]{0,1:T(4,128)}, u32[]{:S(2)}) copy-start(s32[35,4]{0,1:T(4,128)} %param.8) | copy-start | bytes 1684
  0.0 1.9 %copy-start = (f32[2,24,4,4096]{3,2,1,0:T(4,128)S(1)}, f32[2,24,4,4096]{3,2,1,0:T(4,128)}, u32[]{:S(2)}) copy-start(f32[2,24,4,4096]{3,2,1,0:T(4,128)} %own_ref.1) | copy-start | bytes 9437188
  1.9 6.2 %copy-start.1 = (f32[2,24,4,4096]{3,2,1,0:T(4,128)S(1)}, f32[2,24,4,4096]{3,2,1,0:T(4,128)}, u32[]{:S(2)}) copy-start(f32[2,24,4,4096]{3,2,1,0:T(4,128)} %own_ref.1) | copy-start | bytes 9437188
  3.2 4.9 %collective-permute-start = (f32[24,4,4096]{2,1,0:T(4,128)}, f32[24,4,4096]{2,1,0:T(4,128)}, u32[]{:S(2)}, u32[]{:S(2)}) collective-permute-start(f32[24,4,4096]{2,1,0:T(4,128)} %pack.1), channel_id=1, source_target_pairs={{0,1},{1,0},{2,3},{3,2},{4,5},{5,4},{6,7},{7,6},{8,9},{9,8},{10,11... | collective-permute-start | bytes 4718600 | tf_op jit(solution)/shard_map/ppermute | solution.py:517
  10.8 35.8 %copy-start.2 = (f32[3,40,256]{2,1,0:T(8,128)S(1)}, f32[3,40,256]{2,1,0:T(8,128)}, u32[]{:S(2)}) copy-start(f32[3,40,256]{2,1,0:T(8,128)} %get-tuple-element.36.refs_5_.refs_9_) | copy-start | bytes 368644
  10.8 35.8 %copy-start.3 = (bf16[224,128]{1,0:T(8,128)(2,1)S(1)}, bf16[224,128]{1,0:T(8,128)(2,1)}, u32[]{:S(2)}) copy-start(bf16[224,128]{1,0:T(8,128)(2,1)} %get-tuple-element.34.refs_2_.refs_6_) | copy-start | bytes 172036
  10.8 35.8 %copy-start.4 = (bf16[80,192]{1,0:T(8,128)(2,1)S(1)}, bf16[80,192]{1,0:T(8,128)(2,1)}, u32[]{:S(2)}) copy-start(bf16[80,192]{1,0:T(8,128)(2,1)} %get-tuple-element.35.refs_3_.refs_7_) | copy-start | bytes 92164
  10.8 35.8 %copy-start.5 = (bf16[2,512,256]{2,1,0:T(8,128)(2,1)S(1)}, bf16[2,512,256]{2,1,0:T(8,128)(2,1)}, u32[]{:S(2)}) copy-start(bf16[2,512,256]{2,1,0:T(8,128)(2,1)} %constant.12.clone.refs_4_.refs_8_) | copy-start | bytes 1572868
  51.8 11.8 %collective-permute-start.3 = (f32[2,160,128]{2,1,0:T(8,128)S(1)}, f32[2,160,128]{2,1,0:T(8,128)S(1)}, u32[]{:S(2)}, u32[]{:S(2)}) collective-permute-start(f32[2,160,128]{2,1,0:T(8,128)S(1)} %get-tuple-element.45), channel_id=1, source_target_pairs={{0,1},{1,0},{2,3},{3,2},{4,5},{5,4},{6,7},{7,6},{8,9},{9,8},{10,11... | collective-permute-start | bytes 491528 | tf_op jit(solution)/shard_map/ppermute | solution.py:510
  52.6 11.0 %collective-permute-start.4 = (f32[2,160,128]{2,1,0:T(8,128)S(1)}, f32[2,160,128]{2,1,0:T(8,128)S(1)}, u32[]{:S(2)}, u32[]{:S(2)}) collective-permute-start(f32[2,160,128]{2,1,0:T(8,128)S(1)} %get-tuple-element.46), channel_id=1, source_target_pairs={{1,4},{5,8},{9,12},{13,16},{17,20},{21,24},{25,28},{29,2},{3,6},{7... | collective-permute-start | bytes 491528 | tf_op jit(solution)/shard_map/ppermute | solution.py:510
  52.6 11.0 %collective-permute-start.5 = (f32[2,160,256]{2,1,0:T(8,128)S(1)}, f32[2,160,256]{2,1,0:T(8,128)S(1)}, u32[]{:S(2)}, u32[]{:S(2)}) collective-permute-start(f32[2,160,256]{2,1,0:T(8,128)S(1)} %get-tuple-element.47), channel_id=1, source_target_pairs={{0,32},{32,64},{64,96},{96,0},{1,33},{33,65},{65,97},{97,1},{2,34}... | collective-permute-start | bytes 983048 | tf_op jit(solution)/shard_map/ppermute | solution.py:503
  53.9 9.8 %collective-permute-start.6 = (f32[2,160,256]{2,1,0:T(8,128)S(1)}, f32[2,160,256]{2,1,0:T(8,128)S(1)}, u32[]{:S(2)}, u32[]{:S(2)}) collective-permute-start(f32[2,160,256]{2,1,0:T(8,128)S(1)} %get-tuple-element.48), channel_id=1, source_target_pairs={{0,96},{32,0},{64,32},{96,64},{1,97},{33,1},{65,33},{97,65},{2,98}... | collective-permute-start | bytes 983048 | tf_op jit(solution)/shard_map/ppermute | solution.py:503
  60.4 11.5 %collective-permute-start.1 = (f32[2,160,128]{2,1,0:T(8,128)S(1)}, f32[2,160,128]{2,1,0:T(8,128)S(1)}, u32[]{:S(2)}, u32[]{:S(2)}) collective-permute-start(f32[2,160,128]{2,1,0:T(8,128)S(1)} %get-tuple-element.43), channel_id=1, source_target_pairs={{0,1},{1,0},{2,3},{3,2},{4,5},{5,4},{6,7},{7,6},{8,9},{9,8},{10,11... | collective-permute-start | bytes 491528 | tf_op jit(solution)/shard_map/ppermute | solution.py:510
  63.6 11.0 %collective-permute-start.2 = (f32[2,160,128]{2,1,0:T(8,128)S(1)}, f32[2,160,128]{2,1,0:T(8,128)S(1)}, u32[]{:S(2)}, u32[]{:S(2)}) collective-permute-start(f32[2,160,128]{2,1,0:T(8,128)S(1)} %get-tuple-element.44), channel_id=1, source_target_pairs={{1,4},{5,8},{9,12},{13,16},{17,20},{21,24},{25,28},{29,2},{3,6},{7... | collective-permute-start | bytes 491528 | tf_op jit(solution)/shard_map/ppermute | solution.py:510
  69.7 14.8 %collective-permute-start.9 = (f32[2,160,128]{2,1,0:T(8,128)S(1)}, f32[2,160,128]{2,1,0:T(8,128)S(1)}, u32[]{:S(2)}, u32[]{:S(2)}) collective-permute-start(f32[2,160,128]{2,1,0:T(8,128)S(1)} %get-tuple-element.55), channel_id=1, source_target_pairs={{0,1},{1,0},{2,3},{3,2},{4,5},{5,4},{6,7},{7,6},{8,9},{9,8},{10,11... | collective-permute-start | bytes 491528 | tf_op jit(solution)/shard_map/ppermute | solution.py:510
  71.9 12.6 %collective-permute-start.10 = (f32[2,160,128]{2,1,0:T(8,128)S(1)}, f32[2,160,128]{2,1,0:T(8,128)S(1)}, u32[]{:S(2)}, u32[]{:S(2)}) collective-permute-start(f32[2,160,128]{2,1,0:T(8,128)S(1)} %get-tuple-element.56), channel_id=1, source_target_pairs={{1,4},{5,8},{9,12},{13,16},{17,20},{21,24},{25,28},{29,2},{3,6},{7... | collective-permute-start | bytes 491528 | tf_op jit(solution)/shard_map/ppermute | solution.py:510
  71.9 12.6 %collective-permute-start.11 = (f32[2,160,256]{2,1,0:T(8,128)S(1)}, f32[2,160,256]{2,1,0:T(8,128)S(1)}, u32[]{:S(2)}, u32[]{:S(2)}) collective-permute-start(f32[2,160,256]{2,1,0:T(8,128)S(1)} %get-tuple-element.57), channel_id=1, source_target_pairs={{0,32},{32,64},{64,96},{96,0},{1,33},{33,65},{65,97},{97,1},{2,34}... | collective-permute-start | bytes 983048 | tf_op jit(solution)/shard_map/ppermute | solution.py:503
  72.0 12.6 %collective-permute-start.12 = (f32[2,160,256]{2,1,0:T(8,128)S(1)}, f32[2,160,256]{2,1,0:T(8,128)S(1)}, u32[]{:S(2)}, u32[]{:S(2)}) collective-permute-start(f32[2,160,256]{2,1,0:T(8,128)S(1)} %get-tuple-element.58), channel_id=1, source_target_pairs={{0,96},{32,0},{64,32},{96,64},{1,97},{33,1},{65,33},{97,65},{2,98}... | collective-permute-start | bytes 983048 | tf_op jit(solution)/shard_map/ppermute | solution.py:503
  80.8 5.6 %collective-permute-start.7 = (f32[2,160,128]{2,1,0:T(8,128)S(1)}, f32[2,160,128]{2,1,0:T(8,128)S(1)}, u32[]{:S(2)}, u32[]{:S(2)}) collective-permute-start(f32[2,160,128]{2,1,0:T(8,128)S(1)} %get-tuple-element.53), channel_id=1, source_target_pairs={{0,1},{1,0},{2,3},{3,2},{4,5},{5,4},{6,7},{7,6},{8,9},{9,8},{10,11... | collective-permute-start | bytes 491528 | tf_op jit(solution)/shard_map/ppermute | solution.py:510
  84.5 4.7 %collective-permute-start.8 = (f32[2,160,128]{2,1,0:T(8,128)S(1)}, f32[2,160,128]{2,1,0:T(8,128)S(1)}, u32[]{:S(2)}, u32[]{:S(2)}) collective-permute-start(f32[2,160,128]{2,1,0:T(8,128)S(1)} %get-tuple-element.54), channel_id=1, source_target_pairs={{1,4},{5,8},{9,12},{13,16},{17,20},{21,24},{25,28},{29,2},{3,6},{7... | collective-permute-start | bytes 491528 | tf_op jit(solution)/shard_map/ppermute | solution.py:510
  128.8 3.9 %collective-permute-start.13 = (f32[24,4,4096]{2,1,0:T(4,128)S(1)}, f32[24,4,4096]{2,1,0:T(4,128)S(1)}, u32[]{:S(2)}, u32[]{:S(2)}) collective-permute-start(f32[24,4,4096]{2,1,0:T(4,128)S(1)} %get-tuple-element.59), channel_id=1, source_target_pairs={{0,1},{1,0},{2,3},{3,2},{4,5},{5,4},{6,7},{7,6},{8,9},{9,8},{10,11... | collective-permute-start | bytes 4718600 | tf_op jit(solution)/shard_map/ppermute | solution.py:527

commit v4 on v3

--- a/solution.py
+++ b/solution.py
@@ -16,8 +16,10 @@
 SLOTS = 24
 REST = MODES - SLOTS
 SMALL = 16
-PIECE = 2 * MODES * FIELDS
-FULL_AT = 2 * REST * FIELDS
+BLOCKS = 16
+HALVES = 2 * FIELDS
+PIECE = MODES * HALVES
+FULL_AT = REST * HALVES
 ROWS = SLOTS + SMALL
 LANES = 256
 STRIP = 2 * NZ
@@ -137,14 +139,18 @@
     return first, value - first.astype(F32)
 
 
+def by_lanes(value, operator):
+    first, second = pieces_of(value)
+    return first, second, jnp.dot(jnp.concatenate([first, second.astype(BF16)], axis=1), operator, preferred_element_type=F32)
+
+
 def row_fluxes(fields, eval_ref, proj_ref, lanes_ref):
-    points, east, north, source, laplace = [], [], [], [], []
-    for value in fields:
-        first, second = pieces_of(value)
-        both = jnp.concatenate([first, second.astype(BF16)], axis=1)
-        laplace.append(jnp.dot(both, lanes_ref[1], preferred_element_type=F32))
-        first = first.astype(F32)
-        stack = jnp.concatenate([first, second, first, jnp.zeros((8, LANES), F32)], axis=0).astype(BF16)
+    points, east, north, source = [], [], [], []
+    first, second, laplace = by_lanes(jnp.concatenate(fields, axis=0), lanes_ref[1])
+    first = first.astype(F32)
+    for f in range(FIELDS):
+        rows = slice(f * ROWS, (f + 1) * ROWS)
+        stack = jnp.concatenate([first[rows], second[rows], first[rows], jnp.zeros((8, LANES), F32)], axis=0).astype(BF16)
         result = jnp.dot(eval_ref[...], stack, preferred_element_type=F32)
         points.append(result[0:POINTS])
         east.append(result[POINTS : POINTS + ROWS])
@@ -179,7 +185,7 @@
     return east, north, source, laplace
 
 
-def emit_rows(core_ref, g, i, rows_of, tables, east_ref, next_ref, inside_ref, outside_ref):
+def emit_rows(core_ref, g, at, rows_of, tables, east_ref, next_ref, inside_ref, outside_ref):
     eval_ref, proj_ref, lanes_ref, scale_ref = tables
     lane = lax.broadcasted_iota(jnp.int32, (1, 128), 1)
     gain = scale_ref[1]
@@ -188,12 +194,11 @@
         fields, base, weight = rows_of(r)
         east, north, source, laplace = row_fluxes(fields, eval_ref, proj_ref, lanes_ref)
         here = (lane >= r * STRIP) & (lane < (r + 1) * STRIP)
+        slope = by_lanes(jnp.concatenate(north, axis=0), lanes_ref[0])[2]
         for f in range(FIELDS):
             rows = slice(f * ROWS, (f + 1) * ROWS)
             east_ref[STEP * g + r, rows, :] = east[f]
-            first, second = pieces_of(north[f])
-            slope = jnp.dot(jnp.concatenate([first, second.astype(BF16)], axis=1), lanes_ref[0], preferred_element_type=F32)
-            known = gain * (source[f] - slope) + time_step * laplace[f]
+            known = gain * (source[f] - slope[rows]) + time_step * laplace[rows]
             next_ref[STEP * g + r, rows, :] = base[f] + weight * known
             start = pltpu.roll(north[f][:, :128], r * STRIP, 1) if r else north[f][:, :128]
             end = north[f][:, 128:] if r == STEP - 1 else pltpu.roll(north[f][:, 128:], (r + 1) * STRIP, 1)
@@ -202,8 +207,8 @@
 
     def store(inside, outside):
         for f in range(FIELDS):
-            inside_ref[i, f * ROWS : (f + 1) * ROWS, :] = inside[f]
-            outside_ref[i, f * ROWS : (f + 1) * ROWS, :] = outside[f]
+            inside_ref[at, f * ROWS : (f + 1) * ROWS, :] = inside[f]
+            outside_ref[at, f * ROWS : (f + 1) * ROWS, :] = outside[f]
 
     pl.when(core_ref[0] == 0)(lambda: store(high, low))
     pl.when(core_ref[0] == 1)(lambda: store(low, high))
@@ -246,8 +251,8 @@
             for f in range(FIELDS):
                 halves = []
                 for half in range(2):
-                    full = state_ref[STEP * g + r, pl.ds(FULL_AT + half * SLOTS * FIELDS + f, SLOTS, stride=FIELDS), :]
-                    rest = state_ref[STEP * g + r, pl.ds(half * REST * FIELDS + f, SMALL, stride=FIELDS), :]
+                    full = state_ref[STEP * g + r, pl.ds(FULL_AT + half * FIELDS + f, SLOTS, stride=HALVES), :]
+                    rest = state_ref[STEP * g + r, pl.ds(half * FIELDS + f, SMALL, stride=HALVES), :]
                     halves.append(jnp.concatenate([full, rest], axis=0))
                 value = tables[3][0] * jnp.concatenate(halves, axis=1)
                 coef_ref[STEP * g + r, f * ROWS : (f + 1) * ROWS, :] = value
@@ -296,7 +301,10 @@
     if outer:
         edges, (east_ref, next_ref, inside_ref, outside_ref), ends, (strips, side) = refs[9:11], refs[11:15], refs[15:17], refs[17:]
     else:
-        edges, (east_ref, next_ref, inside_ref, outside_ref), ends, (strips, side) = (None, None), refs[11:15], None, (refs[15], None)
+        edges, (east_ref, next_ref, inside_ref, outside_ref), ends, (strips, side) = (None, None), refs[13:17], None, (refs[17], None)
+        for given, held in ((refs[11], inside_ref), (refs[12], outside_ref)):
+            held[0] = given[0]
+            held[GROUPS - 1] = given[1]
     row_at = side_rows(outer, from_ref, *edges, side)
     neighbour_strips(core_ref, inside_from, outside_from, strips)
 
@@ -310,43 +318,41 @@
                 base.append(0.5 * (coef_ref[STEP * g + r, rows, :] + section[f]))
             return section, base, 0.5
 
-        emit_rows(core_ref, g, i, rows_of, tables, east_ref, next_ref, inside_ref, outside_ref)
+        emit_rows(core_ref, g, i if outer else g, rows_of, tables, east_ref, next_ref, inside_ref, outside_ref)
 
     over_groups(outer, body)
     if outer:
         edges_of(east_ref, *ends)
 
 
-def last_kernel(outer, core_ref, *refs):
-    following_ref, from_ref, inside_from, outside_from, scale_ref = refs[:5]
-    if outer:
-        edges, state_ref, (strips, side) = refs[5:7], refs[7], refs[8:]
-    else:
-        edges, state_ref, (strips, side) = (None, None), refs[6], (refs[7], None)
-    row_at = side_rows(outer, from_ref, *edges, side)
+def last_kernel(core_ref, following_ref, from_ref, inside_from, outside_from, scale_ref, edge_before, edge_after, state_ref, strips, side):
     neighbour_strips(core_ref, inside_from, outside_from, strips)
-
-    def body(g, i):
-        for r in range(STEP):
-            for f in range(FIELDS):
-                rows = slice(f * ROWS, (f + 1) * ROWS)
-                missing = from_neighbours(i, r, f, row_at(g, i), strips)
-                value = scale_ref[2] * (following_ref[STEP * g + r, rows, :] - 0.5 * scale_ref[1] * missing)
-                for half in range(2):
-                    lanes = slice(half * 128, (half + 1) * 128)
-                    state_ref[STEP * g + r, pl.ds(FULL_AT + half * SLOTS * FIELDS + f, SLOTS, stride=FIELDS), :] = value[:SLOTS, lanes]
-                    state_ref[STEP * g + r, pl.ds(half * REST * FIELDS + f, REST, stride=FIELDS), :] = value[SLOTS:MODES, lanes]
-
-    over_groups(outer, body)
+    for outer in (True, False):
+        row_at = side_rows(outer, from_ref, edge_before, edge_after, side)
+
+        def body(g, i):
+            for r in range(STEP):
+                for f in range(FIELDS):
+                    rows = slice(f * ROWS, (f + 1) * ROWS)
+                    missing = from_neighbours(g, r, f, row_at(g, i), strips)
+                    value = scale_ref[2] * (following_ref[STEP * g + r, rows, :] - 0.5 * scale_ref[1] * missing)
+                    for half in range(2):
+                        lanes = slice(half * 128, (half + 1) * 128)
+                        state_ref[STEP * g + r, pl.ds(FULL_AT + half * FIELDS + f, SLOTS, stride=HALVES), :] = value[:SLOTS, lanes]
+                        state_ref[STEP * g + r, pl.ds(half * FIELDS + f, REST, stride=HALVES), :] = value[SLOTS:MODES, lanes]
+
+        over_groups(outer, body)
 
 
 TALL = FIELDS * ROWS
 ROWS_SHAPE = jax.ShapeDtypeStruct((XROWS, TALL, LANES), F32)
 EDGE_SHAPE = jax.ShapeDtypeStruct((2, TALL, LANES), F32)
 STRIP_SHAPE = jax.ShapeDtypeStruct((2, TALL, 128), F32)
+STRIPS_SHAPE = jax.ShapeDtypeStruct((GROUPS, TALL, 128), F32)
 PIECES_SHAPE = jax.ShapeDtypeStruct((XROWS, PIECE, 128), F32)
 SIDE = pltpu.VMEM((2, 4, TALL, LANES), F32)
 STRIPS = pltpu.VMEM((2, 2, TALL, 128), F32)
+ALL_STRIPS = pltpu.VMEM((2, GROUPS, TALL, 128), F32)
 
 
 def in_vmem(kernel, core, ins, outs, name, cost, aliases={}, scratch=()):
@@ -383,87 +389,68 @@
     shared = [coef, following, east]
     ins = [*shared, *outer[2:], *tables, *outer[:2]]
     *known, inside, outside, start, end = in_vmem(run(True), core, ins, held + strips + [EDGE_SHAPE] * 2, "second_outer", 8, scratch=[STRIPS, SIDE])
-    outer = exchange_x(start, end) + exchange_y(inside, outside)
-    ins = [*shared, *inner, *tables, *known]
-    *known, inside, outside = in_vmem(run(False), core, ins, held + strips, "second_inner", 20, {9: 0, 10: 1}, [STRIPS])
-    return known, outer, exchange_y(inside, outside)
-
-
-def advanced(core, following, east, outer, inner, scale):
-    def run(outer):
-        return lambda *refs: last_kernel(outer, *refs)
-
-    ins = [following, east, *outer[2:], scale, *outer[:2]]
-    (tile,) = in_vmem(run(True), core, ins, [PIECES_SHAPE], "advanced_outer", 8, scratch=[STRIPS, SIDE])
-    ins = [following, east, *inner, scale, tile]
-    (tile,) = in_vmem(run(False), core, ins, [PIECES_SHAPE], "advanced_inner", 8, {5: 0}, [STRIPS])
-    return tile
-
-
-CHUNK = 4
-
-
-def pack_kernel(core_ref, state_ref, out_ref, done):
-    copy = pltpu.make_async_copy(state_ref.at[1 - core_ref[0]], out_ref, done)
+    edges = exchange_x(start, end)
+    ins = [*shared, *inner, *tables, *known, inside, outside]
+    *known, inside, outside = in_vmem(run(False), core, ins, held + [STRIPS_SHAPE] * 2, "second_inner", 20, {9: 0, 10: 1}, [STRIPS])
+    return known, edges, exchange_y(inside, outside)
+
+
+def advanced(core, following, east, edges, strips, scale):
+    ins = [following, east, *strips, scale, *edges]
+    return in_vmem(last_kernel, core, ins, [PIECES_SHAPE], "advanced", 8, scratch=[ALL_STRIPS, SIDE])[0]
+
+
+def group_rows(full):
+    return slice(REST, MODES) if full else slice(0, REST)
+
+
+def repeat(count, body):
+    lax.fori_loop(0, count, lambda i, _: (body(i), 0)[1], 0)
+
+
+def pack_kernel(core_ref, state_ref, out_ref):
+    row = 1 - core_ref[0]
+
+    def body(s):
+        out_ref[s] = state_ref[row, s]
+
+    repeat(SLOTS, body)
+
+
+def merge_kernel(core_ref, big_ref, state_ref, got_ref, out_ref):
+    core = core_ref[0]
+
+    def put(full):
+        def body(block):
+            out_ref[block, group_rows(full)] = state_ref[core, 0 : SLOTS if full else REST, block]
+            out_ref[block, group_rows(not full)] = got_ref[0 : REST if full else SLOTS, block]
+
+        repeat(BLOCKS, body)
+
+    pl.when(core == big_ref[0])(lambda: put(True))
+    pl.when(core != big_ref[0])(lambda: put(False))
+
+
+def split_kernel(own, core_ref, big_ref, pieces_ref, out_ref):
+    def get(full):
+        slots = SLOTS if full else REST
+
+        def body(block):
+            out_ref[0:slots, block] = pieces_ref[block, group_rows(full)]
+            if not full:
+                out_ref[slots:SLOTS, block] = jnp.zeros((SLOTS - slots, HALVES, 128), F32)
+
+        repeat(BLOCKS, body)
+
+    for full in (False, True):
+        pl.when((core_ref[0] == big_ref[0]) == (full == own))(lambda full=full: get(full))
+
+
+def split_own_kernel(core_ref, big_ref, pieces_ref, out_ref, row, done):
+    split_kernel(True, core_ref, big_ref, pieces_ref, row)
+    copy = pltpu.make_async_copy(row, out_ref.at[core_ref[0]], done)
     copy.start()
     copy.wait()
-
-
-def merge_kernel(core_ref, big_ref, own_ref, got_ref, out_ref):
-    step = pl.program_id(0)
-    own_big = core_ref[0] == big_ref[0]
-
-    def put(read, slots, start):
-        for block in range(CHUNK):
-            for half in range(2):
-                for s in range(slots):
-                    row = start + (half * slots + s) * FIELDS
-                    out_ref[step * CHUNK + block, row : row + FIELDS, :] = read(s, block * LANES + half * 128)
-
-    def own(s, lane):
-        return own_ref[0, s, :, lane : lane + 128]
-
-    def got(s, lane):
-        return got_ref[s, :, pl.ds(pl.multiple_of(step * (CHUNK * LANES) + lane, 128), 128)]
-
-    @pl.when(own_big)
-    def _():
-        put(own, SLOTS, FULL_AT)
-        put(got, REST, 0)
-
-    @pl.when(jnp.logical_not(own_big))
-    def _():
-        put(own, REST, 0)
-        put(got, SLOTS, FULL_AT)
-
-
-def split_kernel(core_ref, big_ref, pieces_ref, out_ref, send_ref):
-    step = pl.program_id(0)
-    own_big = core_ref[0] == big_ref[0]
-
-    def take(slots, start, write):
-        for block in range(CHUNK):
-            for half in range(2):
-                for s in range(SLOTS):
-                    row = start + (half * slots + s) * FIELDS
-                    value = pieces_ref[step * CHUNK + block, row : row + FIELDS, :] if s < slots else jnp.zeros((FIELDS, 128), F32)
-                    write(s, block * LANES + half * 128, value)
-
-    def own(s, lane, value):
-        out_ref[0, s, :, lane : lane + 128] = value
-
-    def send(s, lane, value):
-        send_ref[s, :, pl.ds(pl.multiple_of(step * (CHUNK * LANES) + lane, 128), 128)] = value
-
-    @pl.when(own_big)
-    def _():
-        take(SLOTS, FULL_AT, own)
-        take(REST, 0, send)
-
-    @pl.when(jnp.logical_not(own_big))
-    def _():
-        take(REST, 0, own)
-        take(SLOTS, FULL_AT, send)
 
 
 def finish_kernel(core_ref, got_ref, _, out_ref, done):
@@ -472,26 +459,39 @@
     copy.wait()
 
 
-ROW_SHAPE = jax.ShapeDtypeStruct((SLOTS, FIELDS, 16 * LANES), F32)
-STATE_SHAPE = jax.ShapeDtypeStruct((2, SLOTS, FIELDS, 16 * LANES), F32)
-
-
-def moved(kernel, grid, scalars, ins, outs, shapes, name, aliases={}, scratch=()):
-    spec = pltpu.PrefetchScalarGridSpec(num_scalar_prefetch=scalars, grid=grid, in_specs=ins, out_specs=outs, scratch_shapes=list(scratch))
-    params = pltpu.CompilerParams(vmem_limit_bytes=LIMIT)
-    return pl.pallas_call(kernel, grid_spec=spec, out_shape=shapes, input_output_aliases=aliases, compiler_params=params, name=name)
-
-
-def movers():
-    vmem = pl.BlockSpec(memory_space=pltpu.VMEM)
-    anywhere = pl.BlockSpec(memory_space=pltpu.HBM)
-    row = pl.BlockSpec((1, SLOTS, FIELDS, CHUNK * LANES), lambda i, core, *_: (core[0], 0, 0, i))
-    grid, semaphore = (16 // CHUNK,), [pltpu.SemaphoreType.DMA]
-    pack = moved(pack_kernel, (1,), 1, [anywhere], vmem, ROW_SHAPE, "pack", scratch=semaphore)
-    merge = moved(merge_kernel, grid, 2, [row, vmem], vmem, PIECES_SHAPE, "merge")
-    split = moved(split_kernel, grid, 2, [vmem], [row, vmem], [STATE_SHAPE, ROW_SHAPE], "split")
-    finish = moved(finish_kernel, (1,), 1, [vmem, anywhere], anywhere, STATE_SHAPE, "finish", {2: 0}, semaphore)
-    return pack, merge, split, finish
+ROW = (SLOTS, BLOCKS, HALVES, 128)
+ROW_SHAPE = jax.ShapeDtypeStruct(ROW, F32)
+STATE_SHAPE = jax.ShapeDtypeStruct((2, *ROW), F32)
+SLOTS_SHAPE = jax.ShapeDtypeStruct((BLOCKS, MODES, HALVES, 128), F32)
+
+
+def moved(kernel, places, shape, name, aliases={}, scratch=()):
+    spec = {"s": pl.BlockSpec(memory_space=pltpu.SMEM), "v": pl.BlockSpec(memory_space=pltpu.VMEM), "a": pl.BlockSpec(memory_space=pl.ANY)}
+    return pl.pallas_call(
+        kernel,
+        in_specs=[spec[p] for p in places[:-1]],
+        out_specs=spec[places[-1]],
+        out_shape=shape,
+        input_output_aliases=aliases,
+        scratch_shapes=list(scratch),
+        cost_estimate=pl.CostEstimate(flops=int(2e9), bytes_accessed=0, transcendentals=0),
+        compiler_params=pltpu.CompilerParams(vmem_limit_bytes=LIMIT),
+        name=name,
+    )
+
+
+def to_pieces(core, big, state):
+    state = state.reshape(2, SLOTS, FIELDS, 2 * BLOCKS, 128).transpose(0, 1, 3, 2, 4).reshape(2, *ROW)
+    got = lax.ppermute(moved(pack_kernel, "svv", ROW_SHAPE, "pack")(core, state), "mode", [(0, 1), (1, 0)])
+    return moved(merge_kernel, "ssvvv", SLOTS_SHAPE, "merge")(core, big, state, got)
+
+
+def from_pieces(core, big, pieces):
+    got = lax.ppermute(moved(lambda *refs: split_kernel(False, *refs), "ssvv", ROW_SHAPE, "split_send")(core, big, pieces), "mode", [(0, 1), (1, 0)])
+    semaphore = pltpu.SemaphoreType.DMA
+    state = moved(split_own_kernel, "ssva", STATE_SHAPE, "split_own", scratch=[pltpu.VMEM(ROW, F32), semaphore])(core, big, pieces)
+    state = moved(finish_kernel, "svaa", STATE_SHAPE, "finish", {2: 0}, [semaphore])(core, got, state)
+    return state.reshape(2, SLOTS, 2 * BLOCKS, FIELDS, 128).transpose(0, 1, 3, 2, 4).reshape(2, SLOTS, FIELDS, BLOCKS * LANES)
 
 
 def ring(size, step):
@@ -512,19 +512,15 @@
 
 def shards(chaos_state, mode_group, mode_degrees):
     core = lax.axis_index("mode").astype(jnp.int32).reshape(1)
-    pack, merge, split, finish = movers()
-    swap = [(0, 1), (1, 0)]
-    got = lax.ppermute(pack(core, chaos_state), "mode", swap)
     evaluate, proj, scale, big = make_tables(mode_group, mode_degrees)
     tables = (evaluate, proj, lane_operators(), scale)
-    pieces = merge(core, big, chaos_state, got)
-    tile = lax.all_to_all(pieces, ("gx_lo", "mode"), 0, 0, tiled=True)
+    pieces = to_pieces(core, big, chaos_state)
+    tile = lax.all_to_all(pieces.reshape(XROWS, PIECE, 128), ("gx_lo", "mode"), 0, 0, tiled=True)
     (coef, east, following), outer, inner = first_section(core, tile, tables)
-    (east, following), outer, inner = second_section(core, coef, following, east, outer, inner, tables)
-    tile = advanced(core, following, east, outer, inner, scale)
-    pieces = lax.all_to_all(tile, ("gx_lo", "mode"), 0, 0, tiled=True)
-    state, send = split(core, big, pieces)
-    return finish(core, lax.ppermute(send, "mode", swap), state)
+    (east, following), edges, strips = second_section(core, coef, following, east, outer, inner, tables)
+    tile = advanced(core, following, east, edges, strips, scale)
+    pieces = lax.all_to_all(tile, ("gx_lo", "mode"), 0, 0, tiled=True).reshape(SLOTS_SHAPE.shape)
+    return from_pieces(core, big, pieces)
 
 
 def solution(mesh):

time: 134 us -> 129 us (0.963)
  Pallas kernels: 36.1 us -> 32.9 us
  starting transfers between devices: 17.7 us -> 14.7 us
    pallas_call x6 -> x5, Pallas kernels: 26.1 us -> 23.1 us  [in_vmem(): pl.pallas_call(kernel, in_specs=[pl.BlockSpec(memory_space=pltpu.SMEM)] +...]
    ppermute x4 -> x3, starting transfers between devices: 9.99 us -> 6.98 us  [exchange_y(): lax.ppermute(inside, 'mode', [(0, 1), (1, 0)])]
    ppermute x2, waiting for transfers between devices: 3.47 us -> 1.5 us  [the longest x1 1.06 us: from_pieces(): lax.ppermute(moved(lambda *refs: split_kernel(False, *refs), 'ssvv', ROW_...]
    ppermute x4 -> x3, waiting for transfers between devices: 2.82 us -> 4.12 us  [exchange_y(): lax.ppermute(outside, ('gx_lo', 'gy', 'mode'), swap)]
    pallas_call x4 -> x5, Pallas kernels: 7.74 us -> 7.58 us  [the longest x1 2.35 us: to_pieces(): moved(merge_kernel, 'ssvvv', SLOTS_SHAPE, 'merge')(core, big, state, got)]
  transfers between devices with their start and end apart: 14 -> 12, of which waited for: 3 -> 4; matrix products, arithmetic and copies ran while one was open for 1% -> 1% of each run, Pallas kernels for 16% -> 11%
where the time goes in v4:
time: 129 us; the launch traced here: 128 us
  blocking collectives  71.2 us (55%)
  Pallas kernels  32.9 us (26%)
  starting transfers between devices  14.7 us (11%)
  waiting for transfers between devices  6.88 us (5%)
  local copies, waits for them, and re-layouts  2.61 us (2%)
    all_to_all x1, blocking collectives, shards(): lax.all_to_all(pieces.reshape(XROWS, PIECE, 128), ('gx_lo', 'mode'), 0, 0...  35.9 us
    all_to_all x1, blocking collectives, shards(): lax.all_to_all(tile, ('gx_lo', 'mode'), 0, 0, tiled=True)  35.3 us
    pallas_call x5, Pallas kernels, in_vmem(): pl.pallas_call(kernel, in_specs=[pl.BlockSpec(memory_space=pltpu.SMEM)] +...  23.1 us
    ppermute x3, starting transfers between devices, exchange_y(): lax.ppermute(inside, 'mode', [(0, 1), (1, 0)])  6.98 us
    ppermute x2, starting transfers between devices, exchange_x(): lax.ppermute(start, 'gx_hi', ring(size, -1))  4.14 us
    ppermute x3, waiting for transfers between devices, exchange_y(): lax.ppermute(outside, ('gx_lo', 'gy', 'mode'), swap)  4.12 us
    unnamed x15, local copies, waits for them, and re-layouts  2.61 us
  transfers between devices with their start and end apart: 12, of which 4 were waited for; matrix products, arithmetic and copies ran while one was open for 1% of the time, Pallas kernels for 11%

profile of v4, /device:TPU:1, one launch (start us, length us, event | category | flops | bytes accessed | tf_op | source)
XLA Modules:
  0.0 128.4 jit_solution(9625257006215164440)
XLA Ops:
  0.0 1.9 %copy-done = f32[2,24,4,4096]{3,2,1,0:T(4,128)S(1)} copy-done((f32[2,24,4,4096]{3,2,1,0:T(4,128)S(1)}, f32[2,24,4,4096]{3,2,1,0:T(4,128)}, u32[]{:S(2)}) %copy-start) | copy-done | bytes 3145752
  1.9 1.3 %pack.1 = f32[24,16,8,128]{3,2,1,0:T(8,128)} custom-call(s32[1]{0:T(128)} %bitcast.core_ref.refs_0_, f32[2,24,16,8,128]{4,3,2,1,0:T(8,128)S(1)} %bitcast.17), custom_call_target="tpu_custom_call" | custom-call | flops 2000000000 | tf_op jit(solution)/shard_map/pack/pallas_call | solution.py:485
  3.2 1.4 %collective-permute-start = (f32[24,16,8,128]{3,2,1,0:T(8,128)}, f32[24,16,8,128]{3,2,1,0:T(8,128)}, u32[]{:S(2)}, u32[]{:S(2)}) collective-permute-start(f32[24,16,8,128]{3,2,1,0:T(8,128)} %pack.1), channel_id=1, source_target_pairs={{0,1},{1,0},{2,3},{3,2},{4,5},{5,4},{6,7},{7,6},{8,9},{9,8},{10,11... | collective-permute-start | bytes 4718600 | tf_op jit(solution)/shard_map/ppermute | solution.py:485
  4.6 0.0 copy-done.6
  4.6 0.7 copy.13.degrees_ref
  5.3 2.2 %tables.1 = (bf16[224,128]{1,0:T(8,128)(2,1)}, bf16[80,192]{1,0:T(8,128)(2,1)}, f32[3,40,256]{2,1,0:T(8,128)}, s32[1]{0:T(128)}) custom-call(s32[1,35]{1,0:T(1,128)} %bitcast.19, s32[35,4]{1,0:T(8,128)} %copy.13.degrees_ref, f32[8,192]{1,0:T(8,128)} %constant.10.clone.prow_ref, f32[96,8]{1,0:T(8,128)} %constant.11.clone.pcol_ref), custom_call_target="tpu_custom_call" | custom-call | tf_op jit(solution)/shard_map/tables/pallas_call | solution.py:113
  7.6 0.4 collective-permute-done.got_ref
  8.0 0.0 copy-done.1
  8.0 2.3 %merge.1 = f32[16,35,8,128]{3,2,1,0:T(8,128)S(1)} custom-call(s32[1]{0:T(128)} %bitcast.core_ref.refs_0_, s32[1]{0:T(128)} %get-tuple-element.31.big_ref.refs_1_, f32[2,24,16,8,128]{4,3,2,1,0:T(8,128)S(1)} %bitcast.18, f32[24,16,8,128]{3,2,1,0:T(8,128)} %collective-permute-done.got_ref), custom_call_target="tpu_custom_call" | custom-call | flops 2000000000 | tf_op jit(solution)/shard_map/merge/pallas_call | solution.py:486
  10.4 0.0 copy-start.2
  10.4 0.0 copy-start.3
  10.4 0.0 copy-start.4
  10.4 0.0 copy-start.5
  10.4 35.9 %all_to_all.10.refs_1_ = f32[16,280,128]{2,1,0:T(8,128)S(1)} all-to-all(f32[16,280,128]{2,1,0:T(8,128)S(1)} %bitcast.16), channel_id=1, replica_groups=mesh['gx_hi'=4,'gx_lo'=8,'gy'=2,'mode'=2] {'gx_lo','mode'}, dimensions={0} | all-to-all | bytes 4587520 | tf_op jit(solution)/shard_map/all_to_all | solution.py:518
  46.3 0.0 copy-done.2
  46.3 0.0 copy-done.3
  46.3 0.0 copy-done.4
  46.3 4.5 %first_outer.1 = (f32[16,160,256]{2,1,0:T(8,128)S(1)}, f32[16,160,256]{2,1,0:T(8,128)S(1)}, f32[16,160,256]{2,1,0:T(8,128)S(1)}, f32[2,160,128]{2,1,0:T(8,128)S(...) custom-call(s32[1]{0:T(128)} %bitcast.core_ref.refs_0_, ...), custom_call_target="tpu_custom_call" | custom-call | flops 5000000000 | bytes 15000000 | tf_op jit(solution)/shard_map/first_outer/pallas_call | solution.py:360
  50.8 0.9 collective-permute-start.3
  51.7 0.0 collective-permute-start.4
  51.7 1.2 collective-permute-start.5
  52.9 1.5 %collective-permute-start.6 = (f32[2,160,256]{2,1,0:T(8,128)S(1)}, f32[2,160,256]{2,1,0:T(8,128)S(1)}, u32[]{:S(2)}, u32[]{:S(2)}) collective-permute-start(f32[2,160,256]{2,1,0:T(8,128)S(1)} %get-tuple-element.46), channel_id=1, source_target_pairs={{0,96},{32,0},{64,32},{96,64},{1,97},{33,1},{65,33},{97,65},{2,98}... | collective-permute-start | bytes 983048 | tf_op jit(solution)/shard_map/ppermute | solution.py:503
  54.4 4.5 %first_inner.1 = (f32[16,160,256]{2,1,0:T(8,128)S(1)}, f32[16,160,256]{2,1,0:T(8,128)S(1)}, f32[16,160,256]{2,1,0:T(8,128)S(1)}, f32[2,160,128]{2,1,0:T(8,128)S(1)}, f32[2,160,128]{2,1,0:T(8,128)S(1)}) custom-call(s32[1]{0:T(128)} %bitcast.core_ref.refs_0_, ...), custom_call_target="tpu_custom_call", output_to_operand_aliasing={{0}: (6, {}), {1}: (7, {}), {2}: (8, {})} | custom-call | flops 20000000000 | bytes 60000000 | tf_op jit(solution)/shard_map/first_inner/pallas_call | solution.py:360
  58.9 3.2 %collective-permute-start.1 = (f32[2,160,128]{2,1,0:T(8,128)S(1)}, f32[2,160,128]{2,1,0:T(8,128)S(1)}, u32[]{:S(2)}, u32[]{:S(2)}) collective-permute-start(f32[2,160,128]{2,1,0:T(8,128)S(1)} %get-tuple-element.41), channel_id=1, source_target_pairs={{0,1},{1,0},{2,3},{3,2},{4,5},{5,4},{6,7},{7,6},{8,9},{9,8},{10,11... | collective-permute-start | bytes 491528 | tf_op jit(solution)/shard_map/ppermute | solution.py:510
  62.0 0.0 collective-permute-done.3.refs_4_
  62.0 0.0 collective-permute-start.2
  62.0 0.0 collective-permute-done.4.refs_5_
  62.1 0.0 collective-permute-done.5.refs_10_
  62.1 0.0 collective-permute-done.6.refs_11_
  62.1 5.2 %second_outer.1 = (f32[16,160,256]{2,1,0:T(8,128)S(1)}, f32[16,160,256]{2,1,0:T(8,128)S(1)}, f32[2,160,128]{2,1,0:T(8,128)S(1)}, f32[2,160,128]{2,1,0:T(8,128)S(...) custom-call(s32[1]{0:T(128)} %bitcast.core_ref.refs_0_, f32[16,160,256]{2,1,0:T(8,128)S(1)} %get-tuple-element.38.refs_1_, ...), custom_call_target="tpu_custom_call" | custom-call | flops 8000000000 | bytes 24000000 | tf_op jit(solution)/shard_map/second_outer/pallas_call | solution.py:360
  67.3 0.0 collective-permute-done.1.refs_4_
  67.3 0.0 collective-permute-done.2.refs_5_
  67.3 5.1 %second_inner.1 = (f32[16,160,256]{2,1,0:T(8,128)S(1)}, f32[16,160,256]{2,1,0:T(8,128)S(1)}, f32[4,160,128]{2,1,0:T(8,128)S(1)}, f32[4,160,128]{2,1,0:T(8,128)S(1)}) custom-call(s32[1]{0:T(128)} %bitcast.core_ref.refs_0_, f32[16,160,256]{2,1,0:T(8,128)S(1)} %get-tuple-element.38.refs_1_, ...), custom_call_target="tpu_custom_call", output_to_operand_aliasing={{0}: (10, {}), {1}: (11, {})} | custom-call | flops 20000000000 | bytes 60000000 | tf_op jit(solution)/shard_map/second_inner/pallas_call | solution.py:360
  72.5 2.9 %collective-permute-start.7 = (f32[4,160,128]{2,1,0:T(8,128)S(1)}, f32[4,160,128]{2,1,0:T(8,128)S(1)}, u32[]{:S(2)}, u32[]{:S(2)}) collective-permute-start(f32[4,160,128]{2,1,0:T(8,128)S(1)} %get-tuple-element.53), channel_id=1, source_target_pairs={{0,1},{1,0},{2,3},{3,2},{4,5},{5,4},{6,7},{7,6},{8,9},{9,8},{10,11... | collective-permute-start | bytes 983048 | tf_op jit(solution)/shard_map/ppermute | solution.py:510
  75.4 0.0 collective-permute-start.8
  75.4 0.0 collective-permute-start.9
  75.4 2.7 %collective-permute-start.10 = (f32[2,160,256]{2,1,0:T(8,128)S(1)}, f32[2,160,256]{2,1,0:T(8,128)S(1)}, u32[]{:S(2)}, u32[]{:S(2)}) collective-permute-start(f32[2,160,256]{2,1,0:T(8,128)S(1)} %get-tuple-element.56), channel_id=1, source_target_pairs={{0,96},{32,0},{64,32},{96,64},{1,97},{33,1},{65,33},{97,65},{2,98}... | collective-permute-start | bytes 983048 | tf_op jit(solution)/shard_map/ppermute | solution.py:503
  78.1 0.0 collective-permute-done.7.inside_from
  78.1 4.1 %collective-permute-done.8.outside_from = f32[4,160,128]{2,1,0:T(8,128)S(1)} collective-permute-done((f32[4,160,128]{2,1,0:T(8,128)S(1)}, f32[4,160,128]{2,1,0:T(8,128)S(1)}, u32[]{:S(2)}, u32[]{:S(2)}) %collective-permute-start.8) | collective-permute-done | bytes 327712 | tf_op jit(solution)/shard_map/ppermute | solution.py:510
  82.2 1.2 collective-permute-done.9.edge_before
  83.5 0.0 collective-permute-done.10.edge_after
  83.5 3.7 %advanced.1 = f32[16,280,128]{2,1,0:T(8,128)S(1)} custom-call(s32[1]{0:T(128)} %bitcast.core_ref.refs_0_, f32[16,160,256]{2,1,0:T(8,128)S(1)} %get-tuple-element.51.following_ref, f32[16,160,256]{2,1,0:T(8,128)S(1)} %get-tuple-element.52.from_ref, f32[4,160,128]{2,1,0:T(8,128)S(1)} %collective-permute-done.7.inside_from, ...), custom_call_target="tpu_custom_call" | custom-call | flops 8000000000 | bytes 24000000 | tf_op jit(solution)/shard_map/advanced/pallas_call | solution.py:360
  87.2 35.3 %all_to_all.11 = f32[16,280,128]{2,1,0:T(8,128)S(1)} all-to-all(f32[16,280,128]{2,1,0:T(8,128)S(1)} %advanced.1), channel_id=1, replica_groups=mesh['gx_hi'=4,'gx_lo'=8,'gy'=2,'mode'=2] {'gx_lo','mode'}, dimensions={0} | all-to-all | bytes 4587520 | tf_op jit(solution)/shard_map/all_to_all | solution.py:522
  122.5 0.8 split_send.1
  123.3 0.9 collective-permute-start.11
  124.2 2.0 %split_own.1._ = f32[2,24,16,8,128]{4,3,2,1,0:T(8,128)} custom-call(s32[1]{0:T(128)} %bitcast.core_ref.refs_0_, s32[1]{0:T(128)} %get-tuple-element.31.big_ref.refs_1_, f32[16,35,8,128]{3,2,1,0:T(8,128)S(1)} %bitcast.15), custom_call_target="tpu_custom_call" | custom-call | flops 2000000000 | tf_op jit(solution)/shard_map/split_own/pallas_call | solution.py:492
  126.2 1.1 collective-permute-done.11.got_ref
  127.2 1.1 finish.1
  (4 shorter events, 0.0 us)
Async XLA Ops:
  0.0 1.9 %copy-start = (f32[2,24,4,4096]{3,2,1,0:T(4,128)S(1)}, f32[2,24,4,4096]{3,2,1,0:T(4,128)}, u32[]{:S(2)}) copy-start(f32[2,24,4,4096]{3,2,1,0:T(4,128)} %param.6) | copy-start | bytes 9437188
  1.9 2.7 %copy-start.6 = (s32[35,4]{0,1:T(4,128)S(1)}, s32[35,4]{0,1:T(4,128)}, u32[]{:S(2)}) copy-start(s32[35,4]{0,1:T(4,128)} %param.8) | copy-start | bytes 1684
  1.9 6.1 %copy-start.1 = (f32[2,24,4,4096]{3,2,1,0:T(4,128)S(1)}, f32[2,24,4,4096]{3,2,1,0:T(4,128)}, u32[]{:S(2)}) copy-start(f32[2,24,4,4096]{3,2,1,0:T(4,128)} %param.6) | copy-start | bytes 9437188
  3.2 4.8 %collective-permute-start = (f32[24,16,8,128]{3,2,1,0:T(8,128)}, f32[24,16,8,128]{3,2,1,0:T(8,128)}, u32[]{:S(2)}, u32[]{:S(2)}) collective-permute-start(f32[24,16,8,128]{3,2,1,0:T(8,128)} %pack.1), channel_id=1, source_target_pairs={{0,1},{1,0},{2,3},{3,2},{4,5},{5,4},{6,7},{7,6},{8,9},{9,8},{10,11... | collective-permute-start | bytes 4718600 | tf_op jit(solution)/shard_map/ppermute | solution.py:485
  10.4 35.9 %copy-start.2 = (f32[3,40,256]{2,1,0:T(8,128)S(1)}, f32[3,40,256]{2,1,0:T(8,128)}, u32[]{:S(2)}) copy-start(f32[3,40,256]{2,1,0:T(8,128)} %get-tuple-element.34.refs_5_.refs_9_.scale_ref) | copy-start | bytes 368644
  10.4 35.9 %copy-start.3 = (bf16[224,128]{1,0:T(8,128)(2,1)S(1)}, bf16[224,128]{1,0:T(8,128)(2,1)}, u32[]{:S(2)}) copy-start(bf16[224,128]{1,0:T(8,128)(2,1)} %get-tuple-element.32.refs_2_.refs_6_) | copy-start | bytes 172036
  10.4 35.9 %copy-start.4 = (bf16[80,192]{1,0:T(8,128)(2,1)S(1)}, bf16[80,192]{1,0:T(8,128)(2,1)}, u32[]{:S(2)}) copy-start(bf16[80,192]{1,0:T(8,128)(2,1)} %get-tuple-element.33.refs_3_.refs_7_) | copy-start | bytes 92164
  10.4 35.9 %copy-start.5 = (bf16[2,512,256]{2,1,0:T(8,128)(2,1)S(1)}, bf16[2,512,256]{2,1,0:T(8,128)(2,1)}, u32[]{:S(2)}) copy-start(bf16[2,512,256]{2,1,0:T(8,128)(2,1)} %constant.12.clone.refs_4_.refs_8_) | copy-start | bytes 1572868
  50.8 11.2 %collective-permute-start.3 = (f32[2,160,128]{2,1,0:T(8,128)S(1)}, f32[2,160,128]{2,1,0:T(8,128)S(1)}, u32[]{:S(2)}, u32[]{:S(2)}) collective-permute-start(f32[2,160,128]{2,1,0:T(8,128)S(1)} %get-tuple-element.43), channel_id=1, source_target_pairs={{0,1},{1,0},{2,3},{3,2},{4,5},{5,4},{6,7},{7,6},{8,9},{9,8},{10,11... | collective-permute-start | bytes 491528 | tf_op jit(solution)/shard_map/ppermute | solution.py:510
  51.7 10.3 %collective-permute-start.4 = (f32[2,160,128]{2,1,0:T(8,128)S(1)}, f32[2,160,128]{2,1,0:T(8,128)S(1)}, u32[]{:S(2)}, u32[]{:S(2)}) collective-permute-start(f32[2,160,128]{2,1,0:T(8,128)S(1)} %get-tuple-element.44), channel_id=1, source_target_pairs={{1,4},{5,8},{9,12},{13,16},{17,20},{21,24},{25,28},{29,2},{3,6},{7... | collective-permute-start | bytes 491528 | tf_op jit(solution)/shard_map/ppermute | solution.py:510
  51.7 10.3 %collective-permute-start.5 = (f32[2,160,256]{2,1,0:T(8,128)S(1)}, f32[2,160,256]{2,1,0:T(8,128)S(1)}, u32[]{:S(2)}, u32[]{:S(2)}) collective-permute-start(f32[2,160,256]{2,1,0:T(8,128)S(1)} %get-tuple-element.45), channel_id=1, source_target_pairs={{0,32},{32,64},{64,96},{96,0},{1,33},{33,65},{65,97},{97,1},{2,34}... | collective-permute-start | bytes 983048 | tf_op jit(solution)/shard_map/ppermute | solution.py:503
  52.9 9.1 %collective-permute-start.6 = (f32[2,160,256]{2,1,0:T(8,128)S(1)}, f32[2,160,256]{2,1,0:T(8,128)S(1)}, u32[]{:S(2)}, u32[]{:S(2)}) collective-permute-start(f32[2,160,256]{2,1,0:T(8,128)S(1)} %get-tuple-element.46), channel_id=1, source_target_pairs={{0,96},{32,0},{64,32},{96,64},{1,97},{33,1},{65,33},{97,65},{2,98}... | collective-permute-start | bytes 983048 | tf_op jit(solution)/shard_map/ppermute | solution.py:503
  58.9 8.4 %collective-permute-start.1 = (f32[2,160,128]{2,1,0:T(8,128)S(1)}, f32[2,160,128]{2,1,0:T(8,128)S(1)}, u32[]{:S(2)}, u32[]{:S(2)}) collective-permute-start(f32[2,160,128]{2,1,0:T(8,128)S(1)} %get-tuple-element.41), channel_id=1, source_target_pairs={{0,1},{1,0},{2,3},{3,2},{4,5},{5,4},{6,7},{7,6},{8,9},{9,8},{10,11... | collective-permute-start | bytes 491528 | tf_op jit(solution)/shard_map/ppermute | solution.py:510
  62.0 5.3 %collective-permute-start.2 = (f32[2,160,128]{2,1,0:T(8,128)S(1)}, f32[2,160,128]{2,1,0:T(8,128)S(1)}, u32[]{:S(2)}, u32[]{:S(2)}) collective-permute-start(f32[2,160,128]{2,1,0:T(8,128)S(1)} %get-tuple-element.42), channel_id=1, source_target_pairs={{1,4},{5,8},{9,12},{13,16},{17,20},{21,24},{25,28},{29,2},{3,6},{7... | collective-permute-start | bytes 491528 | tf_op jit(solution)/shard_map/ppermute | solution.py:510
  72.5 5.6 %collective-permute-start.7 = (f32[4,160,128]{2,1,0:T(8,128)S(1)}, f32[4,160,128]{2,1,0:T(8,128)S(1)}, u32[]{:S(2)}, u32[]{:S(2)}) collective-permute-start(f32[4,160,128]{2,1,0:T(8,128)S(1)} %get-tuple-element.53), channel_id=1, source_target_pairs={{0,1},{1,0},{2,3},{3,2},{4,5},{5,4},{6,7},{7,6},{8,9},{9,8},{10,11... | collective-permute-start | bytes 983048 | tf_op jit(solution)/shard_map/ppermute | solution.py:510
  75.4 6.8 %collective-permute-start.8 = (f32[4,160,128]{2,1,0:T(8,128)S(1)}, f32[4,160,128]{2,1,0:T(8,128)S(1)}, u32[]{:S(2)}, u32[]{:S(2)}) collective-permute-start(f32[4,160,128]{2,1,0:T(8,128)S(1)} %get-tuple-element.54), channel_id=1, source_target_pairs={{1,4},{5,8},{9,12},{13,16},{17,20},{21,24},{25,28},{29,2},{3,6},{7... | collective-permute-start | bytes 983048 | tf_op jit(solution)/shard_map/ppermute | solution.py:510
  75.4 8.0 %collective-permute-start.9 = (f32[2,160,256]{2,1,0:T(8,128)S(1)}, f32[2,160,256]{2,1,0:T(8,128)S(1)}, u32[]{:S(2)}, u32[]{:S(2)}) collective-permute-start(f32[2,160,256]{2,1,0:T(8,128)S(1)} %get-tuple-element.55), channel_id=1, source_target_pairs={{0,32},{32,64},{64,96},{96,0},{1,33},{33,65},{65,97},{97,1},{2,34}... | collective-permute-start | bytes 983048 | tf_op jit(solution)/shard_map/ppermute | solution.py:503
  75.4 8.0 %collective-permute-start.10 = (f32[2,160,256]{2,1,0:T(8,128)S(1)}, f32[2,160,256]{2,1,0:T(8,128)S(1)}, u32[]{:S(2)}, u32[]{:S(2)}) collective-permute-start(f32[2,160,256]{2,1,0:T(8,128)S(1)} %get-tuple-element.56), channel_id=1, source_target_pairs={{0,96},{32,0},{64,32},{96,64},{1,97},{33,1},{65,33},{97,65},{2,98}... | collective-permute-start | bytes 983048 | tf_op jit(solution)/shard_map/ppermute | solution.py:503
  123.3 3.9 %collective-permute-start.11 = (f32[24,16,8,128]{3,2,1,0:T(8,128)S(1)}, f32[24,16,8,128]{3,2,1,0:T(8,128)S(1)}, u32[]{:S(2)}, u32[]{:S(2)}) collective-permute-start(f32[24,16,8,128]{3,2,1,0:T(8,128)S(1)} %split_send.1), channel_id=1, source_target_pairs={{0,1},{1,0},{2,3},{3,2},{4,5},{5,4},{6,7},{7,6},{8,9},{9,8},{10,11... | collective-permute-start | bytes 4718600 | tf_op jit(solution)/shard_map/ppermute | solution.py:490

commit v5 on v4

--- a/solution.py
+++ b/solution.py
@@ -144,9 +144,18 @@
     return first, second, jnp.dot(jnp.concatenate([first, second.astype(BF16)], axis=1), operator, preferred_element_type=F32)
 
 
+def plane_laplace(value):
+    plane = lax.broadcasted_iota(jnp.int32, (1, 128), 1) % NZ
+    above = jnp.where(plane == NZ - 1, pltpu.roll(value, NZ - 1, 1), pltpu.roll(value, 127, 1))
+    below = jnp.where(plane == 0, pltpu.roll(value, 129 - NZ, 1), pltpu.roll(value, 1, 1))
+    return above - 2.0 * value + below
+
+
 def row_fluxes(fields, eval_ref, proj_ref, lanes_ref):
     points, east, north, source = [], [], [], []
-    first, second, laplace = by_lanes(jnp.concatenate(fields, axis=0), lanes_ref[1])
+    row = jnp.concatenate(fields, axis=0)
+    laplace = jnp.concatenate([plane_laplace(row[:, :128]), plane_laplace(row[:, 128:])], axis=1)
+    first, second = pieces_of(row)
     first = first.astype(F32)
     for f in range(FIELDS):
         rows = slice(f * ROWS, (f + 1) * ROWS)
@@ -185,21 +194,31 @@
     return east, north, source, laplace
 
 
-def emit_rows(core_ref, g, at, rows_of, tables, east_ref, next_ref, inside_ref, outside_ref):
+def emit_rows(core_ref, g, at, rows_of, tables, east_ref, next_ref, inside_ref, outside_ref, coef_ref=None):
     eval_ref, proj_ref, lanes_ref, scale_ref = tables
     lane = lax.broadcasted_iota(jnp.int32, (1, 128), 1)
     gain = scale_ref[1]
     low, high = [None] * FIELDS, [None] * FIELDS
-    for r in range(STEP):
-        fields, base, weight = rows_of(r)
+    given = [rows_of(r) for r in range(STEP)]
+    found = []
+    for fields, base, weight in given:
         east, north, source, laplace = row_fluxes(fields, eval_ref, proj_ref, lanes_ref)
-        here = (lane >= r * STRIP) & (lane < (r + 1) * STRIP)
         slope = by_lanes(jnp.concatenate(north, axis=0), lanes_ref[0])[2]
+        following = []
         for f in range(FIELDS):
             rows = slice(f * ROWS, (f + 1) * ROWS)
+            known = gain * (source[f] - slope[rows]) + time_step * laplace[rows]
+            following.append(base[f] + weight * known)
+        found.append((east, north, following))
+    for r in range(STEP):
+        east, north, following = found[r]
+        here = (lane >= r * STRIP) & (lane < (r + 1) * STRIP)
+        for f in range(FIELDS):
+            rows = slice(f * ROWS, (f + 1) * ROWS)
+            if coef_ref is not None:
+                coef_ref[STEP * g + r, rows, :] = given[r][0][f]
             east_ref[STEP * g + r, rows, :] = east[f]
-            known = gain * (source[f] - slope[rows]) + time_step * laplace[rows]
-            next_ref[STEP * g + r, rows, :] = base[f] + weight * known
+            next_ref[STEP * g + r, rows, :] = following[f]
             start = pltpu.roll(north[f][:, :128], r * STRIP, 1) if r else north[f][:, :128]
             end = north[f][:, 128:] if r == STEP - 1 else pltpu.roll(north[f][:, 128:], (r + 1) * STRIP, 1)
             low[f] = jnp.where(here, start, low[f]) if r else start
@@ -255,11 +274,10 @@
                     rest = state_ref[STEP * g + r, pl.ds(half * FIELDS + f, SMALL, stride=HALVES), :]
                     halves.append(jnp.concatenate([full, rest], axis=0))
                 value = tables[3][0] * jnp.concatenate(halves, axis=1)
-                coef_ref[STEP * g + r, f * ROWS : (f + 1) * ROWS, :] = value
                 fields.append(value)
             return fields, fields, 1.0
 
-        emit_rows(core_ref, g, i, rows_of, tables, east_ref, next_ref, inside_ref, outside_ref)
+        emit_rows(core_ref, g, i, rows_of, tables, east_ref, next_ref, inside_ref, outside_ref, coef_ref)
 
     over_groups(outer, body)
     if outer:

time: 129 us -> 129 us (level)
  no operation moved by 1% of the time
where the time goes in v5:
time: 129 us; the launch traced here: 128 us
  blocking collectives  71.7 us (56%)
  Pallas kernels  32.1 us (25%)
  starting transfers between devices  14.8 us (11%)
  waiting for transfers between devices  6.78 us (5%)
  local copies, waits for them, and re-layouts  2.61 us (2%)
    all_to_all x1, blocking collectives, shards(): lax.all_to_all(pieces.reshape(XROWS, PIECE, 128), ('gx_lo', 'mode'), 0, 0...  35.9 us
    all_to_all x1, blocking collectives, shards(): lax.all_to_all(tile, ('gx_lo', 'mode'), 0, 0, tiled=True)  35.8 us
    pallas_call x5, Pallas kernels, in_vmem(): pl.pallas_call(kernel, in_specs=[pl.BlockSpec(memory_space=pltpu.SMEM)] +...  22.3 us
    ppermute x3, starting transfers between devices, exchange_y(): lax.ppermute(inside, 'mode', [(0, 1), (1, 0)])  7.11 us
    ppermute x2, starting transfers between devices, exchange_x(): lax.ppermute(start, 'gx_hi', ring(size, -1))  4.13 us
    ppermute x3, waiting for transfers between devices, exchange_y(): lax.ppermute(outside, ('gx_lo', 'gy', 'mode'), swap)  4.12 us
    unnamed x15, local copies, waits for them, and re-layouts  2.61 us
  transfers between devices with their start and end apart: 12, of which 4 were waited for; matrix products, arithmetic and copies ran while one was open for 1% of the time, Pallas kernels for 11%

profile of v5, /device:TPU:1, one launch (start us, length us, event | category | flops | bytes accessed | tf_op | source)
XLA Modules:
  0.0 128.3 jit_solution(8961696535380827771)
XLA Ops:
  0.0 1.9 %copy-done = f32[2,24,4,4096]{3,2,1,0:T(4,128)S(1)} copy-done((f32[2,24,4,4096]{3,2,1,0:T(4,128)S(1)}, f32[2,24,4,4096]{3,2,1,0:T(4,128)}, u32[]{:S(2)}) %copy-start) | copy-done | bytes 3145752
  1.9 1.3 %pack.1 = f32[24,16,8,128]{3,2,1,0:T(8,128)} custom-call(s32[1]{0:T(128)} %bitcast.core_ref.refs_0_, f32[2,24,16,8,128]{4,3,2,1,0:T(8,128)S(1)} %bitcast.17), custom_call_target="tpu_custom_call" | custom-call | flops 2000000000 | tf_op jit(solution)/shard_map/pack/pallas_call | solution.py:503
  3.2 1.4 %collective-permute-start = (f32[24,16,8,128]{3,2,1,0:T(8,128)}, f32[24,16,8,128]{3,2,1,0:T(8,128)}, u32[]{:S(2)}, u32[]{:S(2)}) collective-permute-start(f32[24,16,8,128]{3,2,1,0:T(8,128)} %pack.1), channel_id=1, source_target_pairs={{0,1},{1,0},{2,3},{3,2},{4,5},{5,4},{6,7},{7,6},{8,9},{9,8},{10,11... | collective-permute-start | bytes 4718600 | tf_op jit(solution)/shard_map/ppermute | solution.py:503
  4.6 0.0 copy-done.6
  4.6 0.7 copy.13.degrees_ref
  5.3 2.2 %tables.1 = (bf16[224,128]{1,0:T(8,128)(2,1)}, bf16[80,192]{1,0:T(8,128)(2,1)}, f32[3,40,256]{2,1,0:T(8,128)}, s32[1]{0:T(128)}) custom-call(s32[1,35]{1,0:T(1,128)} %bitcast.19, s32[35,4]{1,0:T(8,128)} %copy.13.degrees_ref, f32[8,192]{1,0:T(8,128)} %constant.10.clone.prow_ref, f32[96,8]{1,0:T(8,128)} %constant.11.clone.pcol_ref), custom_call_target="tpu_custom_call" | custom-call | tf_op jit(solution)/shard_map/tables/pallas_call | solution.py:113
  7.6 0.4 collective-permute-done.got_ref
  8.0 0.0 copy-done.1
  8.0 2.3 %merge.1 = f32[16,35,8,128]{3,2,1,0:T(8,128)S(1)} custom-call(s32[1]{0:T(128)} %bitcast.core_ref.refs_0_, s32[1]{0:T(128)} %get-tuple-element.31.big_ref.refs_1_, f32[2,24,16,8,128]{4,3,2,1,0:T(8,128)S(1)} %bitcast.18, f32[24,16,8,128]{3,2,1,0:T(8,128)} %collective-permute-done.got_ref), custom_call_target="tpu_custom_call" | custom-call | flops 2000000000 | tf_op jit(solution)/shard_map/merge/pallas_call | solution.py:504
  10.4 0.0 copy-start.2
  10.4 0.0 copy-start.3
  10.4 0.0 copy-start.4
  10.4 0.0 copy-start.5
  10.4 35.9 %all_to_all.10.refs_1_ = f32[16,280,128]{2,1,0:T(8,128)S(1)} all-to-all(f32[16,280,128]{2,1,0:T(8,128)S(1)} %bitcast.16), channel_id=1, replica_groups=mesh['gx_hi'=4,'gx_lo'=8,'gy'=2,'mode'=2] {'gx_lo','mode'}, dimensions={0} | all-to-all | bytes 4587520 | tf_op jit(solution)/shard_map/all_to_all | solution.py:536
  46.3 0.0 copy-done.2
  46.3 0.0 copy-done.3
  46.3 0.0 copy-done.4
  46.3 4.3 %first_outer.1 = (f32[16,160,256]{2,1,0:T(8,128)S(1)}, f32[16,160,256]{2,1,0:T(8,128)S(1)}, f32[16,160,256]{2,1,0:T(8,128)S(1)}, f32[2,160,128]{2,1,0:T(8,128)S(...) custom-call(s32[1]{0:T(128)} %bitcast.core_ref.refs_0_, ...), custom_call_target="tpu_custom_call" | custom-call | flops 5000000000 | bytes 15000000 | tf_op jit(solution)/shard_map/first_outer/pallas_call | solution.py:378
  50.5 0.9 collective-permute-start.3
  51.4 0.0 collective-permute-start.4
  51.4 1.2 collective-permute-start.5
  52.6 1.5 %collective-permute-start.6 = (f32[2,160,256]{2,1,0:T(8,128)S(1)}, f32[2,160,256]{2,1,0:T(8,128)S(1)}, u32[]{:S(2)}, u32[]{:S(2)}) collective-permute-start(f32[2,160,256]{2,1,0:T(8,128)S(1)} %get-tuple-element.46), channel_id=1, source_target_pairs={{0,96},{32,0},{64,32},{96,64},{1,97},{33,1},{65,33},{97,65},{2,98}... | collective-permute-start | bytes 983048 | tf_op jit(solution)/shard_map/ppermute | solution.py:521
  54.1 4.2 %first_inner.1 = (f32[16,160,256]{2,1,0:T(8,128)S(1)}, f32[16,160,256]{2,1,0:T(8,128)S(1)}, f32[16,160,256]{2,1,0:T(8,128)S(1)}, f32[2,160,128]{2,1,0:T(8,128)S(1)}, f32[2,160,128]{2,1,0:T(8,128)S(1)}) custom-call(s32[1]{0:T(128)} %bitcast.core_ref.refs_0_, ...), custom_call_target="tpu_custom_call", output_to_operand_aliasing={{0}: (6, {}), {1}: (7, {}), {2}: (8, {})} | custom-call | flops 20000000000 | bytes 60000000 | tf_op jit(solution)/shard_map/first_inner/pallas_call | solution.py:378
  58.3 3.2 %collective-permute-start.1 = (f32[2,160,128]{2,1,0:T(8,128)S(1)}, f32[2,160,128]{2,1,0:T(8,128)S(1)}, u32[]{:S(2)}, u32[]{:S(2)}) collective-permute-start(f32[2,160,128]{2,1,0:T(8,128)S(1)} %get-tuple-element.41), channel_id=1, source_target_pairs={{0,1},{1,0},{2,3},{3,2},{4,5},{5,4},{6,7},{7,6},{8,9},{9,8},{10,11... | collective-permute-start | bytes 491528 | tf_op jit(solution)/shard_map/ppermute | solution.py:528
  61.5 0.0 collective-permute-done.3.refs_4_
  61.5 0.0 collective-permute-start.2
  61.5 0.0 collective-permute-done.4.refs_5_
  61.5 0.0 collective-permute-done.5.refs_10_
  61.5 0.0 collective-permute-done.6.refs_11_
  61.5 5.1 %second_outer.1 = (f32[16,160,256]{2,1,0:T(8,128)S(1)}, f32[16,160,256]{2,1,0:T(8,128)S(1)}, f32[2,160,128]{2,1,0:T(8,128)S(1)}, f32[2,160,128]{2,1,0:T(8,128)S(...) custom-call(s32[1]{0:T(128)} %bitcast.core_ref.refs_0_, f32[16,160,256]{2,1,0:T(8,128)S(1)} %get-tuple-element.38.refs_1_, ...), custom_call_target="tpu_custom_call" | custom-call | flops 8000000000 | bytes 24000000 | tf_op jit(solution)/shard_map/second_outer/pallas_call | solution.py:378
  66.6 0.0 collective-permute-done.1.refs_4_
  66.6 0.0 collective-permute-done.2.refs_5_
  66.7 5.0 %second_inner.1 = (f32[16,160,256]{2,1,0:T(8,128)S(1)}, f32[16,160,256]{2,1,0:T(8,128)S(1)}, f32[4,160,128]{2,1,0:T(8,128)S(1)}, f32[4,160,128]{2,1,0:T(8,128)S(1)}) custom-call(s32[1]{0:T(128)} %bitcast.core_ref.refs_0_, f32[16,160,256]{2,1,0:T(8,128)S(1)} %get-tuple-element.38.refs_1_, ...), custom_call_target="tpu_custom_call", output_to_operand_aliasing={{0}: (10, {}), {1}: (11, {})} | custom-call | flops 20000000000 | bytes 60000000 | tf_op jit(solution)/shard_map/second_inner/pallas_call | solution.py:378
  71.7 3.1 %collective-permute-start.7 = (f32[4,160,128]{2,1,0:T(8,128)S(1)}, f32[4,160,128]{2,1,0:T(8,128)S(1)}, u32[]{:S(2)}, u32[]{:S(2)}) collective-permute-start(f32[4,160,128]{2,1,0:T(8,128)S(1)} %get-tuple-element.53), channel_id=1, source_target_pairs={{0,1},{1,0},{2,3},{3,2},{4,5},{5,4},{6,7},{7,6},{8,9},{9,8},{10,11... | collective-permute-start | bytes 983048 | tf_op jit(solution)/shard_map/ppermute | solution.py:528
  74.7 0.0 collective-permute-start.8
  74.7 0.0 collective-permute-start.9
  74.7 2.7 %collective-permute-start.10 = (f32[2,160,256]{2,1,0:T(8,128)S(1)}, f32[2,160,256]{2,1,0:T(8,128)S(1)}, u32[]{:S(2)}, u32[]{:S(2)}) collective-permute-start(f32[2,160,256]{2,1,0:T(8,128)S(1)} %get-tuple-element.56), channel_id=1, source_target_pairs={{0,96},{32,0},{64,32},{96,64},{1,97},{33,1},{65,33},{97,65},{2,98}... | collective-permute-start | bytes 983048 | tf_op jit(solution)/shard_map/ppermute | solution.py:521
  77.4 0.0 collective-permute-done.7.inside_from
  77.4 4.1 %collective-permute-done.8.outside_from = f32[4,160,128]{2,1,0:T(8,128)S(1)} collective-permute-done((f32[4,160,128]{2,1,0:T(8,128)S(1)}, f32[4,160,128]{2,1,0:T(8,128)S(1)}, u32[]{:S(2)}, u32[]{:S(2)}) %collective-permute-start.8) | collective-permute-done | bytes 327712 | tf_op jit(solution)/shard_map/ppermute | solution.py:528
  81.5 1.1 collective-permute-done.9.edge_before
  82.7 0.0 collective-permute-done.10.edge_after
  82.7 3.7 %advanced.1 = f32[16,280,128]{2,1,0:T(8,128)S(1)} custom-call(s32[1]{0:T(128)} %bitcast.core_ref.refs_0_, f32[16,160,256]{2,1,0:T(8,128)S(1)} %get-tuple-element.51.following_ref, f32[16,160,256]{2,1,0:T(8,128)S(1)} %get-tuple-element.52.from_ref, f32[4,160,128]{2,1,0:T(8,128)S(1)} %collective-permute-done.7.inside_from, ...), custom_call_target="tpu_custom_call" | custom-call | flops 8000000000 | bytes 24000000 | tf_op jit(solution)/shard_map/advanced/pallas_call | solution.py:378
  86.4 35.8 %all_to_all.11 = f32[16,280,128]{2,1,0:T(8,128)S(1)} all-to-all(f32[16,280,128]{2,1,0:T(8,128)S(1)} %advanced.1), channel_id=1, replica_groups=mesh['gx_hi'=4,'gx_lo'=8,'gy'=2,'mode'=2] {'gx_lo','mode'}, dimensions={0} | all-to-all | bytes 4587520 | tf_op jit(solution)/shard_map/all_to_all | solution.py:540
  122.2 0.8 split_send.1
  123.0 0.9 collective-permute-start.11
  123.9 2.0 %split_own.1._ = f32[2,24,16,8,128]{4,3,2,1,0:T(8,128)} custom-call(s32[1]{0:T(128)} %bitcast.core_ref.refs_0_, s32[1]{0:T(128)} %get-tuple-element.31.big_ref.refs_1_, f32[16,35,8,128]{3,2,1,0:T(8,128)S(1)} %bitcast.15), custom_call_target="tpu_custom_call" | custom-call | flops 2000000000 | tf_op jit(solution)/shard_map/split_own/pallas_call | solution.py:510
  125.9 1.1 collective-permute-done.11.got_ref
  127.0 1.1 finish.1
  (4 shorter events, 0.0 us)
Async XLA Ops:
  0.0 1.9 %copy-start = (f32[2,24,4,4096]{3,2,1,0:T(4,128)S(1)}, f32[2,24,4,4096]{3,2,1,0:T(4,128)}, u32[]{:S(2)}) copy-start(f32[2,24,4,4096]{3,2,1,0:T(4,128)} %param.6) | copy-start | bytes 9437188
  1.9 2.7 %copy-start.6 = (s32[35,4]{0,1:T(4,128)S(1)}, s32[35,4]{0,1:T(4,128)}, u32[]{:S(2)}) copy-start(s32[35,4]{0,1:T(4,128)} %param.8) | copy-start | bytes 1684
  1.9 6.1 %copy-start.1 = (f32[2,24,4,4096]{3,2,1,0:T(4,128)S(1)}, f32[2,24,4,4096]{3,2,1,0:T(4,128)}, u32[]{:S(2)}) copy-start(f32[2,24,4,4096]{3,2,1,0:T(4,128)} %param.6) | copy-start | bytes 9437188
  3.2 4.8 %collective-permute-start = (f32[24,16,8,128]{3,2,1,0:T(8,128)}, f32[24,16,8,128]{3,2,1,0:T(8,128)}, u32[]{:S(2)}, u32[]{:S(2)}) collective-permute-start(f32[24,16,8,128]{3,2,1,0:T(8,128)} %pack.1), channel_id=1, source_target_pairs={{0,1},{1,0},{2,3},{3,2},{4,5},{5,4},{6,7},{7,6},{8,9},{9,8},{10,11... | collective-permute-start | bytes 4718600 | tf_op jit(solution)/shard_map/ppermute | solution.py:503
  10.4 35.9 %copy-start.2 = (f32[3,40,256]{2,1,0:T(8,128)S(1)}, f32[3,40,256]{2,1,0:T(8,128)}, u32[]{:S(2)}) copy-start(f32[3,40,256]{2,1,0:T(8,128)} %get-tuple-element.34.refs_5_.refs_9_.scale_ref) | copy-start | bytes 368644
  10.4 35.9 %copy-start.3 = (bf16[224,128]{1,0:T(8,128)(2,1)S(1)}, bf16[224,128]{1,0:T(8,128)(2,1)}, u32[]{:S(2)}) copy-start(bf16[224,128]{1,0:T(8,128)(2,1)} %get-tuple-element.32.refs_2_.refs_6_) | copy-start | bytes 172036
  10.4 35.9 %copy-start.4 = (bf16[80,192]{1,0:T(8,128)(2,1)S(1)}, bf16[80,192]{1,0:T(8,128)(2,1)}, u32[]{:S(2)}) copy-start(bf16[80,192]{1,0:T(8,128)(2,1)} %get-tuple-element.33.refs_3_.refs_7_) | copy-start | bytes 92164
  10.4 35.9 %copy-start.5 = (bf16[2,512,256]{2,1,0:T(8,128)(2,1)S(1)}, bf16[2,512,256]{2,1,0:T(8,128)(2,1)}, u32[]{:S(2)}) copy-start(bf16[2,512,256]{2,1,0:T(8,128)(2,1)} %constant.12.clone.refs_4_.refs_8_) | copy-start | bytes 1572868
  50.5 10.9 %collective-permute-start.3 = (f32[2,160,128]{2,1,0:T(8,128)S(1)}, f32[2,160,128]{2,1,0:T(8,128)S(1)}, u32[]{:S(2)}, u32[]{:S(2)}) collective-permute-start(f32[2,160,128]{2,1,0:T(8,128)S(1)} %get-tuple-element.43), channel_id=1, source_target_pairs={{0,1},{1,0},{2,3},{3,2},{4,5},{5,4},{6,7},{7,6},{8,9},{9,8},{10,11... | collective-permute-start | bytes 491528 | tf_op jit(solution)/shard_map/ppermute | solution.py:528
  51.4 10.1 %collective-permute-start.4 = (f32[2,160,128]{2,1,0:T(8,128)S(1)}, f32[2,160,128]{2,1,0:T(8,128)S(1)}, u32[]{:S(2)}, u32[]{:S(2)}) collective-permute-start(f32[2,160,128]{2,1,0:T(8,128)S(1)} %get-tuple-element.44), channel_id=1, source_target_pairs={{1,4},{5,8},{9,12},{13,16},{17,20},{21,24},{25,28},{29,2},{3,6},{7... | collective-permute-start | bytes 491528 | tf_op jit(solution)/shard_map/ppermute | solution.py:528
  51.4 10.1 %collective-permute-start.5 = (f32[2,160,256]{2,1,0:T(8,128)S(1)}, f32[2,160,256]{2,1,0:T(8,128)S(1)}, u32[]{:S(2)}, u32[]{:S(2)}) collective-permute-start(f32[2,160,256]{2,1,0:T(8,128)S(1)} %get-tuple-element.45), channel_id=1, source_target_pairs={{0,32},{32,64},{64,96},{96,0},{1,33},{33,65},{65,97},{97,1},{2,34}... | collective-permute-start | bytes 983048 | tf_op jit(solution)/shard_map/ppermute | solution.py:521
  52.6 8.9 %collective-permute-start.6 = (f32[2,160,256]{2,1,0:T(8,128)S(1)}, f32[2,160,256]{2,1,0:T(8,128)S(1)}, u32[]{:S(2)}, u32[]{:S(2)}) collective-permute-start(f32[2,160,256]{2,1,0:T(8,128)S(1)} %get-tuple-element.46), channel_id=1, source_target_pairs={{0,96},{32,0},{64,32},{96,64},{1,97},{33,1},{65,33},{97,65},{2,98}... | collective-permute-start | bytes 983048 | tf_op jit(solution)/shard_map/ppermute | solution.py:521
  58.3 8.3 %collective-permute-start.1 = (f32[2,160,128]{2,1,0:T(8,128)S(1)}, f32[2,160,128]{2,1,0:T(8,128)S(1)}, u32[]{:S(2)}, u32[]{:S(2)}) collective-permute-start(f32[2,160,128]{2,1,0:T(8,128)S(1)} %get-tuple-element.41), channel_id=1, source_target_pairs={{0,1},{1,0},{2,3},{3,2},{4,5},{5,4},{6,7},{7,6},{8,9},{9,8},{10,11... | collective-permute-start | bytes 491528 | tf_op jit(solution)/shard_map/ppermute | solution.py:528
  61.5 5.2 %collective-permute-start.2 = (f32[2,160,128]{2,1,0:T(8,128)S(1)}, f32[2,160,128]{2,1,0:T(8,128)S(1)}, u32[]{:S(2)}, u32[]{:S(2)}) collective-permute-start(f32[2,160,128]{2,1,0:T(8,128)S(1)} %get-tuple-element.42), channel_id=1, source_target_pairs={{1,4},{5,8},{9,12},{13,16},{17,20},{21,24},{25,28},{29,2},{3,6},{7... | collective-permute-start | bytes 491528 | tf_op jit(solution)/shard_map/ppermute | solution.py:528
  71.7 5.8 %collective-permute-start.7 = (f32[4,160,128]{2,1,0:T(8,128)S(1)}, f32[4,160,128]{2,1,0:T(8,128)S(1)}, u32[]{:S(2)}, u32[]{:S(2)}) collective-permute-start(f32[4,160,128]{2,1,0:T(8,128)S(1)} %get-tuple-element.53), channel_id=1, source_target_pairs={{0,1},{1,0},{2,3},{3,2},{4,5},{5,4},{6,7},{7,6},{8,9},{9,8},{10,11... | collective-permute-start | bytes 983048 | tf_op jit(solution)/shard_map/ppermute | solution.py:528
  74.7 6.8 %collective-permute-start.8 = (f32[4,160,128]{2,1,0:T(8,128)S(1)}, f32[4,160,128]{2,1,0:T(8,128)S(1)}, u32[]{:S(2)}, u32[]{:S(2)}) collective-permute-start(f32[4,160,128]{2,1,0:T(8,128)S(1)} %get-tuple-element.54), channel_id=1, source_target_pairs={{1,4},{5,8},{9,12},{13,16},{17,20},{21,24},{25,28},{29,2},{3,6},{7... | collective-permute-start | bytes 983048 | tf_op jit(solution)/shard_map/ppermute | solution.py:528
  74.7 7.9 %collective-permute-start.9 = (f32[2,160,256]{2,1,0:T(8,128)S(1)}, f32[2,160,256]{2,1,0:T(8,128)S(1)}, u32[]{:S(2)}, u32[]{:S(2)}) collective-permute-start(f32[2,160,256]{2,1,0:T(8,128)S(1)} %get-tuple-element.55), channel_id=1, source_target_pairs={{0,32},{32,64},{64,96},{96,0},{1,33},{33,65},{65,97},{97,1},{2,34}... | collective-permute-start | bytes 983048 | tf_op jit(solution)/shard_map/ppermute | solution.py:521
  74.7 7.9 %collective-permute-start.10 = (f32[2,160,256]{2,1,0:T(8,128)S(1)}, f32[2,160,256]{2,1,0:T(8,128)S(1)}, u32[]{:S(2)}, u32[]{:S(2)}) collective-permute-start(f32[2,160,256]{2,1,0:T(8,128)S(1)} %get-tuple-element.56), channel_id=1, source_target_pairs={{0,96},{32,0},{64,32},{96,64},{1,97},{33,1},{65,33},{97,65},{2,98}... | collective-permute-start | bytes 983048 | tf_op jit(solution)/shard_map/ppermute | solution.py:521
  123.0 3.9 %collective-permute-start.11 = (f32[24,16,8,128]{3,2,1,0:T(8,128)S(1)}, f32[24,16,8,128]{3,2,1,0:T(8,128)S(1)}, u32[]{:S(2)}, u32[]{:S(2)}) collective-permute-start(f32[24,16,8,128]{3,2,1,0:T(8,128)S(1)} %split_send.1), channel_id=1, source_target_pairs={{0,1},{1,0},{2,3},{3,2},{4,5},{5,4},{6,7},{7,6},{8,9},{9,8},{10,11... | collective-permute-start | bytes 4718600 | tf_op jit(solution)/shard_map/ppermute | solution.py:508

commit v6 on v4

--- a/solution.py
+++ b/solution.py
@@ -392,6 +392,7 @@
     edges = exchange_x(start, end)
     ins = [*shared, *inner, *tables, *known, inside, outside]
     *known, inside, outside = in_vmem(run(False), core, ins, held + [STRIPS_SHAPE] * 2, "second_inner", 20, {9: 0, 10: 1}, [STRIPS])
+    inside, outside, *edges = lax.optimization_barrier((inside, outside, *edges))
     return known, edges, exchange_y(inside, outside)
 
 

time: 129 us -> 132 us (1.023); the launches traced: 128 us -> 130 us
  waiting for transfers between devices: 6.88 us -> 8.59 us
    ppermute x3, waiting for transfers between devices: 4.12 us -> 5.54 us  [exchange_y(): lax.ppermute(outside, ('gx_lo', 'gy', 'mode'), swap)]
  transfers between devices with their start and end apart: 12 -> 12, of which waited for: 4 -> 5; matrix products, arithmetic and copies ran while one was open for 1% -> 1% of each run, Pallas kernels for 11% -> 15%
where the time goes in v6:
time: 132 us; the launch traced here: 130 us
  blocking collectives  70.6 us (53%)
  Pallas kernels  33.1 us (25%)
  starting transfers between devices  14.8 us (11%)
  waiting for transfers between devices  8.59 us (7%)
  local copies, waits for them, and re-layouts  2.61 us (2%)
    all_to_all x1, blocking collectives, shards(): lax.all_to_all(pieces.reshape(XROWS, PIECE, 128), ('gx_lo', 'mode'), 0, 0...  35.9 us
    all_to_all x1, blocking collectives, shards(): lax.all_to_all(tile, ('gx_lo', 'mode'), 0, 0, tiled=True)  34.7 us
    pallas_call x5, Pallas kernels, in_vmem(): pl.pallas_call(kernel, in_specs=[pl.BlockSpec(memory_space=pltpu.SMEM)] +...  23.3 us
    ppermute x3, starting transfers between devices, exchange_y(): lax.ppermute(inside, 'mode', [(0, 1), (1, 0)])  7.12 us
    ppermute x3, waiting for transfers between devices, exchange_y(): lax.ppermute(outside, ('gx_lo', 'gy', 'mode'), swap)  5.54 us
    ppermute x2, starting transfers between devices, exchange_x(): lax.ppermute(start, 'gx_hi', ring(size, -1))  4.13 us
  transfers between devices with their start and end apart: 12, of which 5 were waited for; matrix products, arithmetic and copies ran while one was open for 1% of the time, Pallas kernels for 15%

profile of v6, /device:TPU:1, one launch (start us, length us, event | category | flops | bytes accessed | tf_op | source)
XLA Modules:
  0.0 130.0 jit_solution(14964046668225667732)
XLA Ops:
  0.0 1.9 %copy-done = f32[2,24,4,4096]{3,2,1,0:T(4,128)S(1)} copy-done((f32[2,24,4,4096]{3,2,1,0:T(4,128)S(1)}, f32[2,24,4,4096]{3,2,1,0:T(4,128)}, u32[]{:S(2)}) %copy-start) | copy-done | bytes 3145752
  1.9 1.3 %pack.1 = f32[24,16,8,128]{3,2,1,0:T(8,128)} custom-call(s32[1]{0:T(128)} %bitcast.core_ref.refs_0_, f32[2,24,16,8,128]{4,3,2,1,0:T(8,128)S(1)} %bitcast.17), custom_call_target="tpu_custom_call" | custom-call | flops 2000000000 | tf_op jit(solution)/shard_map/pack/pallas_call | solution.py:486
  3.2 1.4 %collective-permute-start = (f32[24,16,8,128]{3,2,1,0:T(8,128)}, f32[24,16,8,128]{3,2,1,0:T(8,128)}, u32[]{:S(2)}, u32[]{:S(2)}) collective-permute-start(f32[24,16,8,128]{3,2,1,0:T(8,128)} %pack.1), channel_id=1, source_target_pairs={{0,1},{1,0},{2,3},{3,2},{4,5},{5,4},{6,7},{7,6},{8,9},{9,8},{10,11... | collective-permute-start | bytes 4718600 | tf_op jit(solution)/shard_map/ppermute | solution.py:486
  4.6 0.0 copy-done.6
  4.6 0.7 copy.13.degrees_ref
  5.3 2.2 %tables.1 = (bf16[224,128]{1,0:T(8,128)(2,1)}, bf16[80,192]{1,0:T(8,128)(2,1)}, f32[3,40,256]{2,1,0:T(8,128)}, s32[1]{0:T(128)}) custom-call(s32[1,35]{1,0:T(1,128)} %bitcast.19, s32[35,4]{1,0:T(8,128)} %copy.13.degrees_ref, f32[8,192]{1,0:T(8,128)} %constant.10.clone.prow_ref, f32[96,8]{1,0:T(8,128)} %constant.11.clone.pcol_ref), custom_call_target="tpu_custom_call" | custom-call | tf_op jit(solution)/shard_map/tables/pallas_call | solution.py:113
  7.6 0.4 collective-permute-done.got_ref
  8.0 0.0 copy-done.1
  8.0 2.3 %merge.1 = f32[16,35,8,128]{3,2,1,0:T(8,128)S(1)} custom-call(s32[1]{0:T(128)} %bitcast.core_ref.refs_0_, s32[1]{0:T(128)} %get-tuple-element.35.big_ref.refs_1_, f32[2,24,16,8,128]{4,3,2,1,0:T(8,128)S(1)} %bitcast.18, f32[24,16,8,128]{3,2,1,0:T(8,128)} %collective-permute-done.got_ref), custom_call_target="tpu_custom_call" | custom-call | flops 2000000000 | tf_op jit(solution)/shard_map/merge/pallas_call | solution.py:487
  10.4 0.0 copy-start.2
  10.4 0.0 copy-start.3
  10.4 0.0 copy-start.4
  10.4 0.0 copy-start.5
  10.4 35.9 %all_to_all.10.refs_1_ = f32[16,280,128]{2,1,0:T(8,128)S(1)} all-to-all(f32[16,280,128]{2,1,0:T(8,128)S(1)} %bitcast.16), channel_id=1, replica_groups=mesh['gx_hi'=4,'gx_lo'=8,'gy'=2,'mode'=2] {'gx_lo','mode'}, dimensions={0} | all-to-all | bytes 4587520 | tf_op jit(solution)/shard_map/all_to_all | solution.py:519
  46.3 0.0 copy-done.2
  46.3 0.0 copy-done.3
  46.3 0.0 copy-done.4
  46.3 4.5 %first_outer.1 = (f32[16,160,256]{2,1,0:T(8,128)S(1)}, f32[16,160,256]{2,1,0:T(8,128)S(1)}, f32[16,160,256]{2,1,0:T(8,128)S(1)}, f32[2,160,128]{2,1,0:T(8,128)S(...) custom-call(s32[1]{0:T(128)} %bitcast.core_ref.refs_0_, ...), custom_call_target="tpu_custom_call" | custom-call | flops 5000000000 | bytes 15000000 | tf_op jit(solution)/shard_map/first_outer/pallas_call | solution.py:360
  50.8 0.9 collective-permute-start.3
  51.7 0.0 collective-permute-start.4
  51.7 1.2 collective-permute-start.5
  52.9 1.5 %collective-permute-start.6 = (f32[2,160,256]{2,1,0:T(8,128)S(1)}, f32[2,160,256]{2,1,0:T(8,128)S(1)}, u32[]{:S(2)}, u32[]{:S(2)}) collective-permute-start(f32[2,160,256]{2,1,0:T(8,128)S(1)} %get-tuple-element.50), channel_id=1, source_target_pairs={{0,96},{32,0},{64,32},{96,64},{1,97},{33,1},{65,33},{97,65},{2,98}... | collective-permute-start | bytes 983048 | tf_op jit(solution)/shard_map/ppermute | solution.py:504
  54.4 4.5 %first_inner.1 = (f32[16,160,256]{2,1,0:T(8,128)S(1)}, f32[16,160,256]{2,1,0:T(8,128)S(1)}, f32[16,160,256]{2,1,0:T(8,128)S(1)}, f32[2,160,128]{2,1,0:T(8,128)S(1)}, f32[2,160,128]{2,1,0:T(8,128)S(1)}) custom-call(s32[1]{0:T(128)} %bitcast.core_ref.refs_0_, ...), custom_call_target="tpu_custom_call", output_to_operand_aliasing={{0}: (6, {}), {1}: (7, {}), {2}: (8, {})} | custom-call | flops 20000000000 | bytes 60000000 | tf_op jit(solution)/shard_map/first_inner/pallas_call | solution.py:360
  58.9 3.2 %collective-permute-start.1 = (f32[2,160,128]{2,1,0:T(8,128)S(1)}, f32[2,160,128]{2,1,0:T(8,128)S(1)}, u32[]{:S(2)}, u32[]{:S(2)}) collective-permute-start(f32[2,160,128]{2,1,0:T(8,128)S(1)} %get-tuple-element.45), channel_id=1, source_target_pairs={{0,1},{1,0},{2,3},{3,2},{4,5},{5,4},{6,7},{7,6},{8,9},{9,8},{10,11... | collective-permute-start | bytes 491528 | tf_op jit(solution)/shard_map/ppermute | solution.py:511
  62.1 0.0 collective-permute-done.3.refs_4_
  62.1 0.0 collective-permute-start.2
  62.1 0.0 collective-permute-done.4.refs_5_
  62.1 0.0 collective-permute-done.5.refs_10_
  62.1 0.0 collective-permute-done.6.refs_11_
  62.1 5.2 %second_outer.1 = (f32[16,160,256]{2,1,0:T(8,128)S(1)}, f32[16,160,256]{2,1,0:T(8,128)S(1)}, f32[2,160,128]{2,1,0:T(8,128)S(1)}, f32[2,160,128]{2,1,0:T(8,128)S(...) custom-call(s32[1]{0:T(128)} %bitcast.core_ref.refs_0_, f32[16,160,256]{2,1,0:T(8,128)S(1)} %get-tuple-element.42.refs_1_, ...), custom_call_target="tpu_custom_call" | custom-call | flops 8000000000 | bytes 24000000 | tf_op jit(solution)/shard_map/second_outer/pallas_call | solution.py:360
  67.3 0.1 collective-permute-start.7
  67.4 2.7 %collective-permute-start.8 = (f32[2,160,256]{2,1,0:T(8,128)S(1)}, f32[2,160,256]{2,1,0:T(8,128)S(1)}, u32[]{:S(2)}, u32[]{:S(2)}) collective-permute-start(f32[2,160,256]{2,1,0:T(8,128)S(1)} %get-tuple-element.60), channel_id=1, source_target_pairs={{0,96},{32,0},{64,32},{96,64},{1,97},{33,1},{65,33},{97,65},{2,98}... | collective-permute-start | bytes 983048 | tf_op jit(solution)/shard_map/ppermute | solution.py:504
  70.1 0.0 collective-permute-done.1.refs_4_
  70.1 0.0 collective-permute-done.2.refs_5_
  70.1 5.3 %second_inner.1 = (f32[16,160,256]{2,1,0:T(8,128)S(1)}, f32[16,160,256]{2,1,0:T(8,128)S(1)}, f32[4,160,128]{2,1,0:T(8,128)S(1)}, f32[4,160,128]{2,1,0:T(8,128)S(1)}) custom-call(s32[1]{0:T(128)} %bitcast.core_ref.refs_0_, f32[16,160,256]{2,1,0:T(8,128)S(1)} %get-tuple-element.42.refs_1_, ...), custom_call_target="tpu_custom_call", output_to_operand_aliasing={{0}: (10, {}), {1}: (11, {})} | custom-call | flops 20000000000 | bytes 60000000 | tf_op jit(solution)/shard_map/second_inner/pallas_call | solution.py:360
  75.4 0.3 collective-permute-done.7.edge_before
  75.7 0.0 collective-permute-done.8.edge_after
  75.7 3.1 %collective-permute-start.9 = (f32[4,160,128]{2,1,0:T(8,128)S(1)}, f32[4,160,128]{2,1,0:T(8,128)S(1)}, u32[]{:S(2)}, u32[]{:S(2)}) collective-permute-start(f32[4,160,128]{2,1,0:T(8,128)S(1)} %get-tuple-element.61), channel_id=1, source_target_pairs={{0,1},{1,0},{2,3},{3,2},{4,5},{5,4},{6,7},{7,6},{8,9},{9,8},{10,11... | collective-permute-start | bytes 983048 | tf_op jit(solution)/shard_map/ppermute | solution.py:511
  78.7 0.0 collective-permute-start.10
  78.7 1.3 collective-permute-done.9.inside_from
  80.0 5.5 %collective-permute-done.10.outside_from = f32[4,160,128]{2,1,0:T(8,128)S(1)} collective-permute-done((f32[4,160,128]{2,1,0:T(8,128)S(1)}, f32[4,160,128]{2,1,0:T(8,128)S(1)}, u32[]{:S(2)}, u32[]{:S(2)}) %collective-permute-start.10) | collective-permute-done | bytes 327712 | tf_op jit(solution)/shard_map/ppermute | solution.py:511
  85.5 3.7 %advanced.1 = f32[16,280,128]{2,1,0:T(8,128)S(1)} custom-call(s32[1]{0:T(128)} %bitcast.core_ref.refs_0_, f32[16,160,256]{2,1,0:T(8,128)S(1)} %get-tuple-element.55.following_ref, f32[16,160,256]{2,1,0:T(8,128)S(1)} %get-tuple-element.56.from_ref, f32[4,160,128]{2,1,0:T(8,128)S(1)} %collective-permute-done.9.inside_from, ...), custom_call_target="tpu_custom_call" | custom-call | flops 8000000000 | bytes 24000000 | tf_op jit(solution)/shard_map/advanced/pallas_call | solution.py:360
  89.2 34.7 %all_to_all.11 = f32[16,280,128]{2,1,0:T(8,128)S(1)} all-to-all(f32[16,280,128]{2,1,0:T(8,128)S(1)} %advanced.1), channel_id=1, replica_groups=mesh['gx_hi'=4,'gx_lo'=8,'gy'=2,'mode'=2] {'gx_lo','mode'}, dimensions={0} | all-to-all | bytes 4587520 | tf_op jit(solution)/shard_map/all_to_all | solution.py:523
  124.0 0.8 split_send.1
  124.8 0.9 collective-permute-start.11
  125.7 2.0 %split_own.1._ = f32[2,24,16,8,128]{4,3,2,1,0:T(8,128)} custom-call(s32[1]{0:T(128)} %bitcast.core_ref.refs_0_, s32[1]{0:T(128)} %get-tuple-element.35.big_ref.refs_1_, f32[16,35,8,128]{3,2,1,0:T(8,128)S(1)} %bitcast.15), custom_call_target="tpu_custom_call" | custom-call | flops 2000000000 | tf_op jit(solution)/shard_map/split_own/pallas_call | solution.py:493
  127.6 1.1 collective-permute-done.11.got_ref
  128.7 1.1 finish.1
  (4 shorter events, 0.0 us)
Async XLA Ops:
  0.0 1.9 %copy-start = (f32[2,24,4,4096]{3,2,1,0:T(4,128)S(1)}, f32[2,24,4,4096]{3,2,1,0:T(4,128)}, u32[]{:S(2)}) copy-start(f32[2,24,4,4096]{3,2,1,0:T(4,128)} %param.6) | copy-start | bytes 9437188
  1.9 2.7 %copy-start.6 = (s32[35,4]{0,1:T(4,128)S(1)}, s32[35,4]{0,1:T(4,128)}, u32[]{:S(2)}) copy-start(s32[35,4]{0,1:T(4,128)} %param.8) | copy-start | bytes 1684
  1.9 6.1 %copy-start.1 = (f32[2,24,4,4096]{3,2,1,0:T(4,128)S(1)}, f32[2,24,4,4096]{3,2,1,0:T(4,128)}, u32[]{:S(2)}) copy-start(f32[2,24,4,4096]{3,2,1,0:T(4,128)} %param.6) | copy-start | bytes 9437188
  3.2 4.8 %collective-permute-start = (f32[24,16,8,128]{3,2,1,0:T(8,128)}, f32[24,16,8,128]{3,2,1,0:T(8,128)}, u32[]{:S(2)}, u32[]{:S(2)}) collective-permute-start(f32[24,16,8,128]{3,2,1,0:T(8,128)} %pack.1), channel_id=1, source_target_pairs={{0,1},{1,0},{2,3},{3,2},{4,5},{5,4},{6,7},{7,6},{8,9},{9,8},{10,11... | collective-permute-start | bytes 4718600 | tf_op jit(solution)/shard_map/ppermute | solution.py:486
  10.4 35.9 %copy-start.2 = (f32[3,40,256]{2,1,0:T(8,128)S(1)}, f32[3,40,256]{2,1,0:T(8,128)}, u32[]{:S(2)}) copy-start(f32[3,40,256]{2,1,0:T(8,128)} %get-tuple-element.38.refs_5_.refs_9_.scale_ref) | copy-start | bytes 368644
  10.4 35.9 %copy-start.3 = (bf16[224,128]{1,0:T(8,128)(2,1)S(1)}, bf16[224,128]{1,0:T(8,128)(2,1)}, u32[]{:S(2)}) copy-start(bf16[224,128]{1,0:T(8,128)(2,1)} %get-tuple-element.36.refs_2_.refs_6_) | copy-start | bytes 172036
  10.4 35.9 %copy-start.4 = (bf16[80,192]{1,0:T(8,128)(2,1)S(1)}, bf16[80,192]{1,0:T(8,128)(2,1)}, u32[]{:S(2)}) copy-start(bf16[80,192]{1,0:T(8,128)(2,1)} %get-tuple-element.37.refs_3_.refs_7_) | copy-start | bytes 92164
  10.4 35.9 %copy-start.5 = (bf16[2,512,256]{2,1,0:T(8,128)(2,1)S(1)}, bf16[2,512,256]{2,1,0:T(8,128)(2,1)}, u32[]{:S(2)}) copy-start(bf16[2,512,256]{2,1,0:T(8,128)(2,1)} %constant.12.clone.refs_4_.refs_8_) | copy-start | bytes 1572868
  50.8 11.2 %collective-permute-start.3 = (f32[2,160,128]{2,1,0:T(8,128)S(1)}, f32[2,160,128]{2,1,0:T(8,128)S(1)}, u32[]{:S(2)}, u32[]{:S(2)}) collective-permute-start(f32[2,160,128]{2,1,0:T(8,128)S(1)} %get-tuple-element.47), channel_id=1, source_target_pairs={{0,1},{1,0},{2,3},{3,2},{4,5},{5,4},{6,7},{7,6},{8,9},{9,8},{10,11... | collective-permute-start | bytes 491528 | tf_op jit(solution)/shard_map/ppermute | solution.py:511
  51.7 10.4 %collective-permute-start.4 = (f32[2,160,128]{2,1,0:T(8,128)S(1)}, f32[2,160,128]{2,1,0:T(8,128)S(1)}, u32[]{:S(2)}, u32[]{:S(2)}) collective-permute-start(f32[2,160,128]{2,1,0:T(8,128)S(1)} %get-tuple-element.48), channel_id=1, source_target_pairs={{1,4},{5,8},{9,12},{13,16},{17,20},{21,24},{25,28},{29,2},{3,6},{7... | collective-permute-start | bytes 491528 | tf_op jit(solution)/shard_map/ppermute | solution.py:511
  51.7 10.4 %collective-permute-start.5 = (f32[2,160,256]{2,1,0:T(8,128)S(1)}, f32[2,160,256]{2,1,0:T(8,128)S(1)}, u32[]{:S(2)}, u32[]{:S(2)}) collective-permute-start(f32[2,160,256]{2,1,0:T(8,128)S(1)} %get-tuple-element.49), channel_id=1, source_target_pairs={{0,32},{32,64},{64,96},{96,0},{1,33},{33,65},{65,97},{97,1},{2,34}... | collective-permute-start | bytes 983048 | tf_op jit(solution)/shard_map/ppermute | solution.py:504
  52.9 9.2 %collective-permute-start.6 = (f32[2,160,256]{2,1,0:T(8,128)S(1)}, f32[2,160,256]{2,1,0:T(8,128)S(1)}, u32[]{:S(2)}, u32[]{:S(2)}) collective-permute-start(f32[2,160,256]{2,1,0:T(8,128)S(1)} %get-tuple-element.50), channel_id=1, source_target_pairs={{0,96},{32,0},{64,32},{96,64},{1,97},{33,1},{65,33},{97,65},{2,98}... | collective-permute-start | bytes 983048 | tf_op jit(solution)/shard_map/ppermute | solution.py:504
  58.9 11.2 %collective-permute-start.1 = (f32[2,160,128]{2,1,0:T(8,128)S(1)}, f32[2,160,128]{2,1,0:T(8,128)S(1)}, u32[]{:S(2)}, u32[]{:S(2)}) collective-permute-start(f32[2,160,128]{2,1,0:T(8,128)S(1)} %get-tuple-element.45), channel_id=1, source_target_pairs={{0,1},{1,0},{2,3},{3,2},{4,5},{5,4},{6,7},{7,6},{8,9},{9,8},{10,11... | collective-permute-start | bytes 491528 | tf_op jit(solution)/shard_map/ppermute | solution.py:511
  62.1 8.0 %collective-permute-start.2 = (f32[2,160,128]{2,1,0:T(8,128)S(1)}, f32[2,160,128]{2,1,0:T(8,128)S(1)}, u32[]{:S(2)}, u32[]{:S(2)}) collective-permute-start(f32[2,160,128]{2,1,0:T(8,128)S(1)} %get-tuple-element.46), channel_id=1, source_target_pairs={{1,4},{5,8},{9,12},{13,16},{17,20},{21,24},{25,28},{29,2},{3,6},{7... | collective-permute-start | bytes 491528 | tf_op jit(solution)/shard_map/ppermute | solution.py:511
  67.3 8.3 %collective-permute-start.7 = (f32[2,160,256]{2,1,0:T(8,128)S(1)}, f32[2,160,256]{2,1,0:T(8,128)S(1)}, u32[]{:S(2)}, u32[]{:S(2)}) collective-permute-start(f32[2,160,256]{2,1,0:T(8,128)S(1)} %get-tuple-element.59), channel_id=1, source_target_pairs={{0,32},{32,64},{64,96},{96,0},{1,33},{33,65},{65,97},{97,1},{2,34}... | collective-permute-start | bytes 983048 | tf_op jit(solution)/shard_map/ppermute | solution.py:504
  67.4 8.3 %collective-permute-start.8 = (f32[2,160,256]{2,1,0:T(8,128)S(1)}, f32[2,160,256]{2,1,0:T(8,128)S(1)}, u32[]{:S(2)}, u32[]{:S(2)}) collective-permute-start(f32[2,160,256]{2,1,0:T(8,128)S(1)} %get-tuple-element.60), channel_id=1, source_target_pairs={{0,96},{32,0},{64,32},{96,64},{1,97},{33,1},{65,33},{97,65},{2,98}... | collective-permute-start | bytes 983048 | tf_op jit(solution)/shard_map/ppermute | solution.py:504
  75.7 4.3 %collective-permute-start.9 = (f32[4,160,128]{2,1,0:T(8,128)S(1)}, f32[4,160,128]{2,1,0:T(8,128)S(1)}, u32[]{:S(2)}, u32[]{:S(2)}) collective-permute-start(f32[4,160,128]{2,1,0:T(8,128)S(1)} %get-tuple-element.61), channel_id=1, source_target_pairs={{0,1},{1,0},{2,3},{3,2},{4,5},{5,4},{6,7},{7,6},{8,9},{9,8},{10,11... | collective-permute-start | bytes 983048 | tf_op jit(solution)/shard_map/ppermute | solution.py:511
  78.7 6.8 %collective-permute-start.10 = (f32[4,160,128]{2,1,0:T(8,128)S(1)}, f32[4,160,128]{2,1,0:T(8,128)S(1)}, u32[]{:S(2)}, u32[]{:S(2)}) collective-permute-start(f32[4,160,128]{2,1,0:T(8,128)S(1)} %get-tuple-element.62), channel_id=1, source_target_pairs={{1,4},{5,8},{9,12},{13,16},{17,20},{21,24},{25,28},{29,2},{3,6},{7... | collective-permute-start | bytes 983048 | tf_op jit(solution)/shard_map/ppermute | solution.py:511
  124.8 3.9 %collective-permute-start.11 = (f32[24,16,8,128]{3,2,1,0:T(8,128)S(1)}, f32[24,16,8,128]{3,2,1,0:T(8,128)S(1)}, u32[]{:S(2)}, u32[]{:S(2)}) collective-permute-start(f32[24,16,8,128]{3,2,1,0:T(8,128)S(1)} %split_send.1), channel_id=1, source_target_pairs={{0,1},{1,0},{2,3},{3,2},{4,5},{5,4},{6,7},{7,6},{8,9},{9,8},{10,11... | collective-permute-start | bytes 4718600 | tf_op jit(solution)/shard_map/ppermute | solution.py:491
